TPU v7x, 32 devices: a whole 2x2x4 slice. The times are simulated.
32 devices in a mesh: ex: 4 (over z), ey: 4 (over x, core), ez: 2 (over y).
Axes of the slice: x: 2, y: 2, z: 4, core: 2. Of those that a mesh axis runs over, the one named last changes fastest.
Arguments:
- load_raw: float32 [8, 8, 8, 32, 384], P('ex', 'ey', 'ez'), may hold values from -8 to 8
- scaling: float32 [8, 8, 8, 384], P('ex', 'ey', 'ez'), may hold values from 0.6 to 1.8
- fine_matrix: float32 [384, 384], replicated
- fine_inverse: float32 [384, 384], replicated
- prolong_four: float32 [384, 98], replicated
- coarse_four: float32 [98, 98], replicated
- prolong_two: float32 [384, 26], replicated
- coarse_two: float32 [26, 26], replicated
- orient: int32 [3, 8, 8, 8], P(None, 'ex', 'ey', 'ez'), may hold values from 0 to 3
- boundary: int32 [6, 8, 8, 8], P(None, 'ex', 'ey', 'ez'), may hold values from 0 to 1
Outputs:
- solution: float32 [8, 8, 8, 32, 384], P('ex', 'ey', 'ez')
All inputs are finite; a program needn't handle non-finite values.
Results may differ from a plain program's by a relative error of at most 0.0001.
Values sent between devices are 32-bit elements; how exact they have to be, the bound alone decides.
No kernel may reach another device: no remote copies, remote signals or barrier semaphores. Data moves between devices by JAX's collectives and lax.ppermute only.
A program may use at most 64 MiB of HBM per device.

v0:
```python
import functools

import jax
import jax.numpy as jnp
from jax import lax
from jax.experimental import pallas as pl
from jax.experimental.pallas import tpu as pltpu
import numpy as np
from jax.sharding import PartitionSpec as P

FACE_SIDE = 8
FACE = FACE_SIDE * FACE_SIDE
WIDTH = 2 * FACE
AXES = ("ex", "ey", "ez")
TURNS = ((1, 1), (0, 0), (0, 1), (1, 0), (2, 1), (2, 0))
FIRST_TURNS = ((1, 1), (0, 1), (0, 0), (1, 0), (2, 1), (2, 0))
DIMS = (0, 1, 2)
EARLY = (1, 0)
LATE = 2
FETCHED = 5
VMEM_LIMIT = 24 * 1024 * 1024


class Layout:
    def __init__(self, counts, species, sizes):
        self.counts = counts
        self.species = species
        self.sizes = sizes

    def elements(self):
        spans = [range(count) for count in self.counts]
        return [(i, j, k) for i in spans[0] for j in spans[1] for k in spans[2]]

    def number(self, element):
        return (element[0] * self.counts[1] + element[1]) * self.counts[2] + element[2]

    def rows(self, element):
        start = self.number(element) * self.species
        return slice(start, start + self.species)

    def layer(self, dim, position):
        return [element for element in self.elements() if element[dim] == position]

    def pairs(self, dim):
        return (len(self.layer(dim, 0)) + 1) // 2

    def pair_rows(self, pair):
        return slice(pair * self.species, (pair + 1) * self.species)

    def turns(self, dims=(0, 1, 2), order=TURNS):
        return [
            (dim, parity) for dim, parity in order if dim in dims and self.sizes[dim] > 1 + parity
        ]

    def edge(self):
        ends = (0, self.counts[LATE] - 1)
        return [element for element in self.elements() if element[LATE] in ends]

    def sides(self, dim):
        return self.layer(dim, 0), self.layer(dim, self.counts[dim] - 1)

    def message(self, dim):
        return jax.ShapeDtypeStruct((self.pairs(dim) * self.species, WIDTH), jnp.float32)


def columns(dim):
    return slice(dim * WIDTH, (dim + 1) * WIDTH)


def lanes(layout):
    return lax.broadcasted_iota(jnp.int32, (layout.species, WIDTH), 1)


def picked(value, index):
    return jnp.take_along_axis(value, index, axis=1, mode="promise_in_bounds")


def flip_mask(code):
    reach = FACE_SIDE - 1
    return (code & 1) * (reach * FACE_SIDE) + (code >> 1) * reach


def places():
    return [lax.axis_index(axis) for axis in AXES]


def pack(layout, here, dim, load_block, mask_of, outs):
    turns = [(turn, out) for turn, out in zip(layout.turns(), outs) if turn[0] == dim]
    if not turns:
        return
    lane = lanes(layout)
    low = lane < FACE
    even = (here[dim] & 1) == 0
    first = layout.layer(dim, 0)
    last = layout.layer(dim, layout.counts[dim] - 1)
    for pair in range(layout.pairs(dim)):
        sides = []
        for half in range(2):
            where = min(2 * pair + half, len(first) - 1)
            upper = load_block(last[where], dim)
            lower = load_block(first[where], dim)
            lower = picked(lower, lane ^ mask_of(first[where], dim) ^ (half * FACE))
            if half == 0:
                upper = pltpu.roll(upper, FACE, 1)
            sides.append((upper, lower))
        up = jnp.where(low, sides[0][0], sides[1][0])
        down = jnp.where(low, sides[0][1], sides[1][1])
        for (_, parity), out in turns:
            is_lower = even if parity == 0 else jnp.logical_not(even)
            out[layout.pair_rows(pair), :] = jnp.where(is_lower, up, down)


def received(layout, here, dim, messages):
    even = (here[dim] & 1) == 0
    at_start = here[dim] == 0
    at_end = here[dim] == layout.sizes[dim] - 1
    zero = jnp.zeros((layout.species, WIDTH), jnp.float32)
    found = []
    for pair in range(layout.pairs(dim)):
        first, second = [
            messages[dim, parity][layout.pair_rows(pair), :] if (dim, parity) in messages else zero
            for parity in range(2)
        ]
        below = jnp.where(at_start, 0.0, jnp.where(even, second, first))
        above = jnp.where(at_end, 0.0, jnp.where(even, first, second))
        found.append((below, above))
    return found


def unpacked(lane, outside, where, mask):
    below, above = outside[where // 2]
    half = (where % 2) * FACE
    inside = lane & (FACE - 1)
    return picked(below, (inside ^ mask) + half), picked(above, inside + half)


def assemble(layout, here, dim, load_block, messages, mask_of, keep_of, emit, slab=None):
    lane = lanes(layout)
    low = lane < FACE
    count = layout.counts[dim]
    outside = None if messages is None else received(layout, here, dim, messages)
    zero = jnp.zeros((layout.species, WIDTH), jnp.float32)
    for where, start in enumerate(layout.layer(dim, 0)):
        if slab not in (None, start[0]):
            continue
        line = [start[:dim] + (step,) + start[dim + 1 :] for step in range(count)]
        blocks = [load_block(element, dim) for element in line]
        if outside is None:
            from_below, from_above = zero, zero
        else:
            from_below, from_above = unpacked(lane, outside, where, mask_of(start, dim))
        turned = [from_below]
        for step, element in list(enumerate(line))[1:]:
            shared = jnp.where(low, blocks[step], blocks[step - 1])
            turned.append(picked(shared, lane ^ mask_of(element, dim) ^ FACE))
        turned.append(from_above)
        for step, element in enumerate(line):
            value = blocks[step] + jnp.where(low, turned[step], turned[step + 1])
            if step in (0, count - 1):
                value = value * keep_of(element, dim)
            emit(element, value)


def halves(value):
    high = value.astype(jnp.bfloat16)
    return high, (value - high.astype(jnp.float32)).astype(jnp.bfloat16)


def dot(left, right, contract=((1,), (0,))):
    return lax.dot_general(left, right, (contract, ((), ())), preferred_element_type=jnp.float32)


def split_dot(left, right, contract):
    left_high, left_rest = halves(left)
    right_high, right_rest = halves(right)
    return (
        dot(left_high, right_high, contract)
        + dot(left_high, right_rest, contract)
        + dot(left_rest, right_high, contract)
    )


def stacked(value, local, faces):
    high, rest = halves(value)
    size = value.shape[0]
    for part, piece in enumerate((high, rest, high)):
        local[part * size : (part + 1) * size, :] = piece
    for number in range(faces.shape[0]):
        rows = slice(number * FACE, (number + 1) * FACE)
        for part, piece in enumerate((high, high, rest)):
            faces[number, part * FACE : (part + 1) * FACE, :] = piece[rows, :]
        faces[number, 3 * FACE :, :] = jnp.zeros((FACE, value.shape[1]), jnp.bfloat16)


def operator_kernel(fine, *outs):
    stacked(fine[...], *outs)


def smoother_kernel(inverse, four, coarse_four, two, coarse_two, *refs):
    *outs, right, left = refs
    right[...] = jnp.zeros_like(right)
    left[...] = jnp.zeros_like(left)
    start = 0
    for prolong, coarse in ((four, coarse_four), (two, coarse_two)):
        rows = slice(start, start + prolong.shape[0])
        left[rows, :] = prolong[...]
        right[rows, :] = split_dot(coarse[...], prolong[...], ((1,), (0,)))
        start += rounded(prolong.shape[0])
    corrections = split_dot(left[...], right[...], ((0,), (0,)))
    stacked(0.5 * (inverse[...] + corrections), *outs)


def rounded(count):
    return (count + 7) // 8 * 8


def first_kernel(layout, load, orient, boundary, *refs):
    turns = len(layout.turns())
    small, refs = refs[:FETCHED], refs[FETCHED:]
    outs, masks, keeps, staged = refs[:turns], *refs[turns : turns + 3]
    fetched, (codes, fixed, arrived) = refs[turns + 3 : turns + 3 + FETCHED], refs[-3:]
    scalars = [
        pltpu.make_async_copy(source, target, arrived.at[number])
        for number, (source, target) in enumerate(((orient, codes), (boundary, fixed)))
    ]
    strips = [
        pltpu.make_async_copy(
            load.at[:, columns(dim)], staged.at[:, columns(dim)], arrived.at[2 + dim]
        )
        for dim in DIMS
    ]
    fetches = [
        pltpu.make_async_copy(source, target, arrived.at[5 + number])
        for number, (source, target) in enumerate(zip(small, fetched))
    ]
    for copy in scalars + strips + fetches:
        copy.start()
    here = places()
    scalars[0].wait()
    tabulate_masks(layout, codes, masks)
    scalars[1].wait()
    tabulate_keeps(layout, here, fixed, keeps)
    for dim in DIMS:
        strips[dim].wait()
        pack(
            layout,
            here,
            dim,
            lambda element, dim: staged[layout.rows(element), columns(dim)],
            table(layout, masks),
            outs,
        )
    for copy in fetches:
        copy.wait()


def tabulate_masks(layout, codes, masks):
    for element in layout.elements():
        number = layout.number(element)
        for dim in DIMS:
            code = jnp.full((1, WIDTH), codes[(dim,) + element], jnp.int32)
            masks[number : number + 1, columns(dim)] = flip_mask(code)


def tabulate_keeps(layout, here, boundary, keeps):
    low = lax.broadcasted_iota(jnp.int32, (1, WIDTH), 1) < FACE
    for dim in DIMS:
        first = jnp.where(here[dim] == 0, 1, 0)
        last = jnp.where(here[dim] == layout.sizes[dim] - 1, 1, 0)
        for element in layout.elements():
            number = layout.number(element)
            keep = jnp.ones((1, WIDTH), jnp.float32)
            if element[dim] == 0:
                fixed = first * boundary[element + (2 * dim,)]
                keep = jnp.where(low, 1.0 - jnp.full((1, WIDTH), fixed, jnp.float32), keep)
            if element[dim] == layout.counts[dim] - 1:
                fixed = last * boundary[element + (2 * dim + 1,)]
                keep = jnp.where(low, keep, 1.0 - jnp.full((1, WIDTH), fixed, jnp.float32))
            keeps[number : number + 1, columns(dim)] = keep


def table(layout, ref):
    def row(element, dim):
        number = layout.number(element)
        return ref[number : number + 1, columns(dim)]

    return row


def scales(layout, kind, ref):
    def row(element, dim):
        value = ref[element[0], element[1], element[2] : element[2] + 1, columns(dim)]
        return value if kind == "operator" else 1.0 / value

    return row


def taken(layout, dims, refs, order=TURNS):
    turns = layout.turns(dims, order)
    return dict(zip(turns, refs)), refs[len(turns) :]


def combined(kind, begun, result):
    if begun is None:
        return result
    return begun - result if kind == "operator" else begun + result


def reader(layout, whole, edges=None):
    edge = [] if edges is None else layout.edge()

    def block(element, dim):
        if element in edge:
            return edges[layout.pair_rows(edge.index(element)), columns(dim)]
        return whole[layout.rows(element), columns(dim)]

    return block


def local_kernel(layout, kind, given, *refs):
    value, begun, refs = refs[: given[0]], refs[given[0] : sum(given)], refs[sum(given) :]
    masks, keeps, scaling, matrix, out, split, summed = refs
    value = reader(layout, *value)
    begun = reader(layout, *begun) if begun else None
    here = places()
    factor = scales(layout, kind, scaling)
    nodes = out.shape[1]

    def assembled(dim, slab):
        def emit(element, result):
            high, rest = halves(result * factor(element, dim))
            for part, piece in enumerate((high, high, rest)):
                start = part * nodes + dim * WIDTH
                split[layout.rows(element), start : start + WIDTH] = piece

        assemble(
            layout,
            here,
            dim,
            value,
            None,
            table(layout, masks),
            table(layout, keeps),
            emit,
            slab,
        )

    assembled(0, None)
    count = layout.counts[0]
    height = out.shape[0] // count
    for slab in range(count):
        assembled(1, slab)
        assembled(2, slab)
        rows = slice(slab * height, (slab + 1) * height)
        summed[rows, :] = dot(split[rows, :], matrix[...])
        for element in layout.layer(0, slab):
            for dim in DIMS:
                at = (layout.rows(element), columns(dim))
                result = summed[at] * factor(element, dim)
                out[at] = combined(kind, begun and begun(element, dim), result)


def combined(kind, begun, result):
    if begun is None:
        return result
    return begun - result if kind == "operator" else begun + result


def strips_kernel(layout, kind, dims, local, value, *refs):
    messages, refs = (None, refs) if local else taken(layout, dims, refs)
    masks, keeps, scaling, matrix, *before, out, split, summed = refs
    begun = before[0] if before else None
    here = places()
    factor = scales(layout, kind, scaling)

    def assembled(place, slab):
        dim = dims[place]

        def emit(element, result):
            scaled = result * factor(element, dim)
            put_split(split, layout.rows(element), place, len(dims), scaled)

        assemble(
            layout,
            here,
            dim,
            lambda element, dim: value[layout.rows(element), columns(dim)],
            messages,
            table(layout, masks),
            table(layout, keeps),
            emit,
            slab,
        )

    if 0 in dims:
        assembled(dims.index(0), None)
    count = layout.counts[0]
    height = value.shape[0] // count
    for slab in range(count):
        for place, dim in enumerate(dims):
            if dim != 0:
                assembled(place, slab)
        rows = slice(slab * height, (slab + 1) * height)
        summed[rows, :] = dot(split[rows, :], matrix[...])
        for element in layout.layer(0, slab):
            for each in range(3):
                at = (layout.rows(element), columns(each))
                result = summed[at] * factor(element, each)
                out[at] = combined(kind, None if begun is None else begun[at], result)


def combined(kind, begun, result):
    if begun is None:
        return result
    return begun - result if kind == "operator" else begun + result


def outside_faces(layout, here, dims, messages, masks):
    lane = lanes(layout)
    for dim in dims:
        outside = received(layout, here, dim, messages)
        lower, upper = layout.sides(dim)
        for where, element in enumerate(lower):
            mask = table(layout, masks)(element, dim)
            from_below, from_above = unpacked(lane, outside, where, mask)
            yield 2 * dim, where, element, from_below
            yield 2 * dim + 1, where, upper[where], from_above


def put_faces(layout, here, dim, messages, masks, factor, splits):
    low = lanes(layout) < FACE
    row_low = low[:1]
    for number, where, element, face in outside_faces(layout, here, (dim,), messages, masks):
        row = factor(element, dim)
        turned = pltpu.roll(row, FACE, 1)
        side = number % 2
        value = face * (jnp.where(row_low, turned, row) if side else jnp.where(row_low, row, turned))
        high = value.astype(jnp.bfloat16).astype(jnp.float32)
        rows = layout.pair_rows(where)
        splits[side][rows, :WIDTH] = jnp.where(low, value, value - high).astype(jnp.bfloat16)
        splits[side][rows, WIDTH:] = jnp.where(low, value, 0.0).astype(jnp.bfloat16)


def early_faces_kernel(layout, kind, order, *refs):
    messages, refs = taken(layout, EARLY, refs, order)
    masks, scaling, faces, begun, out, *scratch = refs
    count = 2 * len(EARLY)
    splits, sums = scratch[:count], scratch[count:]
    here = places()
    factor = scales(layout, kind, scaling)
    share = {}
    for place, dim in enumerate(EARLY):
        put_faces(layout, here, dim, messages, masks, factor, splits[2 * place : 2 * place + 2])
        for side, elements in enumerate(layout.sides(dim)):
            at = 2 * place + side
            sums[at][...] = dot(splits[at][...], faces[2 * dim + side])
            for where, element in enumerate(elements):
                share.setdefault(element, []).append((at, layout.pair_rows(where)))
    for element in layout.elements():
        for dim in DIMS:
            at = (layout.rows(element), columns(dim))
            parts = [sums[number][rows, columns(dim)] for number, rows in share.get(element, ())]
            if parts:
                result = sum(parts[1:], parts[0]) * factor(element, dim)
                out[at] = combined(kind, begun[at], result)
            else:
                out[at] = begun[at]


def late_faces_kernel(layout, kind, order, *refs):
    messages, refs = taken(layout, (LATE,), refs, order)
    masks, scaling, faces, begun, out, *refs = refs
    sent, splits = refs[: len(layout.turns())], refs[len(layout.turns()) :]
    here = places()
    factor = scales(layout, kind, scaling)
    put_faces(layout, here, LATE, messages, masks, factor, splits)
    edge = layout.edge()
    done = set()
    for side, elements in enumerate(layout.sides(LATE)):
        product = dot(splits[side][...], faces[2 * LATE + side])
        for where, element in enumerate(elements):
            rows = layout.pair_rows(edge.index(element))
            for dim in DIMS:
                part = product[layout.pair_rows(where), columns(dim)] * factor(element, dim)
                at = (rows, columns(dim))
                base = out[at] if element in done else begun[layout.rows(element), columns(dim)]
                out[at] = combined(kind, base, part)
            done.add(element)
    for dim in DIMS:
        pack(layout, here, dim, reader(layout, begun, out), table(layout, masks), sent)


def last_early_kernel(layout, whole, edges, *refs):
    value = reader(layout, whole, edges)
    messages, (masks, keeps, ready) = taken(layout, EARLY, refs)
    for dim in DIMS:

        def emit(element, result):
            ready[layout.rows(element), columns(dim)] = result

        assemble(
            layout,
            places(),
            dim,
            value,
            None if dim == LATE else messages,
            table(layout, masks),
            table(layout, keeps),
            emit,
        )


def last_late_kernel(layout, begun, *refs):
    messages, (masks, out, ready, left) = taken(layout, (LATE,), refs)
    low = lanes(layout) < FACE

    def copy(source, dim):
        return pltpu.make_async_copy(source, out.at[:, columns(dim)], left.at[dim])

    copies = [copy(begun.at[:, columns(dim)], dim) for dim in EARLY]
    for each in copies:
        each.start()
    added = {}
    for number, _, element, face in outside_faces(layout, places(), (LATE,), messages, masks):
        part = jnp.where(low, 0.0, face) if number % 2 else jnp.where(low, face, 0.0)
        added[element] = added[element] + part if element in added else part
    for element in layout.elements():
        value = begun[layout.rows(element), columns(LATE)]
        ready[layout.rows(element), :] = value + added[element] if element in added else value
    copies.append(copy(ready, LATE))
    copies[-1].start()
    for each in copies:
        each.wait()


def in_vmem(count):
    return [pl.BlockSpec(memory_space=pltpu.VMEM)] * count


def in_hbm(count):
    return [pl.BlockSpec(memory_space=pltpu.HBM)] * count


PARAMS = pltpu.CompilerParams(vmem_limit_bytes=VMEM_LIMIT)


def kept_in_hbm(*values):
    return [pltpu.with_memory_space_constraint(value, pltpu.HBM) for value in values]


def cost(flops, size):
    return pl.CostEstimate(flops=flops, bytes_accessed=size, transcendentals=0)


def partners(layout, dim, parity):
    sizes = layout.sizes
    swap = {}
    for place in np.ndindex(*sizes):
        other = list(place)
        lower = place[dim] % 2 == parity
        at = place[dim] + (1 if lower else -1)
        if 0 <= at < sizes[dim]:
            other[dim] = at
        elif dim != 1 and sizes[1] % 2 == 0:
            other[1] = place[1] ^ 1
        elif sizes[dim] % 2 == 0:
            other[dim] = sizes[dim] - 1 - place[dim]
        swap[place] = tuple(other)
    return [
        (int(np.ravel_multi_index(place, sizes)), int(np.ravel_multi_index(other, sizes)))
        for place, other in swap.items()
    ]


def exchange(layout, messages, order=TURNS):
    given = dict(zip(layout.turns(), messages))
    return {
        turn: lax.ppermute(given[turn], AXES, partners(layout, *turn))
        for turn in order
        if turn in given
    }


def body(
    load_raw,
    scaling,
    fine_matrix,
    fine_inverse,
    prolong_four,
    coarse_four,
    prolong_two,
    coarse_two,
    orient,
    boundary,
):
    counts, species, nodes = load_raw.shape[:3], load_raw.shape[3], load_raw.shape[4]
    layout = Layout(counts, species, tuple(lax.axis_size(axis) for axis in AXES))
    load = load_raw.reshape(-1, nodes)
    rows = load.shape[0]
    turns = layout.turns()
    message_shapes = tuple(layout.message(dim) for dim, _ in turns)
    whole = jax.ShapeDtypeStruct(load.shape, jnp.float32)
    matrix_shapes = (
        jax.ShapeDtypeStruct((3 * nodes, nodes), jnp.bfloat16),
        jax.ShapeDtypeStruct((2 * len(DIMS), 4 * FACE, nodes), jnp.bfloat16),
    )
    elements = len(layout.elements())
    tables = tuple(jax.ShapeDtypeStruct((elements, nodes), kind) for kind in (jnp.int32, jnp.float32))
    small = (scaling, prolong_four.T, coarse_four, prolong_two.T, coarse_two)
    sides = jnp.transpose(boundary, (1, 2, 3, 0))

    *sent, masks, keeps, load, scaling, four, coarse_four, two, coarse_two = pl.pallas_call(
        functools.partial(first_kernel, layout),
        out_shape=message_shapes
        + tables
        + (whole,)
        + tuple(jax.ShapeDtypeStruct(each.shape, each.dtype) for each in small),
        in_specs=in_hbm(3 + FETCHED),
        out_specs=tuple(in_vmem(len(turns) + 3 + FETCHED)),
        scratch_shapes=[
            pltpu.SMEM(orient.shape, jnp.int32),
            pltpu.SMEM(sides.shape, jnp.int32),
            pltpu.SemaphoreType.DMA((5 + FETCHED,)),
        ],
        compiler_params=PARAMS,
        name="pack",
    )(*kept_in_hbm(load, orient, sides, *small))

    stack = (rounded(prolong_four.shape[1]) + rounded(prolong_two.shape[1]), nodes)
    smoother = pl.pallas_call(
        smoother_kernel,
        out_shape=matrix_shapes,
        in_specs=in_vmem(5),
        out_specs=tuple(in_vmem(2)),
        scratch_shapes=[pltpu.VMEM(stack, jnp.float32), pltpu.VMEM(stack, jnp.float32)],
        compiler_params=PARAMS,
        cost_estimate=cost(2 * nodes * nodes * nodes, 8 * nodes * nodes),
        name="smoother",
    )(fine_inverse, four, coarse_four, two, coarse_two)
    operator = pl.pallas_call(
        operator_kernel,
        out_shape=matrix_shapes,
        in_specs=in_vmem(1),
        out_specs=tuple(in_vmem(2)),
        compiler_params=PARAMS,
        cost_estimate=cost(0, 10 * nodes * nodes),
        name="operator",
    )(fine_matrix)

    def scratch(dims):
        heights = [len(side) * species for dim in dims for side in layout.sides(dim)]
        splits = [pltpu.VMEM((height, 4 * FACE), jnp.bfloat16) for height in heights]
        return splits, [pltpu.VMEM((height, nodes), jnp.float32) for height in heights]

    edges = jax.ShapeDtypeStruct((len(layout.edge()) * species, nodes), jnp.float32)

    def stage(kind, value, sent, matrix, begun, order=TURNS):
        messages = exchange(layout, sent, order)
        begun = pl.pallas_call(
            functools.partial(local_kernel, layout, kind, (len(value), len(begun))),
            out_shape=whole,
            in_specs=in_vmem(4 + len(value) + len(begun)),
            out_specs=in_vmem(1)[0],
            scratch_shapes=[
                pltpu.VMEM((rows, 3 * nodes), jnp.bfloat16),
                pltpu.VMEM(load.shape, jnp.float32),
            ],
            compiler_params=PARAMS,
            cost_estimate=cost(rows * nodes, 0),
            name=kind + "_local",
        )(*value, *begun, masks, keeps, scaling, matrix[0])
        mine = [messages[turn] for turn in layout.turns(EARLY, order)]
        splits, sums = scratch(EARLY)
        begun = pl.pallas_call(
            functools.partial(early_faces_kernel, layout, kind, order),
            out_shape=whole,
            in_specs=in_vmem(4 + len(mine)),
            out_specs=in_vmem(1)[0],
            scratch_shapes=splits + sums,
            compiler_params=PARAMS,
            cost_estimate=cost(0, 0),
            name=kind + "_faces_early",
        )(*mine, masks, scaling, matrix[1], begun)
        mine = [messages[turn] for turn in layout.turns((LATE,), order)]
        changed, *sent = pl.pallas_call(
            functools.partial(late_faces_kernel, layout, kind, order),
            out_shape=(edges,) + message_shapes,
            in_specs=in_vmem(4 + len(mine)),
            out_specs=tuple(in_vmem(1 + len(turns))),
            scratch_shapes=scratch((LATE,))[0],
            compiler_params=PARAMS,
            cost_estimate=cost(0, 0),
            name=kind + "_faces_late",
        )(*mine, masks, scaling, matrix[1], begun)
        return (begun, changed), sent

    first, sent = stage("smooth", (load,), sent, smoother, (), FIRST_TURNS)
    left, sent = stage("operator", first, sent, operator, (load,))
    total, sent = stage("smooth_more", left, sent, smoother, first)
    messages = exchange(layout, sent)
    early = [messages[turn] for turn in layout.turns(EARLY)]
    late = [messages[turn] for turn in layout.turns((LATE,))]
    begun = pl.pallas_call(
        functools.partial(last_early_kernel, layout),
        out_shape=whole,
        in_specs=in_vmem(4 + len(early)),
        out_specs=in_vmem(1)[0],
        compiler_params=PARAMS,
        cost_estimate=cost(0, 8 * rows * nodes),
        name="last_early",
    )(*total, *early, masks, keeps)
    result = pl.pallas_call(
        functools.partial(last_late_kernel, layout),
        out_shape=whole,
        in_specs=in_vmem(2 + len(late)),
        out_specs=in_hbm(1)[0],
        scratch_shapes=[pltpu.VMEM((rows, WIDTH), jnp.float32), pltpu.SemaphoreType.DMA((3,))],
        compiler_params=PARAMS,
        cost_estimate=cost(0, 8 * rows * nodes),
        name="last_late",
    )(begun, *late, masks)
    return result.reshape(load_raw.shape)


def solution(mesh):
    in_specs = (
        P("ex", "ey", "ez", None, None),
        P("ex", "ey", "ez", None),
        P(),
        P(),
        P(),
        P(),
        P(),
        P(),
        P(None, "ex", "ey", "ez"),
        P(None, "ex", "ey", "ez"),
    )
    out_specs = P("ex", "ey", "ez", None, None)
    return jax.shard_map(body, mesh=mesh, in_specs=in_specs, out_specs=out_specs, check_vma=False)
```

profile of v0, /device:TPU:0, one launch (start us, length us, event | category | flops | bytes accessed | tf_op | source)
XLA Modules:
  0.0 32.3 jit_solution(8720040626391831122)
XLA Ops:
  0.0 1.6 %pack.1 = (f32[128,128]{1,0:T(8,128)S(1)}, f32[128,128]{1,0:T(8,128)S(1)}, f32[128,128]{1,0:T(8,128)S(1)}, f32[128,128]{1,0:T(8,128)S(1)}, f32[64,128]{1,0:T(8,1...) custom-call(f32[512,384]{1,0:T(8,128)} %bitcast.5, ...), custom_call_target="tpu_custom_call" | custom-call | tf_op jit(solution)/shard_map/pack/pallas_call | solution.py:612
  1.6 2.4 %collective-permute-start.1 = (f32[128,128]{1,0:T(8,128)S(1)}, f32[128,128]{1,0:T(8,128)S(1)}, u32[]{:S(2)}, u32[]{:S(2)}) collective-permute-start(f32[128,128]{1,0:T(8,128)S(1)} %get-tuple-element.48), channel_id=1, source_target_pairs={{0,6},{1,7},{2,4},{3,5},{4,2},{5,3},{6,0},{7,1},{8,14},{9,15},{10,... | collective-permute-start | bytes 196616 | tf_op jit(solution)/shard_map/ppermute | solution.py:578
  4.0 0.7 %collective-permute-start.2 = (f32[128,128]{1,0:T(8,128)S(1)}, f32[128,128]{1,0:T(8,128)S(1)}, u32[]{:S(2)}, u32[]{:S(2)}) collective-permute-start(f32[128,128]{1,0:T(8,128)S(1)} %get-tuple-element.49), channel_id=1, source_target_pairs={{0,2},{1,3},{2,0},{3,1},{4,6},{5,7},{6,4},{7,5},{8,16},{9,17},{10,... | collective-permute-start | bytes 196616 | tf_op jit(solution)/shard_map/ppermute | solution.py:578
  4.7 2.5 %collective-permute-start.3 = (f32[128,128]{1,0:T(8,128)S(1)}, f32[128,128]{1,0:T(8,128)S(1)}, u32[]{:S(2)}, u32[]{:S(2)}) collective-permute-start(f32[128,128]{1,0:T(8,128)S(1)} %get-tuple-element.50), channel_id=1, source_target_pairs={{0,8},{1,9},{2,10},{3,11},{4,12},{5,13},{6,14},{7,15},{8,0},{9,1},... | collective-permute-start | bytes 196616 | tf_op jit(solution)/shard_map/ppermute | solution.py:578
  7.2 0.1 collective-permute-start.4
  7.3 1.5 %collective-permute-start = (f32[64,128]{1,0:T(8,128)S(1)}, f32[64,128]{1,0:T(8,128)S(1)}, u32[]{:S(2)}, u32[]{:S(2)}) collective-permute-start(f32[64,128]{1,0:T(8,128)S(1)} %get-tuple-element.40), channel_id=1, source_target_pairs={{0,1},{1,0},{2,3},{3,2},{4,5},{5,4},{6,7},{7,6},{8,9},{9,8},{10,11... | collective-permute-start | bytes 98312 | tf_op jit(solution)/shard_map/ppermute | solution.py:578
  8.9 0.8 %smoother.1 = (bf16[1152,384]{1,0:T(8,128)(2,1)S(1)}, bf16[6,256,384]{2,1,0:T(8,128)(2,1)S(1)}) custom-call(f32[384,384]{1,0:T(8,128)S(1)} %copy-done.1, f32[98,384]{1,0:T(8,128)S(1)} %get-tuple-element.43.four, f32[98,98]{1,0:T(8,128)S(1)} %get-tuple-element.44.coarse_four, f32[26,384]{1,0:T(8,128)S(1)} %get-tuple-element.45.two, ...), custom_call_target="tpu_custom_call" | custom-call | flops 113246208 | bytes 1179648 | tf_op jit(solution)/shard_map/smoother/pallas_call | solution.py:630
  9.7 1.0 %smooth_local.1.refs_7_ = f32[512,384]{1,0:T(8,128)S(1)} custom-call(f32[512,384]{1,0:T(8,128)S(1)} %get-tuple-element.52.refs_0_.refs_2_, s32[16,384]{1,0:T(8,128)S(1)} %get-tuple-element.41.refs_1_.refs_4_.refs_3_, f32[16,384]{1,0:T(8,128)S(1)} %get-tuple-element.53.refs_2_.refs_4_.refs_5_, ...), custom_call_target="tpu_custom_call" | custom-call | flops 196608 | tf_op jit(solution)/shard_map/smooth_local/pallas_call | solution.py:659
  10.6 0.0 collective-permute-done.1.refs_0_
  10.7 0.0 collective-permute-done.2.refs_1_
  10.7 0.0 collective-permute-done.3.refs_2_
  10.7 0.6 %smooth_faces_early.1.refs_4_.refs_0_.refs_2_ = f32[512,384]{1,0:T(8,128)S(1)} custom-call(f32[128,128]{1,0:T(8,128)S(1)} %collective-permute-done.1.refs_0_, f32[128,128]{1,0:T(8,128)S(1)} %collective-permute-done.2.refs_1_, f32[128,128]{1,0:T(8,128)S(1)} %collective-permute-done.3.refs_2_, f32[128,128]{1,0:T(8,128)S(1)} %collective-permute-done.4.refs_3_, ...), custom_call_target="tpu_custom_call" | custom-call | tf_op jit(solution)/shard_map/smooth_faces_early/pallas_call | solution.py:674
  11.3 0.0 copy-start
  11.3 0.0 collective-permute-done.refs_0_
  11.3 0.5 %smooth_faces_late.1 = (f32[256,384]{1,0:T(8,128)S(1)}, f32[128,128]{1,0:T(8,128)S(1)}, f32[128,128]{1,0:T(8,128)S(1)}, f32[128,128]{1,0:T(8,128)S(1)}, f32[128,128]{1,0:T(8,128)S(1)}, /*index=5*/f32[64,128]{1,0:T(8,128)S(1)}) custom-call(f32[64,128]{1,0:T(8,128)S(1)} %collective-permute-done.refs_0_, ...), custom_call_target="tpu_custom_call" | custom-call | tf_op jit(solution)/shard_map/smooth_faces_late/pallas_call | solution.py:685
  11.8 0.4 %collective-permute-start.6 = (f32[128,128]{1,0:T(8,128)S(1)}, f32[128,128]{1,0:T(8,128)S(1)}, u32[]{:S(2)}, u32[]{:S(2)}) collective-permute-start(f32[128,128]{1,0:T(8,128)S(1)} %get-tuple-element.57), channel_id=1, source_target_pairs={{0,6},{1,7},{2,4},{3,5},{4,2},{5,3},{6,0},{7,1},{8,14},{9,15},{10,... | collective-permute-start | bytes 196616 | tf_op jit(solution)/shard_map/ppermute | solution.py:578
  12.2 0.7 %collective-permute-start.7 = (f32[128,128]{1,0:T(8,128)S(1)}, f32[128,128]{1,0:T(8,128)S(1)}, u32[]{:S(2)}, u32[]{:S(2)}) collective-permute-start(f32[128,128]{1,0:T(8,128)S(1)} %get-tuple-element.58), channel_id=1, source_target_pairs={{0,8},{1,9},{2,10},{3,11},{4,12},{5,13},{6,14},{7,15},{8,0},{9,1},... | collective-permute-start | bytes 196616 | tf_op jit(solution)/shard_map/ppermute | solution.py:578
  12.9 0.3 collective-permute-start.8
  13.1 0.3 collective-permute-start.9
  13.4 1.5 %collective-permute-start.5 = (f32[64,128]{1,0:T(8,128)S(1)}, f32[64,128]{1,0:T(8,128)S(1)}, u32[]{:S(2)}, u32[]{:S(2)}) collective-permute-start(f32[64,128]{1,0:T(8,128)S(1)} %get-tuple-element.55), channel_id=1, source_target_pairs={{0,1},{1,0},{2,3},{3,2},{4,5},{5,4},{6,7},{7,6},{8,9},{9,8},{10,11... | collective-permute-start | bytes 98312 | tf_op jit(solution)/shard_map/ppermute | solution.py:578
  14.9 0.2 operator.1
  15.1 1.0 %operator_local.1.refs_7_ = f32[512,384]{1,0:T(8,128)S(1)} custom-call(f32[512,384]{1,0:T(8,128)S(1)} %smooth_faces_early.1.refs_4_.refs_0_.refs_2_, f32[256,384]{1,0:T(8,128)S(1)} %get-tuple-element.61.refs_1_.refs_3_, f32[512,384]{1,0:T(8,128)S(1)} %get-tuple-element.52.refs_0_.refs_2_, s32[16,384]{1,0:T(8,128)S(1)} %get-tuple-element.41.refs_1_.refs_4_.refs_3_, ...), custom_call_target="tpu_custom_call" | custom-call | flops 196608 | tf_op jit(solution)/shard_map/operator_local/pallas_call | solution.py:659
  16.1 0.0 collective-permute-done.6.refs_0_
  16.1 0.4 %collective-permute-done.7.refs_1_ = f32[128,128]{1,0:T(8,128)S(1)} collective-permute-done((f32[128,128]{1,0:T(8,128)S(1)}, f32[128,128]{1,0:T(8,128)S(1)}, u32[]{:S(2)}, u32[]{:S(2)}) %collective-permute-start.7) | collective-permute-done | bytes 65568 | tf_op jit(solution)/shard_map/ppermute | solution.py:578
  16.5 0.6 %operator_faces_early.1.refs_4_.refs_0_ = f32[512,384]{1,0:T(8,128)S(1)} custom-call(f32[128,128]{1,0:T(8,128)S(1)} %collective-permute-done.6.refs_0_, f32[128,128]{1,0:T(8,128)S(1)} %collective-permute-done.7.refs_1_, f32[128,128]{1,0:T(8,128)S(1)} %collective-permute-done.8.refs_2_, f32[128,128]{1,0:T(8,128)S(1)} %collective-permute-done.9.refs_3_, ...), custom_call_target="tpu_custom_call" | custom-call | tf_op jit(solution)/shard_map/operator_faces_early/pallas_call | solution.py:674
  17.1 0.2 collective-permute-done.5.refs_0_
  17.3 0.5 %operator_faces_late.1 = (f32[256,384]{1,0:T(8,128)S(1)}, f32[128,128]{1,0:T(8,128)S(1)}, f32[128,128]{1,0:T(8,128)S(1)}, f32[128,128]{1,0:T(8,128)S(1)}, f32[128,128]{1,0:T(8,128)S(1)}, /*index=5*/f32[64,128]{1,0:T(8,128)S(1)}) custom-call(f32[64,128]{1,0:T(8,128)S(1)} %collective-permute-done.5.refs_0_, ...), custom_call_target="tpu_custom_call" | custom-call | tf_op jit(solution)/shard_map/operator_faces_late/pallas_call | solution.py:685
  17.8 0.7 %collective-permute-start.10 = (f32[128,128]{1,0:T(8,128)S(1)}, f32[128,128]{1,0:T(8,128)S(1)}, u32[]{:S(2)}, u32[]{:S(2)}) collective-permute-start(f32[128,128]{1,0:T(8,128)S(1)} %get-tuple-element.63), channel_id=1, source_target_pairs={{0,6},{1,7},{2,4},{3,5},{4,2},{5,3},{6,0},{7,1},{8,14},{9,15},{10,... | collective-permute-start | bytes 196616 | tf_op jit(solution)/shard_map/ppermute | solution.py:578
  18.5 1.4 %collective-permute-start.11 = (f32[128,128]{1,0:T(8,128)S(1)}, f32[128,128]{1,0:T(8,128)S(1)}, u32[]{:S(2)}, u32[]{:S(2)}) collective-permute-start(f32[128,128]{1,0:T(8,128)S(1)} %get-tuple-element.64), channel_id=1, source_target_pairs={{0,8},{1,9},{2,10},{3,11},{4,12},{5,13},{6,14},{7,15},{8,0},{9,1},... | collective-permute-start | bytes 196616 | tf_op jit(solution)/shard_map/ppermute | solution.py:578
  19.9 1.1 %collective-permute-start.12 = (f32[128,128]{1,0:T(8,128)S(1)}, f32[128,128]{1,0:T(8,128)S(1)}, u32[]{:S(2)}, u32[]{:S(2)}) collective-permute-start(f32[128,128]{1,0:T(8,128)S(1)} %get-tuple-element.65), channel_id=1, source_target_pairs={{0,2},{1,3},{2,0},{3,1},{4,6},{5,7},{6,4},{7,5},{8,16},{9,17},{10,... | collective-permute-start | bytes 196616 | tf_op jit(solution)/shard_map/ppermute | solution.py:578
  20.9 0.0 collective-permute-start.13
  20.9 1.6 %collective-permute-start.14 = (f32[64,128]{1,0:T(8,128)S(1)}, f32[64,128]{1,0:T(8,128)S(1)}, u32[]{:S(2)}, u32[]{:S(2)}) collective-permute-start(f32[64,128]{1,0:T(8,128)S(1)} %get-tuple-element.68), channel_id=1, source_target_pairs={{0,1},{1,0},{2,3},{3,2},{4,5},{5,4},{6,7},{7,6},{8,9},{9,8},{10,11... | collective-permute-start | bytes 98312 | tf_op jit(solution)/shard_map/ppermute | solution.py:578
  22.5 1.0 %smooth_more_local.1.refs_7_ = f32[512,384]{1,0:T(8,128)S(1)} custom-call(f32[512,384]{1,0:T(8,128)S(1)} %operator_faces_early.1.refs_4_.refs_0_, f32[256,384]{1,0:T(8,128)S(1)} %get-tuple-element.67.refs_1_, f32[512,384]{1,0:T(8,128)S(1)} %smooth_faces_early.1.refs_4_.refs_0_.refs_2_, f32[256,384]{1,0:T(8,128)S(1)} %get-tuple-element.61.refs_1_.refs_3_, ...), custom_call_target="tpu_custom_call" | custom-call | flops 196608 | tf_op jit(solution)/shard_map/smooth_more_local/pallas_call | solution.py:659
  23.5 0.0 collective-permute-done.11.refs_1_
  23.5 0.0 collective-permute-done.12.refs_2_
  23.5 0.6 %smooth_more_faces_early.1.refs_4_.whole = f32[512,384]{1,0:T(8,128)S(1)} custom-call(f32[128,128]{1,0:T(8,128)S(1)} %collective-permute-done.10.refs_0_, f32[128,128]{1,0:T(8,128)S(1)} %collective-permute-done.11.refs_1_, f32[128,128]{1,0:T(8,128)S(1)} %collective-permute-done.12.refs_2_, f32[128,128]{1,0:T(8,128)S(1)} %collective-permute-done.13.refs_3_, ...), custom_call_target="tpu_custom_call" | custom-call | tf_op jit(solution)/shard_map/smooth_more_faces_early/pallas_call | solution.py:674
  24.2 0.6 %collective-permute-done.14.refs_0_ = f32[64,128]{1,0:T(8,128)S(1)} collective-permute-done((f32[64,128]{1,0:T(8,128)S(1)}, f32[64,128]{1,0:T(8,128)S(1)}, u32[]{:S(2)}, u32[]{:S(2)}) %collective-permute-start.14) | collective-permute-done | bytes 32800 | tf_op jit(solution)/shard_map/ppermute | solution.py:578
  24.8 0.5 %smooth_more_faces_late.1 = (f32[256,384]{1,0:T(8,128)S(1)}, f32[128,128]{1,0:T(8,128)S(1)}, f32[128,128]{1,0:T(8,128)S(1)}, f32[128,128]{1,0:T(8,128)S(1)}, f32...) custom-call(f32[64,128]{1,0:T(8,128)S(1)} %collective-permute-done.14.refs_0_, ...), custom_call_target="tpu_custom_call" | custom-call | tf_op jit(solution)/shard_map/smooth_more_faces_late/pallas_call | solution.py:685
  25.3 0.1 collective-permute-start.15
  25.4 1.5 %collective-permute-start.16 = (f32[128,128]{1,0:T(8,128)S(1)}, f32[128,128]{1,0:T(8,128)S(1)}, u32[]{:S(2)}, u32[]{:S(2)}) collective-permute-start(f32[128,128]{1,0:T(8,128)S(1)} %get-tuple-element.71), channel_id=1, source_target_pairs={{0,8},{1,9},{2,10},{3,11},{4,12},{5,13},{6,14},{7,15},{8,0},{9,1},... | collective-permute-start | bytes 196616 | tf_op jit(solution)/shard_map/ppermute | solution.py:578
  26.9 0.3 collective-permute-start.17
  27.2 0.2 collective-permute-start.18
  27.4 0.9 %collective-permute-start.19 = (f32[64,128]{1,0:T(8,128)S(1)}, f32[64,128]{1,0:T(8,128)S(1)}, u32[]{:S(2)}, u32[]{:S(2)}) collective-permute-start(f32[64,128]{1,0:T(8,128)S(1)} %get-tuple-element.74), channel_id=1, source_target_pairs={{0,1},{1,0},{2,3},{3,2},{4,5},{5,4},{6,7},{7,6},{8,9},{9,8},{10,11... | collective-permute-start | bytes 98312 | tf_op jit(solution)/shard_map/ppermute | solution.py:578
  28.4 1.0 %collective-permute-done.15.refs_0_ = f32[128,128]{1,0:T(8,128)S(1)} collective-permute-done((f32[128,128]{1,0:T(8,128)S(1)}, f32[128,128]{1,0:T(8,128)S(1)}, u32[]{:S(2)}, u32[]{:S(2)}) %collective-permute-start.15) | collective-permute-done | bytes 65568 | tf_op jit(solution)/shard_map/ppermute | solution.py:578
  29.3 0.9 %collective-permute-done.16.refs_1_ = f32[128,128]{1,0:T(8,128)S(1)} collective-permute-done((f32[128,128]{1,0:T(8,128)S(1)}, f32[128,128]{1,0:T(8,128)S(1)}, u32[]{:S(2)}, u32[]{:S(2)}) %collective-permute-start.16) | collective-permute-done | bytes 65568 | tf_op jit(solution)/shard_map/ppermute | solution.py:578
  30.3 0.5 %last_early.1.begun = f32[512,384]{1,0:T(8,128)S(1)} custom-call(f32[512,384]{1,0:T(8,128)S(1)} %smooth_more_faces_early.1.refs_4_.whole, f32[256,384]{1,0:T(8,128)S(1)} %get-tuple-element.69.edges, f32[128,128]{1,0:T(8,128)S(1)} %collective-permute-done.15.refs_0_, f32[128,128]{1,0:T(8,128)S(1)} %collective-permute-done.16.refs_1_, ...), custom_call_target="tpu_custom_call" | custom-call | bytes 1572864 | tf_op jit(solution)/shard_map/last_early/pallas_call | solution.py:703
  30.8 0.6 %collective-permute-done.19.refs_0_ = f32[64,128]{1,0:T(8,128)S(1)} collective-permute-done((f32[64,128]{1,0:T(8,128)S(1)}, f32[64,128]{1,0:T(8,128)S(1)}, u32[]{:S(2)}, u32[]{:S(2)}) %collective-permute-start.19) | collective-permute-done | bytes 32800 | tf_op jit(solution)/shard_map/ppermute | solution.py:578
  31.3 0.9 %last_late.1 = f32[512,384]{1,0:T(8,128)} custom-call(f32[512,384]{1,0:T(8,128)S(1)} %last_early.1.begun, f32[64,128]{1,0:T(8,128)S(1)} %collective-permute-done.19.refs_0_, s32[16,384]{1,0:T(8,128)S(1)} %get-tuple-element.41.refs_1_.refs_4_.refs_3_), custom_call_target="tpu_custom_call" | custom-call | bytes 1572864 | tf_op jit(solution)/shard_map/last_late/pallas_call | solution.py:712
  (10 shorter events, 0.0 us)
Async XLA Ops:
  0.0 8.9 %copy-start.1 = (f32[384,384]{1,0:T(8,128)S(1)}, f32[384,384]{1,0:T(8,128)}, u32[]{:S(2)}) copy-start(f32[384,384]{1,0:T(8,128)} %inverse.1) | copy-start | bytes 1769476
  1.6 9.1 %collective-permute-start.1 = (f32[128,128]{1,0:T(8,128)S(1)}, f32[128,128]{1,0:T(8,128)S(1)}, u32[]{:S(2)}, u32[]{:S(2)}) collective-permute-start(f32[128,128]{1,0:T(8,128)S(1)} %get-tuple-element.48), channel_id=1, source_target_pairs={{0,6},{1,7},{2,4},{3,5},{4,2},{5,3},{6,0},{7,1},{8,14},{9,15},{10,... | collective-permute-start | bytes 196616 | tf_op jit(solution)/shard_map/ppermute | solution.py:578
  4.0 6.6 %collective-permute-start.2 = (f32[128,128]{1,0:T(8,128)S(1)}, f32[128,128]{1,0:T(8,128)S(1)}, u32[]{:S(2)}, u32[]{:S(2)}) collective-permute-start(f32[128,128]{1,0:T(8,128)S(1)} %get-tuple-element.49), channel_id=1, source_target_pairs={{0,2},{1,3},{2,0},{3,1},{4,6},{5,7},{6,4},{7,5},{8,16},{9,17},{10,... | collective-permute-start | bytes 196616 | tf_op jit(solution)/shard_map/ppermute | solution.py:578
  4.7 6.0 %collective-permute-start.3 = (f32[128,128]{1,0:T(8,128)S(1)}, f32[128,128]{1,0:T(8,128)S(1)}, u32[]{:S(2)}, u32[]{:S(2)}) collective-permute-start(f32[128,128]{1,0:T(8,128)S(1)} %get-tuple-element.50), channel_id=1, source_target_pairs={{0,8},{1,9},{2,10},{3,11},{4,12},{5,13},{6,14},{7,15},{8,0},{9,1},... | collective-permute-start | bytes 196616 | tf_op jit(solution)/shard_map/ppermute | solution.py:578
  7.2 3.5 %collective-permute-start.4 = (f32[128,128]{1,0:T(8,128)S(1)}, f32[128,128]{1,0:T(8,128)S(1)}, u32[]{:S(2)}, u32[]{:S(2)}) collective-permute-start(f32[128,128]{1,0:T(8,128)S(1)} %get-tuple-element.51), channel_id=1, source_target_pairs={{0,2},{1,3},{2,0},{3,1},{4,6},{5,7},{6,4},{7,5},{8,10},{9,11},{10,... | collective-permute-start | bytes 196616 | tf_op jit(solution)/shard_map/ppermute | solution.py:578
  7.3 4.0 %collective-permute-start = (f32[64,128]{1,0:T(8,128)S(1)}, f32[64,128]{1,0:T(8,128)S(1)}, u32[]{:S(2)}, u32[]{:S(2)}) collective-permute-start(f32[64,128]{1,0:T(8,128)S(1)} %get-tuple-element.40), channel_id=1, source_target_pairs={{0,1},{1,0},{2,3},{3,2},{4,5},{5,4},{6,7},{7,6},{8,9},{9,8},{10,11... | collective-permute-start | bytes 98312 | tf_op jit(solution)/shard_map/ppermute | solution.py:578
  11.3 3.6 %copy-start = (f32[384,384]{1,0:T(8,128)S(1)}, f32[384,384]{1,0:T(8,128)}, u32[]{:S(2)}) copy-start(f32[384,384]{1,0:T(8,128)} %fine.1) | copy-start | bytes 1769476
  11.8 4.3 %collective-permute-start.6 = (f32[128,128]{1,0:T(8,128)S(1)}, f32[128,128]{1,0:T(8,128)S(1)}, u32[]{:S(2)}, u32[]{:S(2)}) collective-permute-start(f32[128,128]{1,0:T(8,128)S(1)} %get-tuple-element.57), channel_id=1, source_target_pairs={{0,6},{1,7},{2,4},{3,5},{4,2},{5,3},{6,0},{7,1},{8,14},{9,15},{10,... | collective-permute-start | bytes 196616 | tf_op jit(solution)/shard_map/ppermute | solution.py:578
  12.2 4.3 %collective-permute-start.7 = (f32[128,128]{1,0:T(8,128)S(1)}, f32[128,128]{1,0:T(8,128)S(1)}, u32[]{:S(2)}, u32[]{:S(2)}) collective-permute-start(f32[128,128]{1,0:T(8,128)S(1)} %get-tuple-element.58), channel_id=1, source_target_pairs={{0,8},{1,9},{2,10},{3,11},{4,12},{5,13},{6,14},{7,15},{8,0},{9,1},... | collective-permute-start | bytes 196616 | tf_op jit(solution)/shard_map/ppermute | solution.py:578
  12.9 3.6 %collective-permute-start.8 = (f32[128,128]{1,0:T(8,128)S(1)}, f32[128,128]{1,0:T(8,128)S(1)}, u32[]{:S(2)}, u32[]{:S(2)}) collective-permute-start(f32[128,128]{1,0:T(8,128)S(1)} %get-tuple-element.59), channel_id=1, source_target_pairs={{0,2},{1,3},{2,0},{3,1},{4,6},{5,7},{6,4},{7,5},{8,16},{9,17},{10,... | collective-permute-start | bytes 196616 | tf_op jit(solution)/shard_map/ppermute | solution.py:578
  13.1 3.4 %collective-permute-start.9 = (f32[128,128]{1,0:T(8,128)S(1)}, f32[128,128]{1,0:T(8,128)S(1)}, u32[]{:S(2)}, u32[]{:S(2)}) collective-permute-start(f32[128,128]{1,0:T(8,128)S(1)} %get-tuple-element.60), channel_id=1, source_target_pairs={{0,2},{1,3},{2,0},{3,1},{4,6},{5,7},{6,4},{7,5},{8,10},{9,11},{10,... | collective-permute-start | bytes 196616 | tf_op jit(solution)/shard_map/ppermute | solution.py:578
  13.4 3.9 %collective-permute-start.5 = (f32[64,128]{1,0:T(8,128)S(1)}, f32[64,128]{1,0:T(8,128)S(1)}, u32[]{:S(2)}, u32[]{:S(2)}) collective-permute-start(f32[64,128]{1,0:T(8,128)S(1)} %get-tuple-element.55), channel_id=1, source_target_pairs={{0,1},{1,0},{2,3},{3,2},{4,5},{5,4},{6,7},{7,6},{8,9},{9,8},{10,11... | collective-permute-start | bytes 98312 | tf_op jit(solution)/shard_map/ppermute | solution.py:578
  17.8 5.7 %collective-permute-start.10 = (f32[128,128]{1,0:T(8,128)S(1)}, f32[128,128]{1,0:T(8,128)S(1)}, u32[]{:S(2)}, u32[]{:S(2)}) collective-permute-start(f32[128,128]{1,0:T(8,128)S(1)} %get-tuple-element.63), channel_id=1, source_target_pairs={{0,6},{1,7},{2,4},{3,5},{4,2},{5,3},{6,0},{7,1},{8,14},{9,15},{10,... | collective-permute-start | bytes 196616 | tf_op jit(solution)/shard_map/ppermute | solution.py:578
  18.5 5.0 %collective-permute-start.11 = (f32[128,128]{1,0:T(8,128)S(1)}, f32[128,128]{1,0:T(8,128)S(1)}, u32[]{:S(2)}, u32[]{:S(2)}) collective-permute-start(f32[128,128]{1,0:T(8,128)S(1)} %get-tuple-element.64), channel_id=1, source_target_pairs={{0,8},{1,9},{2,10},{3,11},{4,12},{5,13},{6,14},{7,15},{8,0},{9,1},... | collective-permute-start | bytes 196616 | tf_op jit(solution)/shard_map/ppermute | solution.py:578
  19.9 3.7 %collective-permute-start.12 = (f32[128,128]{1,0:T(8,128)S(1)}, f32[128,128]{1,0:T(8,128)S(1)}, u32[]{:S(2)}, u32[]{:S(2)}) collective-permute-start(f32[128,128]{1,0:T(8,128)S(1)} %get-tuple-element.65), channel_id=1, source_target_pairs={{0,2},{1,3},{2,0},{3,1},{4,6},{5,7},{6,4},{7,5},{8,16},{9,17},{10,... | collective-permute-start | bytes 196616 | tf_op jit(solution)/shard_map/ppermute | solution.py:578
  20.9 2.6 %collective-permute-start.13 = (f32[128,128]{1,0:T(8,128)S(1)}, f32[128,128]{1,0:T(8,128)S(1)}, u32[]{:S(2)}, u32[]{:S(2)}) collective-permute-start(f32[128,128]{1,0:T(8,128)S(1)} %get-tuple-element.66), channel_id=1, source_target_pairs={{0,2},{1,3},{2,0},{3,1},{4,6},{5,7},{6,4},{7,5},{8,10},{9,11},{10,... | collective-permute-start | bytes 196616 | tf_op jit(solution)/shard_map/ppermute | solution.py:578
  20.9 3.9 %collective-permute-start.14 = (f32[64,128]{1,0:T(8,128)S(1)}, f32[64,128]{1,0:T(8,128)S(1)}, u32[]{:S(2)}, u32[]{:S(2)}) collective-permute-start(f32[64,128]{1,0:T(8,128)S(1)} %get-tuple-element.68), channel_id=1, source_target_pairs={{0,1},{1,0},{2,3},{3,2},{4,5},{5,4},{6,7},{7,6},{8,9},{9,8},{10,11... | collective-permute-start | bytes 98312 | tf_op jit(solution)/shard_map/ppermute | solution.py:578
  25.3 4.0 %collective-permute-start.15 = (f32[128,128]{1,0:T(8,128)S(1)}, f32[128,128]{1,0:T(8,128)S(1)}, u32[]{:S(2)}, u32[]{:S(2)}) collective-permute-start(f32[128,128]{1,0:T(8,128)S(1)} %get-tuple-element.70), channel_id=1, source_target_pairs={{0,6},{1,7},{2,4},{3,5},{4,2},{5,3},{6,0},{7,1},{8,14},{9,15},{10,... | collective-permute-start | bytes 196616 | tf_op jit(solution)/shard_map/ppermute | solution.py:578
  25.4 4.9 %collective-permute-start.16 = (f32[128,128]{1,0:T(8,128)S(1)}, f32[128,128]{1,0:T(8,128)S(1)}, u32[]{:S(2)}, u32[]{:S(2)}) collective-permute-start(f32[128,128]{1,0:T(8,128)S(1)} %get-tuple-element.71), channel_id=1, source_target_pairs={{0,8},{1,9},{2,10},{3,11},{4,12},{5,13},{6,14},{7,15},{8,0},{9,1},... | collective-permute-start | bytes 196616 | tf_op jit(solution)/shard_map/ppermute | solution.py:578
  26.9 3.3 %collective-permute-start.17 = (f32[128,128]{1,0:T(8,128)S(1)}, f32[128,128]{1,0:T(8,128)S(1)}, u32[]{:S(2)}, u32[]{:S(2)}) collective-permute-start(f32[128,128]{1,0:T(8,128)S(1)} %get-tuple-element.72), channel_id=1, source_target_pairs={{0,2},{1,3},{2,0},{3,1},{4,6},{5,7},{6,4},{7,5},{8,16},{9,17},{10,... | collective-permute-start | bytes 196616 | tf_op jit(solution)/shard_map/ppermute | solution.py:578
  27.2 3.1 %collective-permute-start.18 = (f32[128,128]{1,0:T(8,128)S(1)}, f32[128,128]{1,0:T(8,128)S(1)}, u32[]{:S(2)}, u32[]{:S(2)}) collective-permute-start(f32[128,128]{1,0:T(8,128)S(1)} %get-tuple-element.73), channel_id=1, source_target_pairs={{0,2},{1,3},{2,0},{3,1},{4,6},{5,7},{6,4},{7,5},{8,10},{9,11},{10,... | collective-permute-start | bytes 196616 | tf_op jit(solution)/shard_map/ppermute | solution.py:578
  27.4 3.9 %collective-permute-start.19 = (f32[64,128]{1,0:T(8,128)S(1)}, f32[64,128]{1,0:T(8,128)S(1)}, u32[]{:S(2)}, u32[]{:S(2)}) collective-permute-start(f32[64,128]{1,0:T(8,128)S(1)} %get-tuple-element.74), channel_id=1, source_target_pairs={{0,1},{1,0},{2,3},{3,2},{4,5},{5,4},{6,7},{7,6},{8,9},{9,8},{10,11... | collective-permute-start | bytes 98312 | tf_op jit(solution)/shard_map/ppermute | solution.py:578
where the time goes:
time: 32.4 us; the launch traced here: 32.3 us
  starting transfers between devices  18.1 us (56%)
  Pallas kernels  10.2 us (31%)
  waiting for transfers between devices  3.71 us (11%)
    ppermute x20, starting transfers between devices, exchange(): lax.ppermute(given[turn], AXES, partners(layout, *turn))  18.1 us
    ppermute x20, waiting for transfers between devices, exchange(): lax.ppermute(given[turn], AXES, partners(layout, *turn))  3.71 us
    pallas_call x3, Pallas kernels, stage(): pl.pallas_call(functools.partial(local_kernel, layout, kind, (len(value),...  2.97 us
    pallas_call x3, Pallas kernels, stage(): pl.pallas_call(functools.partial(early_faces_kernel, layout, kind, order)...  1.9 us
    pallas_call x1, Pallas kernels, body(): pl.pallas_call(functools.partial(first_kernel, layout), out_shape=message...  1.56 us
    pallas_call x3, Pallas kernels, stage(): pl.pallas_call(functools.partial(late_faces_kernel, layout, kind, order),...  1.41 us
    pallas_call x1, Pallas kernels, body(): pl.pallas_call(functools.partial(last_late_kernel, layout), out_shape=who...  0.91 us
    pallas_call x1, Pallas kernels, body(): pl.pallas_call(smoother_kernel, out_shape=matrix_shapes, in_specs=in_vmem...  0.79 us
  transfers between devices with their start and end apart: 20, of which 6 were waited for; matrix products, arithmetic and copies ran while one was open for 0% of the time, Pallas kernels for 20%

commit v1 on v0

--- a/solution.py
+++ b/solution.py
@@ -39,10 +39,22 @@
         return slice(start, start + self.species)
 
     def layer(self, dim, position):
-        return [element for element in self.elements() if element[dim] == position]
+        found = [element for element in self.elements() if element[dim] == position]
+        return sorted(found, key=lambda element: (element[:LATE], element not in self.edge()))
 
     def pairs(self, dim):
         return (len(self.layer(dim, 0)) + 1) // 2
+
+    def early_pairs(self, dim):
+        first, edge = self.layer(dim, 0), self.edge()
+        ends = [(2 * pair, min(2 * pair + 1, len(first) - 1)) for pair in range(self.pairs(dim))]
+        if dim == LATE:
+            return []
+        return [
+            pair
+            for pair, places in enumerate(ends)
+            if not any(first[place] in edge for place in places)
+        ]
 
     def pair_rows(self, pair):
         return slice(pair * self.species, (pair + 1) * self.species)
@@ -84,7 +96,7 @@
     return [lax.axis_index(axis) for axis in AXES]
 
 
-def pack(layout, here, dim, load_block, mask_of, outs):
+def pack(layout, here, dim, load_block, mask_of, outs, only=None):
     turns = [(turn, out) for turn, out in zip(layout.turns(), outs) if turn[0] == dim]
     if not turns:
         return
@@ -93,7 +105,7 @@
     even = (here[dim] & 1) == 0
     first = layout.layer(dim, 0)
     last = layout.layer(dim, layout.counts[dim] - 1)
-    for pair in range(layout.pairs(dim)):
+    for pair in range(layout.pairs(dim)) if only is None else only:
         sides = []
         for half in range(2):
             where = min(2 * pair + half, len(first) - 1)
@@ -443,9 +455,9 @@
 
 def early_faces_kernel(layout, kind, order, *refs):
     messages, refs = taken(layout, EARLY, refs, order)
-    masks, scaling, faces, begun, out, *scratch = refs
-    count = 2 * len(EARLY)
-    splits, sums = scratch[:count], scratch[count:]
+    turns, count = len(layout.turns(EARLY)), 2 * len(EARLY)
+    masks, scaling, faces, begun, out, *refs = refs
+    ready, splits, sums = refs[:turns], refs[turns : turns + count], refs[turns + count :]
     here = places()
     factor = scales(layout, kind, scaling)
     share = {}
@@ -465,10 +477,22 @@
                 out[at] = combined(kind, begun[at], result)
             else:
                 out[at] = begun[at]
+    outs = dict(zip(layout.turns(EARLY), ready))
+    for dim in EARLY:
+        pack(
+            layout,
+            here,
+            dim,
+            reader(layout, out),
+            table(layout, masks),
+            [outs.get(turn) for turn in layout.turns()],
+            layout.early_pairs(dim),
+        )
 
 
 def late_faces_kernel(layout, kind, order, *refs):
     messages, refs = taken(layout, (LATE,), refs, order)
+    ready, refs = taken(layout, EARLY, refs)
     masks, scaling, faces, begun, out, *refs = refs
     sent, splits = refs[: len(layout.turns())], refs[len(layout.turns()) :]
     here = places()
@@ -486,8 +510,14 @@
                 base = out[at] if element in done else begun[layout.rows(element), columns(dim)]
                 out[at] = combined(kind, base, part)
             done.add(element)
+    for turn, message in zip(layout.turns(), sent):
+        for pair in layout.early_pairs(turn[0]):
+            rows = layout.pair_rows(pair)
+            message[rows, :] = ready[turn][rows, :]
     for dim in DIMS:
-        pack(layout, here, dim, reader(layout, begun, out), table(layout, masks), sent)
+        early = layout.early_pairs(dim)
+        only = [pair for pair in range(layout.pairs(dim)) if pair not in early]
+        pack(layout, here, dim, reader(layout, begun, out), table(layout, masks), sent, only)
 
 
 def last_early_kernel(layout, whole, edges, *refs):
@@ -671,11 +701,12 @@
         )(*value, *begun, masks, keeps, scaling, matrix[0])
         mine = [messages[turn] for turn in layout.turns(EARLY, order)]
         splits, sums = scratch(EARLY)
-        begun = pl.pallas_call(
+        early_turns = layout.turns(EARLY)
+        begun, *ready = pl.pallas_call(
             functools.partial(early_faces_kernel, layout, kind, order),
-            out_shape=whole,
+            out_shape=(whole,) + tuple(layout.message(dim) for dim, _ in early_turns),
             in_specs=in_vmem(4 + len(mine)),
-            out_specs=in_vmem(1)[0],
+            out_specs=tuple(in_vmem(1 + len(early_turns))),
             scratch_shapes=splits + sums,
             compiler_params=PARAMS,
             cost_estimate=cost(0, 0),
@@ -685,13 +716,13 @@
         changed, *sent = pl.pallas_call(
             functools.partial(late_faces_kernel, layout, kind, order),
             out_shape=(edges,) + message_shapes,
-            in_specs=in_vmem(4 + len(mine)),
+            in_specs=in_vmem(4 + len(mine) + len(ready)),
             out_specs=tuple(in_vmem(1 + len(turns))),
             scratch_shapes=scratch((LATE,))[0],
             compiler_params=PARAMS,
             cost_estimate=cost(0, 0),
             name=kind + "_faces_late",
-        )(*mine, masks, scaling, matrix[1], begun)
+        )(*mine, *ready, masks, scaling, matrix[1], begun)
         return (begun, changed), sent
 
     first, sent = stage("smooth", (load,), sent, smoother, (), FIRST_TURNS)

time: 32.4 us -> 32.4 us (level)
  no operation moved by 1% of the time
where the time goes in v1:
time: 32.4 us; the launch traced here: 32.3 us
  starting transfers between devices  18.1 us (56%)
  Pallas kernels  10.4 us (32%)
  waiting for transfers between devices  3.54 us (11%)
    ppermute x20, starting transfers between devices, exchange(): lax.ppermute(given[turn], AXES, partners(layout, *turn))  18.1 us
    ppermute x20, waiting for transfers between devices, exchange(): lax.ppermute(given[turn], AXES, partners(layout, *turn))  3.54 us
    pallas_call x3, Pallas kernels, stage(): pl.pallas_call(functools.partial(local_kernel, layout, kind, (len(value),...  2.97 us
    pallas_call x3, Pallas kernels, stage(): pl.pallas_call(functools.partial(early_faces_kernel, layout, kind, order)...  2.08 us
    pallas_call x1, Pallas kernels, body(): pl.pallas_call(functools.partial(first_kernel, layout), out_shape=message...  1.56 us
    pallas_call x3, Pallas kernels, stage(): pl.pallas_call(functools.partial(late_faces_kernel, layout, kind, order),...  1.37 us
    pallas_call x1, Pallas kernels, body(): pl.pallas_call(functools.partial(last_late_kernel, layout), out_shape=who...  0.91 us
    pallas_call x1, Pallas kernels, body(): pl.pallas_call(smoother_kernel, out_shape=matrix_shapes, in_specs=in_vmem...  0.79 us
  transfers between devices with their start and end apart: 20, of which 6 were waited for; matrix products, arithmetic and copies ran while one was open for 0% of the time, Pallas kernels for 20%

profile of v1, /device:TPU:0, one launch (start us, length us, event | category | flops | bytes accessed | tf_op | source)
XLA Modules:
  0.0 32.3 jit_solution(16171675850552469053)
XLA Ops:
  0.0 1.6 %pack.1 = (f32[128,128]{1,0:T(8,128)S(1)}, f32[128,128]{1,0:T(8,128)S(1)}, f32[128,128]{1,0:T(8,128)S(1)}, f32[128,128]{1,0:T(8,128)S(1)}, f32[64,128]{1,0:T(8,1...) custom-call(f32[512,384]{1,0:T(8,128)} %bitcast.5, ...), custom_call_target="tpu_custom_call" | custom-call | tf_op jit(solution)/shard_map/pack/pallas_call | solution.py:642
  1.6 2.4 %collective-permute-start.1 = (f32[128,128]{1,0:T(8,128)S(1)}, f32[128,128]{1,0:T(8,128)S(1)}, u32[]{:S(2)}, u32[]{:S(2)}) collective-permute-start(f32[128,128]{1,0:T(8,128)S(1)} %get-tuple-element.56), channel_id=1, source_target_pairs={{0,6},{1,7},{2,4},{3,5},{4,2},{5,3},{6,0},{7,1},{8,14},{9,15},{10,... | collective-permute-start | bytes 196616 | tf_op jit(solution)/shard_map/ppermute | solution.py:608
  4.0 0.7 %collective-permute-start.2 = (f32[128,128]{1,0:T(8,128)S(1)}, f32[128,128]{1,0:T(8,128)S(1)}, u32[]{:S(2)}, u32[]{:S(2)}) collective-permute-start(f32[128,128]{1,0:T(8,128)S(1)} %get-tuple-element.57), channel_id=1, source_target_pairs={{0,2},{1,3},{2,0},{3,1},{4,6},{5,7},{6,4},{7,5},{8,16},{9,17},{10,... | collective-permute-start | bytes 196616 | tf_op jit(solution)/shard_map/ppermute | solution.py:608
  4.7 2.5 %collective-permute-start.3 = (f32[128,128]{1,0:T(8,128)S(1)}, f32[128,128]{1,0:T(8,128)S(1)}, u32[]{:S(2)}, u32[]{:S(2)}) collective-permute-start(f32[128,128]{1,0:T(8,128)S(1)} %get-tuple-element.58), channel_id=1, source_target_pairs={{0,8},{1,9},{2,10},{3,11},{4,12},{5,13},{6,14},{7,15},{8,0},{9,1},... | collective-permute-start | bytes 196616 | tf_op jit(solution)/shard_map/ppermute | solution.py:608
  7.2 0.1 collective-permute-start.4
  7.3 1.5 %collective-permute-start = (f32[64,128]{1,0:T(8,128)S(1)}, f32[64,128]{1,0:T(8,128)S(1)}, u32[]{:S(2)}, u32[]{:S(2)}) collective-permute-start(f32[64,128]{1,0:T(8,128)S(1)} %get-tuple-element.55), channel_id=1, source_target_pairs={{0,1},{1,0},{2,3},{3,2},{4,5},{5,4},{6,7},{7,6},{8,9},{9,8},{10,11... | collective-permute-start | bytes 98312 | tf_op jit(solution)/shard_map/ppermute | solution.py:608
  8.9 0.8 %smoother.1 = (bf16[1152,384]{1,0:T(8,128)(2,1)S(1)}, bf16[6,256,384]{2,1,0:T(8,128)(2,1)S(1)}) custom-call(f32[384,384]{1,0:T(8,128)S(1)} %copy-done.1, f32[98,384]{1,0:T(8,128)S(1)} %get-tuple-element.62.four, f32[98,98]{1,0:T(8,128)S(1)} %get-tuple-element.63.coarse_four, f32[26,384]{1,0:T(8,128)S(1)} %get-tuple-element.64.two, ...), custom_call_target="tpu_custom_call" | custom-call | flops 113246208 | bytes 1179648 | tf_op jit(solution)/shard_map/smoother/pallas_call | solution.py:660
  9.7 1.0 %smooth_local.1.refs_7_ = f32[512,384]{1,0:T(8,128)S(1)} custom-call(f32[512,384]{1,0:T(8,128)S(1)} %get-tuple-element.67.refs_0_.refs_2_, s32[16,384]{1,0:T(8,128)S(1)} %get-tuple-element.60.refs_1_.refs_4_.refs_5_.refs_3_, f32[16,384]{1,0:T(8,128)S(1)} %get-tuple-element.68.refs_2_.refs_4_.refs_5_, ...), custom_call_target="tpu_custom_call" | custom-call | flops 196608 | tf_op jit(solution)/shard_map/smooth_local/pallas_call | solution.py:689
  10.6 0.0 collective-permute-done.1.refs_0_
  10.7 0.0 collective-permute-done.2.refs_1_
  10.7 0.0 collective-permute-done.4.refs_3_
  10.7 0.7 %smooth_faces_early.1 = (f32[512,384]{1,0:T(8,128)S(1)}, f32[128,128]{1,0:T(8,128)S(1)}, f32[128,128]{1,0:T(8,128)S(1)}, f32[128,128]{1,0:T(8,128)S(1)}, f32[128,128]{1,0:T(8,128)S(1)}) custom-call(f32[128,128]{1,0:T(8,128)S(1)} %collective-permute-done.1.refs_0_, f32[128,128]{1,0:T(8,128)S(1)} %collective-permute-done.2.refs_1_, ...), custom_call_target="tpu_custom_call" | custom-call | tf_op jit(solution)/shard_map/smooth_faces_early/pallas_call | solution.py:705
  11.4 0.0 copy-start
  11.4 0.0 collective-permute-done.refs_0_
  11.4 0.5 %smooth_faces_late.1 = (f32[256,384]{1,0:T(8,128)S(1)}, f32[128,128]{1,0:T(8,128)S(1)}, f32[128,128]{1,0:T(8,128)S(1)}, f32[128,128]{1,0:T(8,128)S(1)}, f32[128,128]{1,0:T(8,128)S(1)}, /*index=5*/f32[64,128]{1,0:T(8,128)S(1)}) custom-call(f32[64,128]{1,0:T(8,128)S(1)} %collective-permute-done.refs_0_, f32[128,128]{1,0:T(8,128)S(1)} %get-tuple-element.70.refs_1_, ...), custom_call_target="tpu_custom_call" | custom-call | tf_op jit(solution)/shard_map/smooth_faces_late/pallas_call | solution.py:716
  11.9 0.4 %collective-permute-start.6 = (f32[128,128]{1,0:T(8,128)S(1)}, f32[128,128]{1,0:T(8,128)S(1)}, u32[]{:S(2)}, u32[]{:S(2)}) collective-permute-start(f32[128,128]{1,0:T(8,128)S(1)} %get-tuple-element.76), channel_id=1, source_target_pairs={{0,6},{1,7},{2,4},{3,5},{4,2},{5,3},{6,0},{7,1},{8,14},{9,15},{10,... | collective-permute-start | bytes 196616 | tf_op jit(solution)/shard_map/ppermute | solution.py:608
  12.2 0.7 %collective-permute-start.7 = (f32[128,128]{1,0:T(8,128)S(1)}, f32[128,128]{1,0:T(8,128)S(1)}, u32[]{:S(2)}, u32[]{:S(2)}) collective-permute-start(f32[128,128]{1,0:T(8,128)S(1)} %get-tuple-element.77), channel_id=1, source_target_pairs={{0,8},{1,9},{2,10},{3,11},{4,12},{5,13},{6,14},{7,15},{8,0},{9,1},... | collective-permute-start | bytes 196616 | tf_op jit(solution)/shard_map/ppermute | solution.py:608
  12.9 0.3 collective-permute-start.8
  13.2 0.3 collective-permute-start.9
  13.4 1.5 %collective-permute-start.5 = (f32[64,128]{1,0:T(8,128)S(1)}, f32[64,128]{1,0:T(8,128)S(1)}, u32[]{:S(2)}, u32[]{:S(2)}) collective-permute-start(f32[64,128]{1,0:T(8,128)S(1)} %get-tuple-element.75), channel_id=1, source_target_pairs={{0,1},{1,0},{2,3},{3,2},{4,5},{5,4},{6,7},{7,6},{8,9},{9,8},{10,11... | collective-permute-start | bytes 98312 | tf_op jit(solution)/shard_map/ppermute | solution.py:608
  15.0 0.2 operator.1
  15.1 1.0 %operator_local.1.refs_7_ = f32[512,384]{1,0:T(8,128)S(1)} custom-call(f32[512,384]{1,0:T(8,128)S(1)} %get-tuple-element.74.refs_8_.refs_0_.refs_2_, f32[256,384]{1,0:T(8,128)S(1)} %get-tuple-element.81.refs_1_.refs_3_, f32[512,384]{1,0:T(8,128)S(1)} %get-tuple-element.67.refs_0_.refs_2_, s32[16,384]{1,0:T(8,128)S(1)} %get-tuple-element.60.refs_1_.refs_4_.refs_5_.refs_3_, ...), custom_call_target="tpu_custom_call" | custom-call | flops 196608 | tf_op jit(solution)/shard_map/operator_local/pallas_call | solution.py:689
  16.1 0.0 collective-permute-done.6.refs_0_
  16.1 0.4 %collective-permute-done.7.refs_1_ = f32[128,128]{1,0:T(8,128)S(1)} collective-permute-done((f32[128,128]{1,0:T(8,128)S(1)}, f32[128,128]{1,0:T(8,128)S(1)}, u32[]{:S(2)}, u32[]{:S(2)}) %collective-permute-start.7) | collective-permute-done | bytes 65568 | tf_op jit(solution)/shard_map/ppermute | solution.py:608
  16.5 0.0 collective-permute-done.8.refs_2_
  16.5 0.0 collective-permute-done.9.refs_3_
  16.5 0.7 %operator_faces_early.1 = (f32[512,384]{1,0:T(8,128)S(1)}, f32[128,128]{1,0:T(8,128)S(1)}, f32[128,128]{1,0:T(8,128)S(1)}, f32[128,128]{1,0:T(8,128)S(1)}, f32[128,128]{1,0:T(8,128)S(1)}) custom-call(f32[128,128]{1,0:T(8,128)S(1)} %collective-permute-done.6.refs_0_, f32[128,128]{1,0:T(8,128)S(1)} %collective-permute-done.7.refs_1_, ...), custom_call_target="tpu_custom_call" | custom-call | tf_op jit(solution)/shard_map/operator_faces_early/pallas_call | solution.py:705
  17.2 0.1 collective-permute-done.5.refs_0_
  17.4 0.5 %operator_faces_late.1 = (f32[256,384]{1,0:T(8,128)S(1)}, f32[128,128]{1,0:T(8,128)S(1)}, f32[128,128]{1,0:T(8,128)S(1)}, f32[128,128]{1,0:T(8,128)S(1)}, f32[128,128]{1,0:T(8,128)S(1)}, /*index=5*/f32[64,128]{1,0:T(8,128)S(1)}) custom-call(f32[64,128]{1,0:T(8,128)S(1)} %collective-permute-done.5.refs_0_, f32[128,128]{1,0:T(8,128)S(1)} %get-tuple-element.83.refs_1_, ...), custom_call_target="tpu_custom_call" | custom-call | tf_op jit(solution)/shard_map/operator_faces_late/pallas_call | solution.py:716
  17.8 0.8 %collective-permute-start.10 = (f32[128,128]{1,0:T(8,128)S(1)}, f32[128,128]{1,0:T(8,128)S(1)}, u32[]{:S(2)}, u32[]{:S(2)}) collective-permute-start(f32[128,128]{1,0:T(8,128)S(1)} %get-tuple-element.88), channel_id=1, source_target_pairs={{0,6},{1,7},{2,4},{3,5},{4,2},{5,3},{6,0},{7,1},{8,14},{9,15},{10,... | collective-permute-start | bytes 196616 | tf_op jit(solution)/shard_map/ppermute | solution.py:608
  18.6 1.4 %collective-permute-start.11 = (f32[128,128]{1,0:T(8,128)S(1)}, f32[128,128]{1,0:T(8,128)S(1)}, u32[]{:S(2)}, u32[]{:S(2)}) collective-permute-start(f32[128,128]{1,0:T(8,128)S(1)} %get-tuple-element.89), channel_id=1, source_target_pairs={{0,8},{1,9},{2,10},{3,11},{4,12},{5,13},{6,14},{7,15},{8,0},{9,1},... | collective-permute-start | bytes 196616 | tf_op jit(solution)/shard_map/ppermute | solution.py:608
  20.0 1.1 %collective-permute-start.12 = (f32[128,128]{1,0:T(8,128)S(1)}, f32[128,128]{1,0:T(8,128)S(1)}, u32[]{:S(2)}, u32[]{:S(2)}) collective-permute-start(f32[128,128]{1,0:T(8,128)S(1)} %get-tuple-element.90), channel_id=1, source_target_pairs={{0,2},{1,3},{2,0},{3,1},{4,6},{5,7},{6,4},{7,5},{8,16},{9,17},{10,... | collective-permute-start | bytes 196616 | tf_op jit(solution)/shard_map/ppermute | solution.py:608
  21.0 1.5 %collective-permute-start.14 = (f32[64,128]{1,0:T(8,128)S(1)}, f32[64,128]{1,0:T(8,128)S(1)}, u32[]{:S(2)}, u32[]{:S(2)}) collective-permute-start(f32[64,128]{1,0:T(8,128)S(1)} %get-tuple-element.94), channel_id=1, source_target_pairs={{0,1},{1,0},{2,3},{3,2},{4,5},{5,4},{6,7},{7,6},{8,9},{9,8},{10,11... | collective-permute-start | bytes 98312 | tf_op jit(solution)/shard_map/ppermute | solution.py:608
  22.6 1.0 %smooth_more_local.1.refs_7_ = f32[512,384]{1,0:T(8,128)S(1)} custom-call(f32[512,384]{1,0:T(8,128)S(1)} %get-tuple-element.87.refs_8_.refs_0_, f32[256,384]{1,0:T(8,128)S(1)} %get-tuple-element.92.refs_1_, f32[512,384]{1,0:T(8,128)S(1)} %get-tuple-element.74.refs_8_.refs_0_.refs_2_, f32[256,384]{1,0:T(8,128)S(1)} %get-tuple-element.81.refs_1_.refs_3_, ...), custom_call_target="tpu_custom_call" | custom-call | flops 196608 | tf_op jit(solution)/shard_map/smooth_more_local/pallas_call | solution.py:689
  23.6 0.0 collective-permute-done.10.refs_0_
  23.6 0.7 %smooth_more_faces_early.1 = (f32[512,384]{1,0:T(8,128)S(1)}, f32[128,128]{1,0:T(8,128)S(1)}, f32[128,128]{1,0:T(8,128)S(1)}, f32[128,128]{1,0:T(8,128)S(1)}, f32[128,128]{1,0:T(8,128)S(1)}) custom-call(f32[128,128]{1,0:T(8,128)S(1)} %collective-permute-done.10.refs_0_, f32[128,128]{1,0:T(8,128)S(1)} %collective-permute-done.11.refs_1_, ...), custom_call_target="tpu_custom_call" | custom-call | tf_op jit(solution)/shard_map/smooth_more_faces_early/pallas_call | solution.py:705
  24.3 0.6 %collective-permute-done.14.refs_0_ = f32[64,128]{1,0:T(8,128)S(1)} collective-permute-done((f32[64,128]{1,0:T(8,128)S(1)}, f32[64,128]{1,0:T(8,128)S(1)}, u32[]{:S(2)}, u32[]{:S(2)}) %collective-permute-start.14) | collective-permute-done | bytes 32800 | tf_op jit(solution)/shard_map/ppermute | solution.py:608
  24.9 0.5 %smooth_more_faces_late.1 = (f32[256,384]{1,0:T(8,128)S(1)}, f32[128,128]{1,0:T(8,128)S(1)}, f32[128,128]{1,0:T(8,128)S(1)}, f32[128,128]{1,0:T(8,128)S(1)}, f32...) custom-call(f32[64,128]{1,0:T(8,128)S(1)} %collective-permute-done.14.refs_0_, f32[128,128]{1,0:T(8,128)S(1)} %get-tuple-element.95.refs_1_, ...), custom_call_target="tpu_custom_call" | custom-call | tf_op jit(solution)/shard_map/smooth_more_faces_late/pallas_call | solution.py:716
  25.4 0.1 collective-permute-start.15
  25.5 1.5 %collective-permute-start.16 = (f32[128,128]{1,0:T(8,128)S(1)}, f32[128,128]{1,0:T(8,128)S(1)}, u32[]{:S(2)}, u32[]{:S(2)}) collective-permute-start(f32[128,128]{1,0:T(8,128)S(1)} %get-tuple-element.101), channel_id=1, source_target_pairs={{0,8},{1,9},{2,10},{3,11},{4,12},{5,13},{6,14},{7,15},{8,0},{9,1},... | collective-permute-start | bytes 196616 | tf_op jit(solution)/shard_map/ppermute | solution.py:608
  26.9 0.3 collective-permute-start.17
  27.2 0.2 collective-permute-start.18
  27.5 1.0 %collective-permute-start.19 = (f32[64,128]{1,0:T(8,128)S(1)}, f32[64,128]{1,0:T(8,128)S(1)}, u32[]{:S(2)}, u32[]{:S(2)}) collective-permute-start(f32[64,128]{1,0:T(8,128)S(1)} %get-tuple-element.104), channel_id=1, source_target_pairs={{0,1},{1,0},{2,3},{3,2},{4,5},{5,4},{6,7},{7,6},{8,9},{9,8},{10,11... | collective-permute-start | bytes 98312 | tf_op jit(solution)/shard_map/ppermute | solution.py:608
  28.4 1.0 %collective-permute-done.15.refs_0_ = f32[128,128]{1,0:T(8,128)S(1)} collective-permute-done((f32[128,128]{1,0:T(8,128)S(1)}, f32[128,128]{1,0:T(8,128)S(1)}, u32[]{:S(2)}, u32[]{:S(2)}) %collective-permute-start.15) | collective-permute-done | bytes 65568 | tf_op jit(solution)/shard_map/ppermute | solution.py:608
  29.5 0.9 %collective-permute-done.16.refs_1_ = f32[128,128]{1,0:T(8,128)S(1)} collective-permute-done((f32[128,128]{1,0:T(8,128)S(1)}, f32[128,128]{1,0:T(8,128)S(1)}, u32[]{:S(2)}, u32[]{:S(2)}) %collective-permute-start.16) | collective-permute-done | bytes 65568 | tf_op jit(solution)/shard_map/ppermute | solution.py:608
  30.4 0.5 %last_early.1.begun = f32[512,384]{1,0:T(8,128)S(1)} custom-call(f32[512,384]{1,0:T(8,128)S(1)} %get-tuple-element.93.refs_8_.whole, f32[256,384]{1,0:T(8,128)S(1)} %get-tuple-element.99.edges, f32[128,128]{1,0:T(8,128)S(1)} %collective-permute-done.15.refs_0_, f32[128,128]{1,0:T(8,128)S(1)} %collective-permute-done.16.refs_1_, ...), custom_call_target="tpu_custom_call" | custom-call | bytes 1572864 | tf_op jit(solution)/shard_map/last_early/pallas_call | solution.py:734
  30.9 0.5 %collective-permute-done.19.refs_0_ = f32[64,128]{1,0:T(8,128)S(1)} collective-permute-done((f32[64,128]{1,0:T(8,128)S(1)}, f32[64,128]{1,0:T(8,128)S(1)}, u32[]{:S(2)}, u32[]{:S(2)}) %collective-permute-start.19) | collective-permute-done | bytes 32800 | tf_op jit(solution)/shard_map/ppermute | solution.py:608
  31.4 0.9 %last_late.1 = f32[512,384]{1,0:T(8,128)} custom-call(f32[512,384]{1,0:T(8,128)S(1)} %last_early.1.begun, f32[64,128]{1,0:T(8,128)S(1)} %collective-permute-done.19.refs_0_, s32[16,384]{1,0:T(8,128)S(1)} %get-tuple-element.60.refs_1_.refs_4_.refs_5_.refs_3_), custom_call_target="tpu_custom_call" | custom-call | bytes 1572864 | tf_op jit(solution)/shard_map/last_late/pallas_call | solution.py:743
  (10 shorter events, 0.0 us)
Async XLA Ops:
  0.0 8.9 %copy-start.1 = (f32[384,384]{1,0:T(8,128)S(1)}, f32[384,384]{1,0:T(8,128)}, u32[]{:S(2)}) copy-start(f32[384,384]{1,0:T(8,128)} %inverse.1) | copy-start | bytes 1769476
  1.6 9.1 %collective-permute-start.1 = (f32[128,128]{1,0:T(8,128)S(1)}, f32[128,128]{1,0:T(8,128)S(1)}, u32[]{:S(2)}, u32[]{:S(2)}) collective-permute-start(f32[128,128]{1,0:T(8,128)S(1)} %get-tuple-element.56), channel_id=1, source_target_pairs={{0,6},{1,7},{2,4},{3,5},{4,2},{5,3},{6,0},{7,1},{8,14},{9,15},{10,... | collective-permute-start | bytes 196616 | tf_op jit(solution)/shard_map/ppermute | solution.py:608
  4.0 6.6 %collective-permute-start.2 = (f32[128,128]{1,0:T(8,128)S(1)}, f32[128,128]{1,0:T(8,128)S(1)}, u32[]{:S(2)}, u32[]{:S(2)}) collective-permute-start(f32[128,128]{1,0:T(8,128)S(1)} %get-tuple-element.57), channel_id=1, source_target_pairs={{0,2},{1,3},{2,0},{3,1},{4,6},{5,7},{6,4},{7,5},{8,16},{9,17},{10,... | collective-permute-start | bytes 196616 | tf_op jit(solution)/shard_map/ppermute | solution.py:608
  4.7 6.0 %collective-permute-start.3 = (f32[128,128]{1,0:T(8,128)S(1)}, f32[128,128]{1,0:T(8,128)S(1)}, u32[]{:S(2)}, u32[]{:S(2)}) collective-permute-start(f32[128,128]{1,0:T(8,128)S(1)} %get-tuple-element.58), channel_id=1, source_target_pairs={{0,8},{1,9},{2,10},{3,11},{4,12},{5,13},{6,14},{7,15},{8,0},{9,1},... | collective-permute-start | bytes 196616 | tf_op jit(solution)/shard_map/ppermute | solution.py:608
  7.2 3.5 %collective-permute-start.4 = (f32[128,128]{1,0:T(8,128)S(1)}, f32[128,128]{1,0:T(8,128)S(1)}, u32[]{:S(2)}, u32[]{:S(2)}) collective-permute-start(f32[128,128]{1,0:T(8,128)S(1)} %get-tuple-element.59), channel_id=1, source_target_pairs={{0,2},{1,3},{2,0},{3,1},{4,6},{5,7},{6,4},{7,5},{8,10},{9,11},{10,... | collective-permute-start | bytes 196616 | tf_op jit(solution)/shard_map/ppermute | solution.py:608
  7.3 4.1 %collective-permute-start = (f32[64,128]{1,0:T(8,128)S(1)}, f32[64,128]{1,0:T(8,128)S(1)}, u32[]{:S(2)}, u32[]{:S(2)}) collective-permute-start(f32[64,128]{1,0:T(8,128)S(1)} %get-tuple-element.55), channel_id=1, source_target_pairs={{0,1},{1,0},{2,3},{3,2},{4,5},{5,4},{6,7},{7,6},{8,9},{9,8},{10,11... | collective-permute-start | bytes 98312 | tf_op jit(solution)/shard_map/ppermute | solution.py:608
  11.4 3.6 %copy-start = (f32[384,384]{1,0:T(8,128)S(1)}, f32[384,384]{1,0:T(8,128)}, u32[]{:S(2)}) copy-start(f32[384,384]{1,0:T(8,128)} %fine.1) | copy-start | bytes 1769476
  11.9 4.3 %collective-permute-start.6 = (f32[128,128]{1,0:T(8,128)S(1)}, f32[128,128]{1,0:T(8,128)S(1)}, u32[]{:S(2)}, u32[]{:S(2)}) collective-permute-start(f32[128,128]{1,0:T(8,128)S(1)} %get-tuple-element.76), channel_id=1, source_target_pairs={{0,6},{1,7},{2,4},{3,5},{4,2},{5,3},{6,0},{7,1},{8,14},{9,15},{10,... | collective-permute-start | bytes 196616 | tf_op jit(solution)/shard_map/ppermute | solution.py:608
  12.2 4.3 %collective-permute-start.7 = (f32[128,128]{1,0:T(8,128)S(1)}, f32[128,128]{1,0:T(8,128)S(1)}, u32[]{:S(2)}, u32[]{:S(2)}) collective-permute-start(f32[128,128]{1,0:T(8,128)S(1)} %get-tuple-element.77), channel_id=1, source_target_pairs={{0,8},{1,9},{2,10},{3,11},{4,12},{5,13},{6,14},{7,15},{8,0},{9,1},... | collective-permute-start | bytes 196616 | tf_op jit(solution)/shard_map/ppermute | solution.py:608
  12.9 3.6 %collective-permute-start.8 = (f32[128,128]{1,0:T(8,128)S(1)}, f32[128,128]{1,0:T(8,128)S(1)}, u32[]{:S(2)}, u32[]{:S(2)}) collective-permute-start(f32[128,128]{1,0:T(8,128)S(1)} %get-tuple-element.78), channel_id=1, source_target_pairs={{0,2},{1,3},{2,0},{3,1},{4,6},{5,7},{6,4},{7,5},{8,16},{9,17},{10,... | collective-permute-start | bytes 196616 | tf_op jit(solution)/shard_map/ppermute | solution.py:608
  13.2 3.4 %collective-permute-start.9 = (f32[128,128]{1,0:T(8,128)S(1)}, f32[128,128]{1,0:T(8,128)S(1)}, u32[]{:S(2)}, u32[]{:S(2)}) collective-permute-start(f32[128,128]{1,0:T(8,128)S(1)} %get-tuple-element.79), channel_id=1, source_target_pairs={{0,2},{1,3},{2,0},{3,1},{4,6},{5,7},{6,4},{7,5},{8,10},{9,11},{10,... | collective-permute-start | bytes 196616 | tf_op jit(solution)/shard_map/ppermute | solution.py:608
  13.4 3.9 %collective-permute-start.5 = (f32[64,128]{1,0:T(8,128)S(1)}, f32[64,128]{1,0:T(8,128)S(1)}, u32[]{:S(2)}, u32[]{:S(2)}) collective-permute-start(f32[64,128]{1,0:T(8,128)S(1)} %get-tuple-element.75), channel_id=1, source_target_pairs={{0,1},{1,0},{2,3},{3,2},{4,5},{5,4},{6,7},{7,6},{8,9},{9,8},{10,11... | collective-permute-start | bytes 98312 | tf_op jit(solution)/shard_map/ppermute | solution.py:608
  17.8 5.7 %collective-permute-start.10 = (f32[128,128]{1,0:T(8,128)S(1)}, f32[128,128]{1,0:T(8,128)S(1)}, u32[]{:S(2)}, u32[]{:S(2)}) collective-permute-start(f32[128,128]{1,0:T(8,128)S(1)} %get-tuple-element.88), channel_id=1, source_target_pairs={{0,6},{1,7},{2,4},{3,5},{4,2},{5,3},{6,0},{7,1},{8,14},{9,15},{10,... | collective-permute-start | bytes 196616 | tf_op jit(solution)/shard_map/ppermute | solution.py:608
  18.6 5.0 %collective-permute-start.11 = (f32[128,128]{1,0:T(8,128)S(1)}, f32[128,128]{1,0:T(8,128)S(1)}, u32[]{:S(2)}, u32[]{:S(2)}) collective-permute-start(f32[128,128]{1,0:T(8,128)S(1)} %get-tuple-element.89), channel_id=1, source_target_pairs={{0,8},{1,9},{2,10},{3,11},{4,12},{5,13},{6,14},{7,15},{8,0},{9,1},... | collective-permute-start | bytes 196616 | tf_op jit(solution)/shard_map/ppermute | solution.py:608
  20.0 3.6 %collective-permute-start.12 = (f32[128,128]{1,0:T(8,128)S(1)}, f32[128,128]{1,0:T(8,128)S(1)}, u32[]{:S(2)}, u32[]{:S(2)}) collective-permute-start(f32[128,128]{1,0:T(8,128)S(1)} %get-tuple-element.90), channel_id=1, source_target_pairs={{0,2},{1,3},{2,0},{3,1},{4,6},{5,7},{6,4},{7,5},{8,16},{9,17},{10,... | collective-permute-start | bytes 196616 | tf_op jit(solution)/shard_map/ppermute | solution.py:608
  21.0 2.6 %collective-permute-start.13 = (f32[128,128]{1,0:T(8,128)S(1)}, f32[128,128]{1,0:T(8,128)S(1)}, u32[]{:S(2)}, u32[]{:S(2)}) collective-permute-start(f32[128,128]{1,0:T(8,128)S(1)} %get-tuple-element.91), channel_id=1, source_target_pairs={{0,2},{1,3},{2,0},{3,1},{4,6},{5,7},{6,4},{7,5},{8,10},{9,11},{10,... | collective-permute-start | bytes 196616 | tf_op jit(solution)/shard_map/ppermute | solution.py:608
  21.0 3.9 %collective-permute-start.14 = (f32[64,128]{1,0:T(8,128)S(1)}, f32[64,128]{1,0:T(8,128)S(1)}, u32[]{:S(2)}, u32[]{:S(2)}) collective-permute-start(f32[64,128]{1,0:T(8,128)S(1)} %get-tuple-element.94), channel_id=1, source_target_pairs={{0,1},{1,0},{2,3},{3,2},{4,5},{5,4},{6,7},{7,6},{8,9},{9,8},{10,11... | collective-permute-start | bytes 98312 | tf_op jit(solution)/shard_map/ppermute | solution.py:608
  25.4 4.1 %collective-permute-start.15 = (f32[128,128]{1,0:T(8,128)S(1)}, f32[128,128]{1,0:T(8,128)S(1)}, u32[]{:S(2)}, u32[]{:S(2)}) collective-permute-start(f32[128,128]{1,0:T(8,128)S(1)} %get-tuple-element.100), channel_id=1, source_target_pairs={{0,6},{1,7},{2,4},{3,5},{4,2},{5,3},{6,0},{7,1},{8,14},{9,15},{10,... | collective-permute-start | bytes 196616 | tf_op jit(solution)/shard_map/ppermute | solution.py:608
  25.5 4.9 %collective-permute-start.16 = (f32[128,128]{1,0:T(8,128)S(1)}, f32[128,128]{1,0:T(8,128)S(1)}, u32[]{:S(2)}, u32[]{:S(2)}) collective-permute-start(f32[128,128]{1,0:T(8,128)S(1)} %get-tuple-element.101), channel_id=1, source_target_pairs={{0,8},{1,9},{2,10},{3,11},{4,12},{5,13},{6,14},{7,15},{8,0},{9,1},... | collective-permute-start | bytes 196616 | tf_op jit(solution)/shard_map/ppermute | solution.py:608
  26.9 3.4 %collective-permute-start.17 = (f32[128,128]{1,0:T(8,128)S(1)}, f32[128,128]{1,0:T(8,128)S(1)}, u32[]{:S(2)}, u32[]{:S(2)}) collective-permute-start(f32[128,128]{1,0:T(8,128)S(1)} %get-tuple-element.102), channel_id=1, source_target_pairs={{0,2},{1,3},{2,0},{3,1},{4,6},{5,7},{6,4},{7,5},{8,16},{9,17},{10,... | collective-permute-start | bytes 196616 | tf_op jit(solution)/shard_map/ppermute | solution.py:608
  27.2 3.1 %collective-permute-start.18 = (f32[128,128]{1,0:T(8,128)S(1)}, f32[128,128]{1,0:T(8,128)S(1)}, u32[]{:S(2)}, u32[]{:S(2)}) collective-permute-start(f32[128,128]{1,0:T(8,128)S(1)} %get-tuple-element.103), channel_id=1, source_target_pairs={{0,2},{1,3},{2,0},{3,1},{4,6},{5,7},{6,4},{7,5},{8,10},{9,11},{10,... | collective-permute-start | bytes 196616 | tf_op jit(solution)/shard_map/ppermute | solution.py:608
  27.5 3.9 %collective-permute-start.19 = (f32[64,128]{1,0:T(8,128)S(1)}, f32[64,128]{1,0:T(8,128)S(1)}, u32[]{:S(2)}, u32[]{:S(2)}) collective-permute-start(f32[64,128]{1,0:T(8,128)S(1)} %get-tuple-element.104), channel_id=1, source_target_pairs={{0,1},{1,0},{2,3},{3,2},{4,5},{5,4},{6,7},{7,6},{8,9},{9,8},{10,11... | collective-permute-start | bytes 98312 | tf_op jit(solution)/shard_map/ppermute | solution.py:608

commit v2 on v0

--- a/solution.py
+++ b/solution.py
@@ -17,7 +17,7 @@
 DIMS = (0, 1, 2)
 EARLY = (1, 0)
 LATE = 2
-FETCHED = 5
+FETCHED = 4
 VMEM_LIMIT = 24 * 1024 * 1024
 
 
@@ -514,12 +514,9 @@
     messages, (masks, out, ready, left) = taken(layout, (LATE,), refs)
     low = lanes(layout) < FACE
 
-    def copy(source, dim):
-        return pltpu.make_async_copy(source, out.at[:, columns(dim)], left.at[dim])
-
-    copies = [copy(begun.at[:, columns(dim)], dim) for dim in EARLY]
-    for each in copies:
-        each.start()
+    cut = len(EARLY) * WIDTH
+    early = pltpu.make_async_copy(begun.at[:, :cut], out.at[:, :cut], left.at[0])
+    early.start()
     added = {}
     for number, _, element, face in outside_faces(layout, places(), (LATE,), messages, masks):
         part = jnp.where(low, 0.0, face) if number % 2 else jnp.where(low, face, 0.0)
@@ -527,10 +524,10 @@
     for element in layout.elements():
         value = begun[layout.rows(element), columns(LATE)]
         ready[layout.rows(element), :] = value + added[element] if element in added else value
-    copies.append(copy(ready, LATE))
-    copies[-1].start()
-    for each in copies:
-        each.wait()
+    late = pltpu.make_async_copy(ready, out.at[:, cut:], left.at[1])
+    late.start()
+    early.wait()
+    late.wait()
 
 
 def in_vmem(count):
@@ -606,10 +603,10 @@
     )
     elements = len(layout.elements())
     tables = tuple(jax.ShapeDtypeStruct((elements, nodes), kind) for kind in (jnp.int32, jnp.float32))
-    small = (scaling, prolong_four.T, coarse_four, prolong_two.T, coarse_two)
+    small = (scaling, coarse_four, prolong_two.T, coarse_two)
     sides = jnp.transpose(boundary, (1, 2, 3, 0))
 
-    *sent, masks, keeps, load, scaling, four, coarse_four, two, coarse_two = pl.pallas_call(
+    *sent, masks, keeps, load, scaling, coarse_four, two, coarse_two = pl.pallas_call(
         functools.partial(first_kernel, layout),
         out_shape=message_shapes
         + tables
@@ -636,7 +633,7 @@
         compiler_params=PARAMS,
         cost_estimate=cost(2 * nodes * nodes * nodes, 8 * nodes * nodes),
         name="smoother",
-    )(fine_inverse, four, coarse_four, two, coarse_two)
+    )(fine_inverse, prolong_four.T, coarse_four, two, coarse_two)
     operator = pl.pallas_call(
         operator_kernel,
         out_shape=matrix_shapes,
@@ -714,7 +711,7 @@
         out_shape=whole,
         in_specs=in_vmem(2 + len(late)),
         out_specs=in_hbm(1)[0],
-        scratch_shapes=[pltpu.VMEM((rows, WIDTH), jnp.float32), pltpu.SemaphoreType.DMA((3,))],
+        scratch_shapes=[pltpu.VMEM((rows, WIDTH), jnp.float32), pltpu.SemaphoreType.DMA((2,))],
         compiler_params=PARAMS,
         cost_estimate=cost(0, 8 * rows * nodes),
         name="last_late",

time: 32.4 us -> 33.3 us (1.028)
  waiting for transfers between devices: 3.71 us -> 5.97 us
  starting transfers between devices: 18.1 us -> 15.9 us
  local copies, waits for them, and re-layouts: 0.01 us -> 0.92 us
    ppermute x20, waiting for transfers between devices: 3.71 us -> 5.97 us  [exchange(): lax.ppermute(given[turn], AXES, partners(layout, *turn))]
    ppermute x20, starting transfers between devices: 18.1 us -> 15.9 us  [exchange(): lax.ppermute(given[turn], AXES, partners(layout, *turn))]
    unnamed x4 -> x6, local copies, waits for them, and re-layouts: 0.01 us -> 0.92 us
  transfers between devices with their start and end apart: 20 -> 20, of which waited for: 6 -> 7; matrix products, arithmetic and copies ran while one was open for 0% -> 0% of each run, Pallas kernels for 20% -> 19%
where the time goes in v2:
time: 33.3 us; the launch traced here: 33.2 us
  starting transfers between devices  15.9 us (48%)
  Pallas kernels  10.2 us (31%)
  waiting for transfers between devices  5.97 us (18%)
  local copies, waits for them, and re-layouts  0.92 us (3%)
    ppermute x20, starting transfers between devices, exchange(): lax.ppermute(given[turn], AXES, partners(layout, *turn))  15.9 us
    ppermute x20, waiting for transfers between devices, exchange(): lax.ppermute(given[turn], AXES, partners(layout, *turn))  5.97 us
    pallas_call x3, Pallas kernels, stage(): pl.pallas_call(functools.partial(local_kernel, layout, kind, (len(value),...  2.97 us
    pallas_call x3, Pallas kernels, stage(): pl.pallas_call(functools.partial(early_faces_kernel, layout, kind, order)...  1.9 us
    pallas_call x1, Pallas kernels, body(): pl.pallas_call(functools.partial(first_kernel, layout), out_shape=message...  1.55 us
    pallas_call x3, Pallas kernels, stage(): pl.pallas_call(functools.partial(late_faces_kernel, layout, kind, order),...  1.41 us
    unnamed x6, local copies, waits for them, and re-layouts  0.92 us
    pallas_call x1, Pallas kernels, body(): pl.pallas_call(functools.partial(last_late_kernel, layout), out_shape=who...  0.9 us
  transfers between devices with their start and end apart: 20, of which 7 were waited for; matrix products, arithmetic and copies ran while one was open for 0% of the time, Pallas kernels for 19%

profile of v2, /device:TPU:0, one launch (start us, length us, event | category | flops | bytes accessed | tf_op | source)
XLA Modules:
  0.0 33.2 jit_solution(14947791892995222800)
XLA Ops:
  0.0 1.6 %pack.1 = (f32[128,128]{1,0:T(8,128)S(1)}, f32[128,128]{1,0:T(8,128)S(1)}, f32[128,128]{1,0:T(8,128)S(1)}, f32[128,128]{1,0:T(8,128)S(1)}, f32[64,128]{1,0:T(8,1...) custom-call(f32[512,384]{1,0:T(8,128)} %bitcast.6, ...), custom_call_target="tpu_custom_call" | custom-call | tf_op jit(solution)/shard_map/pack/pallas_call | solution.py:609
  1.6 2.4 %collective-permute-start.1 = (f32[128,128]{1,0:T(8,128)S(1)}, f32[128,128]{1,0:T(8,128)S(1)}, u32[]{:S(2)}, u32[]{:S(2)}) collective-permute-start(f32[128,128]{1,0:T(8,128)S(1)} %get-tuple-element.46), channel_id=1, source_target_pairs={{0,6},{1,7},{2,4},{3,5},{4,2},{5,3},{6,0},{7,1},{8,14},{9,15},{10,... | collective-permute-start | bytes 196616 | tf_op jit(solution)/shard_map/ppermute | solution.py:575
  4.0 0.7 %collective-permute-start.2 = (f32[128,128]{1,0:T(8,128)S(1)}, f32[128,128]{1,0:T(8,128)S(1)}, u32[]{:S(2)}, u32[]{:S(2)}) collective-permute-start(f32[128,128]{1,0:T(8,128)S(1)} %get-tuple-element.47), channel_id=1, source_target_pairs={{0,2},{1,3},{2,0},{3,1},{4,6},{5,7},{6,4},{7,5},{8,16},{9,17},{10,... | collective-permute-start | bytes 196616 | tf_op jit(solution)/shard_map/ppermute | solution.py:575
  4.7 2.5 %collective-permute-start.3 = (f32[128,128]{1,0:T(8,128)S(1)}, f32[128,128]{1,0:T(8,128)S(1)}, u32[]{:S(2)}, u32[]{:S(2)}) collective-permute-start(f32[128,128]{1,0:T(8,128)S(1)} %get-tuple-element.48), channel_id=1, source_target_pairs={{0,8},{1,9},{2,10},{3,11},{4,12},{5,13},{6,14},{7,15},{8,0},{9,1},... | collective-permute-start | bytes 196616 | tf_op jit(solution)/shard_map/ppermute | solution.py:575
  7.2 0.1 collective-permute-start.4
  7.3 1.5 %collective-permute-start = (f32[64,128]{1,0:T(8,128)S(1)}, f32[64,128]{1,0:T(8,128)S(1)}, u32[]{:S(2)}, u32[]{:S(2)}) collective-permute-start(f32[64,128]{1,0:T(8,128)S(1)} %get-tuple-element.39), channel_id=1, source_target_pairs={{0,1},{1,0},{2,3},{3,2},{4,5},{5,4},{6,7},{7,6},{8,9},{9,8},{10,11... | collective-permute-start | bytes 98312 | tf_op jit(solution)/shard_map/ppermute | solution.py:575
  8.9 0.9 %copy-done.2 = f32[384,98]{0,1:T(8,128)S(1)} copy-done((f32[384,98]{0,1:T(8,128)S(1)}, f32[384,98]{0,1:T(8,128)}, u32[]{:S(2)}) %copy-start.2) | copy-done | bytes 150552
  9.8 0.8 %smoother.1 = (bf16[1152,384]{1,0:T(8,128)(2,1)S(1)}, bf16[6,256,384]{2,1,0:T(8,128)(2,1)S(1)}) custom-call(f32[384,384]{1,0:T(8,128)S(1)} %copy-done.1, f32[98,384]{1,0:T(8,128)S(1)} %bitcast.5, f32[98,98]{1,0:T(8,128)S(1)} %get-tuple-element.42.coarse_four, f32[26,384]{1,0:T(8,128)S(1)} %get-tuple-element.43.two, f32[26,26]{1,0:T(8,128)S(1)} %get-tuple-element.44.coarse_two), custom_call_target="tpu_custom_call" | custom-call | flops 113246208 | bytes 1179648 | tf_op jit(solution)/shard_map/smoother/pallas_call | solution.py:627
  10.6 1.0 %smooth_local.1.refs_7_ = f32[512,384]{1,0:T(8,128)S(1)} custom-call(f32[512,384]{1,0:T(8,128)S(1)} %get-tuple-element.50.refs_0_.refs_2_, s32[16,384]{1,0:T(8,128)S(1)} %get-tuple-element.40.refs_1_.refs_4_.refs_3_, f32[16,384]{1,0:T(8,128)S(1)} %get-tuple-element.51.refs_2_.refs_4_.refs_5_, ...), custom_call_target="tpu_custom_call" | custom-call | flops 196608 | tf_op jit(solution)/shard_map/smooth_local/pallas_call | solution.py:656
  11.5 0.0 collective-permute-done.1.refs_0_
  11.6 0.0 collective-permute-done.2.refs_1_
  11.6 0.0 collective-permute-done.3.refs_2_
  11.6 0.6 %smooth_faces_early.1.refs_4_.refs_0_.refs_2_ = f32[512,384]{1,0:T(8,128)S(1)} custom-call(f32[128,128]{1,0:T(8,128)S(1)} %collective-permute-done.1.refs_0_, f32[128,128]{1,0:T(8,128)S(1)} %collective-permute-done.2.refs_1_, f32[128,128]{1,0:T(8,128)S(1)} %collective-permute-done.3.refs_2_, f32[128,128]{1,0:T(8,128)S(1)} %collective-permute-done.4.refs_3_, ...), custom_call_target="tpu_custom_call" | custom-call | tf_op jit(solution)/shard_map/smooth_faces_early/pallas_call | solution.py:671
  12.2 0.0 copy-start
  12.2 0.5 %smooth_faces_late.1 = (f32[256,384]{1,0:T(8,128)S(1)}, f32[128,128]{1,0:T(8,128)S(1)}, f32[128,128]{1,0:T(8,128)S(1)}, f32[128,128]{1,0:T(8,128)S(1)}, f32[128,128]{1,0:T(8,128)S(1)}, /*index=5*/f32[64,128]{1,0:T(8,128)S(1)}) custom-call(f32[64,128]{1,0:T(8,128)S(1)} %collective-permute-done.refs_0_, ...), custom_call_target="tpu_custom_call" | custom-call | tf_op jit(solution)/shard_map/smooth_faces_late/pallas_call | solution.py:682
  12.7 0.4 %collective-permute-start.6 = (f32[128,128]{1,0:T(8,128)S(1)}, f32[128,128]{1,0:T(8,128)S(1)}, u32[]{:S(2)}, u32[]{:S(2)}) collective-permute-start(f32[128,128]{1,0:T(8,128)S(1)} %get-tuple-element.55), channel_id=1, source_target_pairs={{0,6},{1,7},{2,4},{3,5},{4,2},{5,3},{6,0},{7,1},{8,14},{9,15},{10,... | collective-permute-start | bytes 196616 | tf_op jit(solution)/shard_map/ppermute | solution.py:575
  13.1 0.0 collective-permute-start.7
  13.1 0.3 collective-permute-start.8
  13.4 0.2 collective-permute-start.9
  13.6 1.3 %collective-permute-start.5 = (f32[64,128]{1,0:T(8,128)S(1)}, f32[64,128]{1,0:T(8,128)S(1)}, u32[]{:S(2)}, u32[]{:S(2)}) collective-permute-start(f32[64,128]{1,0:T(8,128)S(1)} %get-tuple-element.53), channel_id=1, source_target_pairs={{0,1},{1,0},{2,3},{3,2},{4,5},{5,4},{6,7},{7,6},{8,9},{9,8},{10,11... | collective-permute-start | bytes 98312 | tf_op jit(solution)/shard_map/ppermute | solution.py:575
  14.9 0.2 operator.1
  15.1 1.0 %operator_local.1.refs_7_ = f32[512,384]{1,0:T(8,128)S(1)} custom-call(f32[512,384]{1,0:T(8,128)S(1)} %smooth_faces_early.1.refs_4_.refs_0_.refs_2_, f32[256,384]{1,0:T(8,128)S(1)} %get-tuple-element.59.refs_1_.refs_3_, f32[512,384]{1,0:T(8,128)S(1)} %get-tuple-element.50.refs_0_.refs_2_, s32[16,384]{1,0:T(8,128)S(1)} %get-tuple-element.40.refs_1_.refs_4_.refs_3_, ...), custom_call_target="tpu_custom_call" | custom-call | flops 196608 | tf_op jit(solution)/shard_map/operator_local/pallas_call | solution.py:656
  16.1 0.9 %collective-permute-done.6.refs_0_ = f32[128,128]{1,0:T(8,128)S(1)} collective-permute-done((f32[128,128]{1,0:T(8,128)S(1)}, f32[128,128]{1,0:T(8,128)S(1)}, u32[]{:S(2)}, u32[]{:S(2)}) %collective-permute-start.6) | collective-permute-done | bytes 65568 | tf_op jit(solution)/shard_map/ppermute | solution.py:575
  16.9 0.5 %collective-permute-done.7.refs_1_ = f32[128,128]{1,0:T(8,128)S(1)} collective-permute-done((f32[128,128]{1,0:T(8,128)S(1)}, f32[128,128]{1,0:T(8,128)S(1)}, u32[]{:S(2)}, u32[]{:S(2)}) %collective-permute-start.7) | collective-permute-done | bytes 65568 | tf_op jit(solution)/shard_map/ppermute | solution.py:575
  17.4 0.0 collective-permute-done.8.refs_2_
  17.4 0.0 collective-permute-done.9.refs_3_
  17.4 0.6 %operator_faces_early.1.refs_4_.refs_0_ = f32[512,384]{1,0:T(8,128)S(1)} custom-call(f32[128,128]{1,0:T(8,128)S(1)} %collective-permute-done.6.refs_0_, f32[128,128]{1,0:T(8,128)S(1)} %collective-permute-done.7.refs_1_, f32[128,128]{1,0:T(8,128)S(1)} %collective-permute-done.8.refs_2_, f32[128,128]{1,0:T(8,128)S(1)} %collective-permute-done.9.refs_3_, ...), custom_call_target="tpu_custom_call" | custom-call | tf_op jit(solution)/shard_map/operator_faces_early/pallas_call | solution.py:671
  18.0 0.5 %operator_faces_late.1 = (f32[256,384]{1,0:T(8,128)S(1)}, f32[128,128]{1,0:T(8,128)S(1)}, f32[128,128]{1,0:T(8,128)S(1)}, f32[128,128]{1,0:T(8,128)S(1)}, f32[128,128]{1,0:T(8,128)S(1)}, /*index=5*/f32[64,128]{1,0:T(8,128)S(1)}) custom-call(f32[64,128]{1,0:T(8,128)S(1)} %collective-permute-done.5.refs_0_, ...), custom_call_target="tpu_custom_call" | custom-call | tf_op jit(solution)/shard_map/operator_faces_late/pallas_call | solution.py:682
  18.5 0.9 %collective-permute-start.10 = (f32[128,128]{1,0:T(8,128)S(1)}, f32[128,128]{1,0:T(8,128)S(1)}, u32[]{:S(2)}, u32[]{:S(2)}) collective-permute-start(f32[128,128]{1,0:T(8,128)S(1)} %get-tuple-element.61), channel_id=1, source_target_pairs={{0,6},{1,7},{2,4},{3,5},{4,2},{5,3},{6,0},{7,1},{8,14},{9,15},{10,... | collective-permute-start | bytes 196616 | tf_op jit(solution)/shard_map/ppermute | solution.py:575
  19.4 1.3 %collective-permute-start.11 = (f32[128,128]{1,0:T(8,128)S(1)}, f32[128,128]{1,0:T(8,128)S(1)}, u32[]{:S(2)}, u32[]{:S(2)}) collective-permute-start(f32[128,128]{1,0:T(8,128)S(1)} %get-tuple-element.62), channel_id=1, source_target_pairs={{0,8},{1,9},{2,10},{3,11},{4,12},{5,13},{6,14},{7,15},{8,0},{9,1},... | collective-permute-start | bytes 196616 | tf_op jit(solution)/shard_map/ppermute | solution.py:575
  20.7 1.1 %collective-permute-start.12 = (f32[128,128]{1,0:T(8,128)S(1)}, f32[128,128]{1,0:T(8,128)S(1)}, u32[]{:S(2)}, u32[]{:S(2)}) collective-permute-start(f32[128,128]{1,0:T(8,128)S(1)} %get-tuple-element.63), channel_id=1, source_target_pairs={{0,2},{1,3},{2,0},{3,1},{4,6},{5,7},{6,4},{7,5},{8,16},{9,17},{10,... | collective-permute-start | bytes 196616 | tf_op jit(solution)/shard_map/ppermute | solution.py:575
  21.8 0.0 collective-permute-start.13
  21.8 0.5 %collective-permute-start.14 = (f32[64,128]{1,0:T(8,128)S(1)}, f32[64,128]{1,0:T(8,128)S(1)}, u32[]{:S(2)}, u32[]{:S(2)}) collective-permute-start(f32[64,128]{1,0:T(8,128)S(1)} %get-tuple-element.66), channel_id=1, source_target_pairs={{0,1},{1,0},{2,3},{3,2},{4,5},{5,4},{6,7},{7,6},{8,9},{9,8},{10,11... | collective-permute-start | bytes 98312 | tf_op jit(solution)/shard_map/ppermute | solution.py:575
  22.3 1.0 %smooth_more_local.1.refs_7_ = f32[512,384]{1,0:T(8,128)S(1)} custom-call(f32[512,384]{1,0:T(8,128)S(1)} %operator_faces_early.1.refs_4_.refs_0_, f32[256,384]{1,0:T(8,128)S(1)} %get-tuple-element.65.refs_1_, f32[512,384]{1,0:T(8,128)S(1)} %smooth_faces_early.1.refs_4_.refs_0_.refs_2_, f32[256,384]{1,0:T(8,128)S(1)} %get-tuple-element.59.refs_1_.refs_3_, ...), custom_call_target="tpu_custom_call" | custom-call | flops 196608 | tf_op jit(solution)/shard_map/smooth_more_local/pallas_call | solution.py:656
  23.3 1.0 %collective-permute-done.11.refs_1_ = f32[128,128]{1,0:T(8,128)S(1)} collective-permute-done((f32[128,128]{1,0:T(8,128)S(1)}, f32[128,128]{1,0:T(8,128)S(1)}, u32[]{:S(2)}, u32[]{:S(2)}) %collective-permute-start.11) | collective-permute-done | bytes 65568 | tf_op jit(solution)/shard_map/ppermute | solution.py:575
  24.4 0.6 %smooth_more_faces_early.1.refs_4_.whole = f32[512,384]{1,0:T(8,128)S(1)} custom-call(f32[128,128]{1,0:T(8,128)S(1)} %collective-permute-done.10.refs_0_, f32[128,128]{1,0:T(8,128)S(1)} %collective-permute-done.11.refs_1_, f32[128,128]{1,0:T(8,128)S(1)} %collective-permute-done.12.refs_2_, f32[128,128]{1,0:T(8,128)S(1)} %collective-permute-done.13.refs_3_, ...), custom_call_target="tpu_custom_call" | custom-call | tf_op jit(solution)/shard_map/smooth_more_faces_early/pallas_call | solution.py:671
  25.0 0.7 %collective-permute-done.14.refs_0_ = f32[64,128]{1,0:T(8,128)S(1)} collective-permute-done((f32[64,128]{1,0:T(8,128)S(1)}, f32[64,128]{1,0:T(8,128)S(1)}, u32[]{:S(2)}, u32[]{:S(2)}) %collective-permute-start.14) | collective-permute-done | bytes 32800 | tf_op jit(solution)/shard_map/ppermute | solution.py:575
  25.7 0.5 %smooth_more_faces_late.1 = (f32[256,384]{1,0:T(8,128)S(1)}, f32[128,128]{1,0:T(8,128)S(1)}, f32[128,128]{1,0:T(8,128)S(1)}, f32[128,128]{1,0:T(8,128)S(1)}, f32...) custom-call(f32[64,128]{1,0:T(8,128)S(1)} %collective-permute-done.14.refs_0_, ...), custom_call_target="tpu_custom_call" | custom-call | tf_op jit(solution)/shard_map/smooth_more_faces_late/pallas_call | solution.py:682
  26.2 0.1 collective-permute-start.15
  26.3 1.5 %collective-permute-start.16 = (f32[128,128]{1,0:T(8,128)S(1)}, f32[128,128]{1,0:T(8,128)S(1)}, u32[]{:S(2)}, u32[]{:S(2)}) collective-permute-start(f32[128,128]{1,0:T(8,128)S(1)} %get-tuple-element.69), channel_id=1, source_target_pairs={{0,8},{1,9},{2,10},{3,11},{4,12},{5,13},{6,14},{7,15},{8,0},{9,1},... | collective-permute-start | bytes 196616 | tf_op jit(solution)/shard_map/ppermute | solution.py:575
  27.8 0.3 collective-permute-start.17
  28.1 0.2 collective-permute-start.18
  28.3 0.5 %collective-permute-start.19 = (f32[64,128]{1,0:T(8,128)S(1)}, f32[64,128]{1,0:T(8,128)S(1)}, u32[]{:S(2)}, u32[]{:S(2)}) collective-permute-start(f32[64,128]{1,0:T(8,128)S(1)} %get-tuple-element.72), channel_id=1, source_target_pairs={{0,1},{1,0},{2,3},{3,2},{4,5},{5,4},{6,7},{7,6},{8,9},{9,8},{10,11... | collective-permute-start | bytes 98312 | tf_op jit(solution)/shard_map/ppermute | solution.py:575
  28.8 1.4 %collective-permute-done.15.refs_0_ = f32[128,128]{1,0:T(8,128)S(1)} collective-permute-done((f32[128,128]{1,0:T(8,128)S(1)}, f32[128,128]{1,0:T(8,128)S(1)}, u32[]{:S(2)}, u32[]{:S(2)}) %collective-permute-start.15) | collective-permute-done | bytes 65568 | tf_op jit(solution)/shard_map/ppermute | solution.py:575
  30.2 1.0 %collective-permute-done.16.refs_1_ = f32[128,128]{1,0:T(8,128)S(1)} collective-permute-done((f32[128,128]{1,0:T(8,128)S(1)}, f32[128,128]{1,0:T(8,128)S(1)}, u32[]{:S(2)}, u32[]{:S(2)}) %collective-permute-start.16) | collective-permute-done | bytes 65568 | tf_op jit(solution)/shard_map/ppermute | solution.py:575
  31.2 0.5 %last_early.1.begun = f32[512,384]{1,0:T(8,128)S(1)} custom-call(f32[512,384]{1,0:T(8,128)S(1)} %smooth_more_faces_early.1.refs_4_.whole, f32[256,384]{1,0:T(8,128)S(1)} %get-tuple-element.67.edges, f32[128,128]{1,0:T(8,128)S(1)} %collective-permute-done.15.refs_0_, f32[128,128]{1,0:T(8,128)S(1)} %collective-permute-done.16.refs_1_, ...), custom_call_target="tpu_custom_call" | custom-call | bytes 1572864 | tf_op jit(solution)/shard_map/last_early/pallas_call | solution.py:700
  31.7 0.6 %collective-permute-done.19.refs_0_ = f32[64,128]{1,0:T(8,128)S(1)} collective-permute-done((f32[64,128]{1,0:T(8,128)S(1)}, f32[64,128]{1,0:T(8,128)S(1)}, u32[]{:S(2)}, u32[]{:S(2)}) %collective-permute-start.19) | collective-permute-done | bytes 32800 | tf_op jit(solution)/shard_map/ppermute | solution.py:575
  32.3 0.9 %last_late.1 = f32[512,384]{1,0:T(8,128)} custom-call(f32[512,384]{1,0:T(8,128)S(1)} %last_early.1.begun, f32[64,128]{1,0:T(8,128)S(1)} %collective-permute-done.19.refs_0_, s32[16,384]{1,0:T(8,128)S(1)} %get-tuple-element.40.refs_1_.refs_4_.refs_3_), custom_call_target="tpu_custom_call" | custom-call | bytes 1572864 | tf_op jit(solution)/shard_map/last_late/pallas_call | solution.py:709
  (12 shorter events, 0.0 us)
Async XLA Ops:
  0.0 8.8 %copy-start.1 = (f32[384,384]{1,0:T(8,128)S(1)}, f32[384,384]{1,0:T(8,128)}, u32[]{:S(2)}) copy-start(f32[384,384]{1,0:T(8,128)} %inverse.1) | copy-start | bytes 1769476
  1.6 10.0 %collective-permute-start.1 = (f32[128,128]{1,0:T(8,128)S(1)}, f32[128,128]{1,0:T(8,128)S(1)}, u32[]{:S(2)}, u32[]{:S(2)}) collective-permute-start(f32[128,128]{1,0:T(8,128)S(1)} %get-tuple-element.46), channel_id=1, source_target_pairs={{0,6},{1,7},{2,4},{3,5},{4,2},{5,3},{6,0},{7,1},{8,14},{9,15},{10,... | collective-permute-start | bytes 196616 | tf_op jit(solution)/shard_map/ppermute | solution.py:575
  4.0 7.6 %collective-permute-start.2 = (f32[128,128]{1,0:T(8,128)S(1)}, f32[128,128]{1,0:T(8,128)S(1)}, u32[]{:S(2)}, u32[]{:S(2)}) collective-permute-start(f32[128,128]{1,0:T(8,128)S(1)} %get-tuple-element.47), channel_id=1, source_target_pairs={{0,2},{1,3},{2,0},{3,1},{4,6},{5,7},{6,4},{7,5},{8,16},{9,17},{10,... | collective-permute-start | bytes 196616 | tf_op jit(solution)/shard_map/ppermute | solution.py:575
  4.7 6.9 %collective-permute-start.3 = (f32[128,128]{1,0:T(8,128)S(1)}, f32[128,128]{1,0:T(8,128)S(1)}, u32[]{:S(2)}, u32[]{:S(2)}) collective-permute-start(f32[128,128]{1,0:T(8,128)S(1)} %get-tuple-element.48), channel_id=1, source_target_pairs={{0,8},{1,9},{2,10},{3,11},{4,12},{5,13},{6,14},{7,15},{8,0},{9,1},... | collective-permute-start | bytes 196616 | tf_op jit(solution)/shard_map/ppermute | solution.py:575
  7.2 4.4 %collective-permute-start.4 = (f32[128,128]{1,0:T(8,128)S(1)}, f32[128,128]{1,0:T(8,128)S(1)}, u32[]{:S(2)}, u32[]{:S(2)}) collective-permute-start(f32[128,128]{1,0:T(8,128)S(1)} %get-tuple-element.49), channel_id=1, source_target_pairs={{0,2},{1,3},{2,0},{3,1},{4,6},{5,7},{6,4},{7,5},{8,10},{9,11},{10,... | collective-permute-start | bytes 196616 | tf_op jit(solution)/shard_map/ppermute | solution.py:575
  7.3 4.9 %collective-permute-start = (f32[64,128]{1,0:T(8,128)S(1)}, f32[64,128]{1,0:T(8,128)S(1)}, u32[]{:S(2)}, u32[]{:S(2)}) collective-permute-start(f32[64,128]{1,0:T(8,128)S(1)} %get-tuple-element.39), channel_id=1, source_target_pairs={{0,1},{1,0},{2,3},{3,2},{4,5},{5,4},{6,7},{7,6},{8,9},{9,8},{10,11... | collective-permute-start | bytes 98312 | tf_op jit(solution)/shard_map/ppermute | solution.py:575
  8.8 0.9 %copy-start.2 = (f32[384,98]{0,1:T(8,128)S(1)}, f32[384,98]{0,1:T(8,128)}, u32[]{:S(2)}) copy-start(f32[384,98]{0,1:T(8,128)} %param.14) | copy-start | bytes 451588
  12.2 2.7 %copy-start = (f32[384,384]{1,0:T(8,128)S(1)}, f32[384,384]{1,0:T(8,128)}, u32[]{:S(2)}) copy-start(f32[384,384]{1,0:T(8,128)} %fine.1) | copy-start | bytes 1769476
  12.7 4.2 %collective-permute-start.6 = (f32[128,128]{1,0:T(8,128)S(1)}, f32[128,128]{1,0:T(8,128)S(1)}, u32[]{:S(2)}, u32[]{:S(2)}) collective-permute-start(f32[128,128]{1,0:T(8,128)S(1)} %get-tuple-element.55), channel_id=1, source_target_pairs={{0,6},{1,7},{2,4},{3,5},{4,2},{5,3},{6,0},{7,1},{8,14},{9,15},{10,... | collective-permute-start | bytes 196616 | tf_op jit(solution)/shard_map/ppermute | solution.py:575
  13.1 4.3 %collective-permute-start.7 = (f32[128,128]{1,0:T(8,128)S(1)}, f32[128,128]{1,0:T(8,128)S(1)}, u32[]{:S(2)}, u32[]{:S(2)}) collective-permute-start(f32[128,128]{1,0:T(8,128)S(1)} %get-tuple-element.56), channel_id=1, source_target_pairs={{0,8},{1,9},{2,10},{3,11},{4,12},{5,13},{6,14},{7,15},{8,0},{9,1},... | collective-permute-start | bytes 196616 | tf_op jit(solution)/shard_map/ppermute | solution.py:575
  13.1 4.3 %collective-permute-start.8 = (f32[128,128]{1,0:T(8,128)S(1)}, f32[128,128]{1,0:T(8,128)S(1)}, u32[]{:S(2)}, u32[]{:S(2)}) collective-permute-start(f32[128,128]{1,0:T(8,128)S(1)} %get-tuple-element.57), channel_id=1, source_target_pairs={{0,2},{1,3},{2,0},{3,1},{4,6},{5,7},{6,4},{7,5},{8,16},{9,17},{10,... | collective-permute-start | bytes 196616 | tf_op jit(solution)/shard_map/ppermute | solution.py:575
  13.4 4.0 %collective-permute-start.9 = (f32[128,128]{1,0:T(8,128)S(1)}, f32[128,128]{1,0:T(8,128)S(1)}, u32[]{:S(2)}, u32[]{:S(2)}) collective-permute-start(f32[128,128]{1,0:T(8,128)S(1)} %get-tuple-element.58), channel_id=1, source_target_pairs={{0,2},{1,3},{2,0},{3,1},{4,6},{5,7},{6,4},{7,5},{8,10},{9,11},{10,... | collective-permute-start | bytes 196616 | tf_op jit(solution)/shard_map/ppermute | solution.py:575
  13.6 4.4 %collective-permute-start.5 = (f32[64,128]{1,0:T(8,128)S(1)}, f32[64,128]{1,0:T(8,128)S(1)}, u32[]{:S(2)}, u32[]{:S(2)}) collective-permute-start(f32[64,128]{1,0:T(8,128)S(1)} %get-tuple-element.53), channel_id=1, source_target_pairs={{0,1},{1,0},{2,3},{3,2},{4,5},{5,4},{6,7},{7,6},{8,9},{9,8},{10,11... | collective-permute-start | bytes 98312 | tf_op jit(solution)/shard_map/ppermute | solution.py:575
  18.5 4.8 %collective-permute-start.10 = (f32[128,128]{1,0:T(8,128)S(1)}, f32[128,128]{1,0:T(8,128)S(1)}, u32[]{:S(2)}, u32[]{:S(2)}) collective-permute-start(f32[128,128]{1,0:T(8,128)S(1)} %get-tuple-element.61), channel_id=1, source_target_pairs={{0,6},{1,7},{2,4},{3,5},{4,2},{5,3},{6,0},{7,1},{8,14},{9,15},{10,... | collective-permute-start | bytes 196616 | tf_op jit(solution)/shard_map/ppermute | solution.py:575
  19.4 4.9 %collective-permute-start.11 = (f32[128,128]{1,0:T(8,128)S(1)}, f32[128,128]{1,0:T(8,128)S(1)}, u32[]{:S(2)}, u32[]{:S(2)}) collective-permute-start(f32[128,128]{1,0:T(8,128)S(1)} %get-tuple-element.62), channel_id=1, source_target_pairs={{0,8},{1,9},{2,10},{3,11},{4,12},{5,13},{6,14},{7,15},{8,0},{9,1},... | collective-permute-start | bytes 196616 | tf_op jit(solution)/shard_map/ppermute | solution.py:575
  20.7 3.7 %collective-permute-start.12 = (f32[128,128]{1,0:T(8,128)S(1)}, f32[128,128]{1,0:T(8,128)S(1)}, u32[]{:S(2)}, u32[]{:S(2)}) collective-permute-start(f32[128,128]{1,0:T(8,128)S(1)} %get-tuple-element.63), channel_id=1, source_target_pairs={{0,2},{1,3},{2,0},{3,1},{4,6},{5,7},{6,4},{7,5},{8,16},{9,17},{10,... | collective-permute-start | bytes 196616 | tf_op jit(solution)/shard_map/ppermute | solution.py:575
  21.8 2.5 %collective-permute-start.13 = (f32[128,128]{1,0:T(8,128)S(1)}, f32[128,128]{1,0:T(8,128)S(1)}, u32[]{:S(2)}, u32[]{:S(2)}) collective-permute-start(f32[128,128]{1,0:T(8,128)S(1)} %get-tuple-element.64), channel_id=1, source_target_pairs={{0,2},{1,3},{2,0},{3,1},{4,6},{5,7},{6,4},{7,5},{8,10},{9,11},{10,... | collective-permute-start | bytes 196616 | tf_op jit(solution)/shard_map/ppermute | solution.py:575
  21.8 3.9 %collective-permute-start.14 = (f32[64,128]{1,0:T(8,128)S(1)}, f32[64,128]{1,0:T(8,128)S(1)}, u32[]{:S(2)}, u32[]{:S(2)}) collective-permute-start(f32[64,128]{1,0:T(8,128)S(1)} %get-tuple-element.66), channel_id=1, source_target_pairs={{0,1},{1,0},{2,3},{3,2},{4,5},{5,4},{6,7},{7,6},{8,9},{9,8},{10,11... | collective-permute-start | bytes 98312 | tf_op jit(solution)/shard_map/ppermute | solution.py:575
  26.2 4.0 %collective-permute-start.15 = (f32[128,128]{1,0:T(8,128)S(1)}, f32[128,128]{1,0:T(8,128)S(1)}, u32[]{:S(2)}, u32[]{:S(2)}) collective-permute-start(f32[128,128]{1,0:T(8,128)S(1)} %get-tuple-element.68), channel_id=1, source_target_pairs={{0,6},{1,7},{2,4},{3,5},{4,2},{5,3},{6,0},{7,1},{8,14},{9,15},{10,... | collective-permute-start | bytes 196616 | tf_op jit(solution)/shard_map/ppermute | solution.py:575
  26.3 4.9 %collective-permute-start.16 = (f32[128,128]{1,0:T(8,128)S(1)}, f32[128,128]{1,0:T(8,128)S(1)}, u32[]{:S(2)}, u32[]{:S(2)}) collective-permute-start(f32[128,128]{1,0:T(8,128)S(1)} %get-tuple-element.69), channel_id=1, source_target_pairs={{0,8},{1,9},{2,10},{3,11},{4,12},{5,13},{6,14},{7,15},{8,0},{9,1},... | collective-permute-start | bytes 196616 | tf_op jit(solution)/shard_map/ppermute | solution.py:575
  27.8 3.3 %collective-permute-start.17 = (f32[128,128]{1,0:T(8,128)S(1)}, f32[128,128]{1,0:T(8,128)S(1)}, u32[]{:S(2)}, u32[]{:S(2)}) collective-permute-start(f32[128,128]{1,0:T(8,128)S(1)} %get-tuple-element.70), channel_id=1, source_target_pairs={{0,2},{1,3},{2,0},{3,1},{4,6},{5,7},{6,4},{7,5},{8,16},{9,17},{10,... | collective-permute-start | bytes 196616 | tf_op jit(solution)/shard_map/ppermute | solution.py:575
  28.1 3.0 %collective-permute-start.18 = (f32[128,128]{1,0:T(8,128)S(1)}, f32[128,128]{1,0:T(8,128)S(1)}, u32[]{:S(2)}, u32[]{:S(2)}) collective-permute-start(f32[128,128]{1,0:T(8,128)S(1)} %get-tuple-element.71), channel_id=1, source_target_pairs={{0,2},{1,3},{2,0},{3,1},{4,6},{5,7},{6,4},{7,5},{8,10},{9,11},{10,... | collective-permute-start | bytes 196616 | tf_op jit(solution)/shard_map/ppermute | solution.py:575
  28.3 3.9 %collective-permute-start.19 = (f32[64,128]{1,0:T(8,128)S(1)}, f32[64,128]{1,0:T(8,128)S(1)}, u32[]{:S(2)}, u32[]{:S(2)}) collective-permute-start(f32[64,128]{1,0:T(8,128)S(1)} %get-tuple-element.72), channel_id=1, source_target_pairs={{0,1},{1,0},{2,3},{3,2},{4,5},{5,4},{6,7},{7,6},{8,9},{9,8},{10,11... | collective-permute-start | bytes 98312 | tf_op jit(solution)/shard_map/ppermute | solution.py:575

commit v3 on v0

--- a/solution.py
+++ b/solution.py
@@ -84,13 +84,26 @@
     return [lax.axis_index(axis) for axis in AXES]
 
 
+def write_flags(layout, here, flags):
+    for dim in DIMS:
+        tests = ((here[dim] & 1) == 0, here[dim] == 0, here[dim] == layout.sizes[dim] - 1)
+        for number, test in enumerate(tests):
+            row = 3 * dim + number
+            flags[row : row + 1, :] = jnp.full((1, WIDTH), jnp.where(test, 1, 0), jnp.int32)
+
+
+def flagged(layout, flags, dim):
+    rows = [flags[3 * dim + number : 3 * dim + number + 1, :] for number in range(3)]
+    return [jnp.broadcast_to(row, (layout.species, WIDTH)) == 1 for row in rows]
+
+
 def pack(layout, here, dim, load_block, mask_of, outs):
     turns = [(turn, out) for turn, out in zip(layout.turns(), outs) if turn[0] == dim]
     if not turns:
         return
     lane = lanes(layout)
     low = lane < FACE
-    even = (here[dim] & 1) == 0
+    even = flagged(layout, here, dim)[0]
     first = layout.layer(dim, 0)
     last = layout.layer(dim, layout.counts[dim] - 1)
     for pair in range(layout.pairs(dim)):
@@ -111,9 +124,7 @@
 
 
 def received(layout, here, dim, messages):
-    even = (here[dim] & 1) == 0
-    at_start = here[dim] == 0
-    at_end = here[dim] == layout.sizes[dim] - 1
+    even, at_start, at_end = flagged(layout, here, dim)
     zero = jnp.zeros((layout.species, WIDTH), jnp.float32)
     found = []
     for pair in range(layout.pairs(dim)):
@@ -217,8 +228,8 @@
 def first_kernel(layout, load, orient, boundary, *refs):
     turns = len(layout.turns())
     small, refs = refs[:FETCHED], refs[FETCHED:]
-    outs, masks, keeps, staged = refs[:turns], *refs[turns : turns + 3]
-    fetched, (codes, fixed, arrived) = refs[turns + 3 : turns + 3 + FETCHED], refs[-3:]
+    outs, masks, keeps, staged, flags = refs[:turns], *refs[turns : turns + 4]
+    fetched, (codes, fixed, arrived) = refs[turns + 4 : turns + 4 + FETCHED], refs[-3:]
     scalars = [
         pltpu.make_async_copy(source, target, arrived.at[number])
         for number, (source, target) in enumerate(((orient, codes), (boundary, fixed)))
@@ -236,6 +247,7 @@
     for copy in scalars + strips + fetches:
         copy.start()
     here = places()
+    write_flags(layout, here, flags)
     scalars[0].wait()
     tabulate_masks(layout, codes, masks)
     scalars[1].wait()
@@ -244,7 +256,7 @@
         strips[dim].wait()
         pack(
             layout,
-            here,
+            flags,
             dim,
             lambda element, dim: staged[layout.rows(element), columns(dim)],
             table(layout, masks),
@@ -322,7 +334,7 @@
     masks, keeps, scaling, matrix, out, split, summed = refs
     value = reader(layout, *value)
     begun = reader(layout, *begun) if begun else None
-    here = places()
+    here = None
     factor = scales(layout, kind, scaling)
     nodes = out.shape[1]
 
@@ -443,10 +455,9 @@
 
 def early_faces_kernel(layout, kind, order, *refs):
     messages, refs = taken(layout, EARLY, refs, order)
-    masks, scaling, faces, begun, out, *scratch = refs
+    here, masks, scaling, faces, begun, out, *scratch = refs
     count = 2 * len(EARLY)
     splits, sums = scratch[:count], scratch[count:]
-    here = places()
     factor = scales(layout, kind, scaling)
     share = {}
     for place, dim in enumerate(EARLY):
@@ -469,9 +480,8 @@
 
 def late_faces_kernel(layout, kind, order, *refs):
     messages, refs = taken(layout, (LATE,), refs, order)
-    masks, scaling, faces, begun, out, *refs = refs
+    here, masks, scaling, faces, begun, out, *refs = refs
     sent, splits = refs[: len(layout.turns())], refs[len(layout.turns()) :]
-    here = places()
     factor = scales(layout, kind, scaling)
     put_faces(layout, here, LATE, messages, masks, factor, splits)
     edge = layout.edge()
@@ -492,7 +502,7 @@
 
 def last_early_kernel(layout, whole, edges, *refs):
     value = reader(layout, whole, edges)
-    messages, (masks, keeps, ready) = taken(layout, EARLY, refs)
+    messages, (here, masks, keeps, ready) = taken(layout, EARLY, refs)
     for dim in DIMS:
 
         def emit(element, result):
@@ -500,7 +510,7 @@
 
         assemble(
             layout,
-            places(),
+            here,
             dim,
             value,
             None if dim == LATE else messages,
@@ -511,7 +521,7 @@
 
 
 def last_late_kernel(layout, begun, *refs):
-    messages, (masks, out, ready, left) = taken(layout, (LATE,), refs)
+    messages, (here, masks, out, ready, left) = taken(layout, (LATE,), refs)
     low = lanes(layout) < FACE
 
     def copy(source, dim):
@@ -521,7 +531,7 @@
     for each in copies:
         each.start()
     added = {}
-    for number, _, element, face in outside_faces(layout, places(), (LATE,), messages, masks):
+    for number, _, element, face in outside_faces(layout, here, (LATE,), messages, masks):
         part = jnp.where(low, 0.0, face) if number % 2 else jnp.where(low, face, 0.0)
         added[element] = added[element] + part if element in added else part
     for element in layout.elements():
@@ -609,14 +619,14 @@
     small = (scaling, prolong_four.T, coarse_four, prolong_two.T, coarse_two)
     sides = jnp.transpose(boundary, (1, 2, 3, 0))
 
-    *sent, masks, keeps, load, scaling, four, coarse_four, two, coarse_two = pl.pallas_call(
+    *sent, masks, keeps, load, flags, scaling, four, coarse_four, two, coarse_two = pl.pallas_call(
         functools.partial(first_kernel, layout),
         out_shape=message_shapes
         + tables
-        + (whole,)
+        + (whole, jax.ShapeDtypeStruct((3 * len(DIMS), WIDTH), jnp.int32))
         + tuple(jax.ShapeDtypeStruct(each.shape, each.dtype) for each in small),
         in_specs=in_hbm(3 + FETCHED),
-        out_specs=tuple(in_vmem(len(turns) + 3 + FETCHED)),
+        out_specs=tuple(in_vmem(len(turns) + 4 + FETCHED)),
         scratch_shapes=[
             pltpu.SMEM(orient.shape, jnp.int32),
             pltpu.SMEM(sides.shape, jnp.int32),
@@ -674,24 +684,24 @@
         begun = pl.pallas_call(
             functools.partial(early_faces_kernel, layout, kind, order),
             out_shape=whole,
-            in_specs=in_vmem(4 + len(mine)),
+            in_specs=in_vmem(5 + len(mine)),
             out_specs=in_vmem(1)[0],
             scratch_shapes=splits + sums,
             compiler_params=PARAMS,
             cost_estimate=cost(0, 0),
             name=kind + "_faces_early",
-        )(*mine, masks, scaling, matrix[1], begun)
+        )(*mine, flags, masks, scaling, matrix[1], begun)
         mine = [messages[turn] for turn in layout.turns((LATE,), order)]
         changed, *sent = pl.pallas_call(
             functools.partial(late_faces_kernel, layout, kind, order),
             out_shape=(edges,) + message_shapes,
-            in_specs=in_vmem(4 + len(mine)),
+            in_specs=in_vmem(5 + len(mine)),
             out_specs=tuple(in_vmem(1 + len(turns))),
             scratch_shapes=scratch((LATE,))[0],
             compiler_params=PARAMS,
             cost_estimate=cost(0, 0),
             name=kind + "_faces_late",
-        )(*mine, masks, scaling, matrix[1], begun)
+        )(*mine, flags, masks, scaling, matrix[1], begun)
         return (begun, changed), sent
 
     first, sent = stage("smooth", (load,), sent, smoother, (), FIRST_TURNS)
@@ -703,22 +713,22 @@
     begun = pl.pallas_call(
         functools.partial(last_early_kernel, layout),
         out_shape=whole,
-        in_specs=in_vmem(4 + len(early)),
+        in_specs=in_vmem(5 + len(early)),
         out_specs=in_vmem(1)[0],
         compiler_params=PARAMS,
         cost_estimate=cost(0, 8 * rows * nodes),
         name="last_early",
-    )(*total, *early, masks, keeps)
+    )(*total, *early, flags, masks, keeps)
     result = pl.pallas_call(
         functools.partial(last_late_kernel, layout),
         out_shape=whole,
-        in_specs=in_vmem(2 + len(late)),
+        in_specs=in_vmem(3 + len(late)),
         out_specs=in_hbm(1)[0],
         scratch_shapes=[pltpu.VMEM((rows, WIDTH), jnp.float32), pltpu.SemaphoreType.DMA((3,))],
         compiler_params=PARAMS,
         cost_estimate=cost(0, 8 * rows * nodes),
         name="last_late",
-    )(begun, *late, masks)
+    )(begun, *late, flags, masks)
     return result.reshape(load_raw.shape)
 
 

time: 32.4 us -> 32.4 us (level)
  no operation moved by 1% of the time
where the time goes in v3:
time: 32.4 us; the launch traced here: 32.2 us
  starting transfers between devices  18.2 us (56%)
  Pallas kernels  10.2 us (31%)
  waiting for transfers between devices  3.69 us (11%)
    ppermute x20, starting transfers between devices, exchange(): lax.ppermute(given[turn], AXES, partners(layout, *turn))  18.2 us
    ppermute x20, waiting for transfers between devices, exchange(): lax.ppermute(given[turn], AXES, partners(layout, *turn))  3.69 us
    pallas_call x3, Pallas kernels, stage(): pl.pallas_call(functools.partial(local_kernel, layout, kind, (len(value),...  2.96 us
    pallas_call x3, Pallas kernels, stage(): pl.pallas_call(functools.partial(early_faces_kernel, layout, kind, order)...  1.85 us
    pallas_call x1, Pallas kernels, body(): pl.pallas_call(functools.partial(first_kernel, layout), out_shape=message...  1.56 us
    pallas_call x3, Pallas kernels, stage(): pl.pallas_call(functools.partial(late_faces_kernel, layout, kind, order),...  1.4 us
    pallas_call x1, Pallas kernels, body(): pl.pallas_call(functools.partial(last_late_kernel, layout), out_shape=who...  0.9 us
    pallas_call x1, Pallas kernels, body(): pl.pallas_call(smoother_kernel, out_shape=matrix_shapes, in_specs=in_vmem...  0.79 us
  transfers between devices with their start and end apart: 20, of which 6 were waited for; matrix products, arithmetic and copies ran while one was open for 0% of the time, Pallas kernels for 20%

profile of v3, /device:TPU:0, one launch (start us, length us, event | category | flops | bytes accessed | tf_op | source)
XLA Modules:
  0.0 32.2 jit_solution(15008203810305861815)
XLA Ops:
  0.0 1.6 %pack.1 = (f32[128,128]{1,0:T(8,128)S(1)}, f32[128,128]{1,0:T(8,128)S(1)}, f32[128,128]{1,0:T(8,128)S(1)}, f32[128,128]{1,0:T(8,128)S(1)}, f32[64,128]{1,0:T(8,1...) custom-call(f32[512,384]{1,0:T(8,128)} %bitcast.5, ...), custom_call_target="tpu_custom_call" | custom-call | tf_op jit(solution)/shard_map/pack/pallas_call | solution.py:622
  1.6 2.4 %collective-permute-start.1 = (f32[128,128]{1,0:T(8,128)S(1)}, f32[128,128]{1,0:T(8,128)S(1)}, u32[]{:S(2)}, u32[]{:S(2)}) collective-permute-start(f32[128,128]{1,0:T(8,128)S(1)} %get-tuple-element.50), channel_id=1, source_target_pairs={{0,6},{1,7},{2,4},{3,5},{4,2},{5,3},{6,0},{7,1},{8,14},{9,15},{10,... | collective-permute-start | bytes 196616 | tf_op jit(solution)/shard_map/ppermute | solution.py:588
  4.0 0.7 %collective-permute-start.2 = (f32[128,128]{1,0:T(8,128)S(1)}, f32[128,128]{1,0:T(8,128)S(1)}, u32[]{:S(2)}, u32[]{:S(2)}) collective-permute-start(f32[128,128]{1,0:T(8,128)S(1)} %get-tuple-element.51), channel_id=1, source_target_pairs={{0,2},{1,3},{2,0},{3,1},{4,6},{5,7},{6,4},{7,5},{8,16},{9,17},{10,... | collective-permute-start | bytes 196616 | tf_op jit(solution)/shard_map/ppermute | solution.py:588
  4.7 2.5 %collective-permute-start.3 = (f32[128,128]{1,0:T(8,128)S(1)}, f32[128,128]{1,0:T(8,128)S(1)}, u32[]{:S(2)}, u32[]{:S(2)}) collective-permute-start(f32[128,128]{1,0:T(8,128)S(1)} %get-tuple-element.52), channel_id=1, source_target_pairs={{0,8},{1,9},{2,10},{3,11},{4,12},{5,13},{6,14},{7,15},{8,0},{9,1},... | collective-permute-start | bytes 196616 | tf_op jit(solution)/shard_map/ppermute | solution.py:588
  7.2 0.1 collective-permute-start.4
  7.3 1.5 %collective-permute-start = (f32[64,128]{1,0:T(8,128)S(1)}, f32[64,128]{1,0:T(8,128)S(1)}, u32[]{:S(2)}, u32[]{:S(2)}) collective-permute-start(f32[64,128]{1,0:T(8,128)S(1)} %get-tuple-element.41), channel_id=1, source_target_pairs={{0,1},{1,0},{2,3},{3,2},{4,5},{5,4},{6,7},{7,6},{8,9},{9,8},{10,11... | collective-permute-start | bytes 98312 | tf_op jit(solution)/shard_map/ppermute | solution.py:588
  8.9 0.8 %smoother.1 = (bf16[1152,384]{1,0:T(8,128)(2,1)S(1)}, bf16[6,256,384]{2,1,0:T(8,128)(2,1)S(1)}) custom-call(f32[384,384]{1,0:T(8,128)S(1)} %copy-done.1, f32[98,384]{1,0:T(8,128)S(1)} %get-tuple-element.45.four, f32[98,98]{1,0:T(8,128)S(1)} %get-tuple-element.46.coarse_four, f32[26,384]{1,0:T(8,128)S(1)} %get-tuple-element.47.two, ...), custom_call_target="tpu_custom_call" | custom-call | flops 113246208 | bytes 1179648 | tf_op jit(solution)/shard_map/smoother/pallas_call | solution.py:640
  9.7 1.0 %smooth_local.1.refs_8_ = f32[512,384]{1,0:T(8,128)S(1)} custom-call(f32[512,384]{1,0:T(8,128)S(1)} %get-tuple-element.54.refs_0_.refs_2_, s32[16,384]{1,0:T(8,128)S(1)} %get-tuple-element.43.refs_1_.refs_5_.refs_2_.refs_3_.refs_4_, f32[16,384]{1,0:T(8,128)S(1)} %get-tuple-element.55.refs_2_.refs_4_.refs_5_.refs_6_, ...), custom_call_target="tpu_custom_call" | custom-call | flops 196608 | tf_op jit(solution)/shard_map/smooth_local/pallas_call | solution.py:669
  10.6 0.0 collective-permute-done.1.refs_0_
  10.6 0.0 collective-permute-done.2.refs_1_
  10.7 0.0 collective-permute-done.4.refs_3_
  10.7 0.6 %smooth_faces_early.1.refs_5_.refs_0_.refs_2_ = f32[512,384]{1,0:T(8,128)S(1)} custom-call(f32[128,128]{1,0:T(8,128)S(1)} %collective-permute-done.1.refs_0_, f32[128,128]{1,0:T(8,128)S(1)} %collective-permute-done.2.refs_1_, f32[128,128]{1,0:T(8,128)S(1)} %collective-permute-done.3.refs_2_, f32[128,128]{1,0:T(8,128)S(1)} %collective-permute-done.4.refs_3_, ...), custom_call_target="tpu_custom_call" | custom-call | tf_op jit(solution)/shard_map/smooth_faces_early/pallas_call | solution.py:684
  11.3 0.0 copy-start
  11.3 0.0 collective-permute-done.refs_0_
  11.3 0.5 %smooth_faces_late.1 = (f32[256,384]{1,0:T(8,128)S(1)}, f32[128,128]{1,0:T(8,128)S(1)}, f32[128,128]{1,0:T(8,128)S(1)}, f32[128,128]{1,0:T(8,128)S(1)}, f32[128,128]{1,0:T(8,128)S(1)}, /*index=5*/f32[64,128]{1,0:T(8,128)S(1)}) custom-call(f32[64,128]{1,0:T(8,128)S(1)} %collective-permute-done.refs_0_, s32[9,128]{1,0:T(8,128)S(1)} %get-tuple-element.42.refs_4_.refs_1_, ...), custom_call_target="tpu_custom_call" | custom-call | tf_op jit(solution)/shard_map/smooth_faces_late/pallas_call | solution.py:695
  11.8 0.4 %collective-permute-start.6 = (f32[128,128]{1,0:T(8,128)S(1)}, f32[128,128]{1,0:T(8,128)S(1)}, u32[]{:S(2)}, u32[]{:S(2)}) collective-permute-start(f32[128,128]{1,0:T(8,128)S(1)} %get-tuple-element.59), channel_id=1, source_target_pairs={{0,6},{1,7},{2,4},{3,5},{4,2},{5,3},{6,0},{7,1},{8,14},{9,15},{10,... | collective-permute-start | bytes 196616 | tf_op jit(solution)/shard_map/ppermute | solution.py:588
  12.2 0.7 %collective-permute-start.7 = (f32[128,128]{1,0:T(8,128)S(1)}, f32[128,128]{1,0:T(8,128)S(1)}, u32[]{:S(2)}, u32[]{:S(2)}) collective-permute-start(f32[128,128]{1,0:T(8,128)S(1)} %get-tuple-element.60), channel_id=1, source_target_pairs={{0,8},{1,9},{2,10},{3,11},{4,12},{5,13},{6,14},{7,15},{8,0},{9,1},... | collective-permute-start | bytes 196616 | tf_op jit(solution)/shard_map/ppermute | solution.py:588
  12.8 0.3 collective-permute-start.8
  13.1 0.3 collective-permute-start.9
  13.4 1.5 %collective-permute-start.5 = (f32[64,128]{1,0:T(8,128)S(1)}, f32[64,128]{1,0:T(8,128)S(1)}, u32[]{:S(2)}, u32[]{:S(2)}) collective-permute-start(f32[64,128]{1,0:T(8,128)S(1)} %get-tuple-element.57), channel_id=1, source_target_pairs={{0,1},{1,0},{2,3},{3,2},{4,5},{5,4},{6,7},{7,6},{8,9},{9,8},{10,11... | collective-permute-start | bytes 98312 | tf_op jit(solution)/shard_map/ppermute | solution.py:588
  14.9 0.2 operator.1
  15.1 1.0 %operator_local.1.refs_8_ = f32[512,384]{1,0:T(8,128)S(1)} custom-call(f32[512,384]{1,0:T(8,128)S(1)} %smooth_faces_early.1.refs_5_.refs_0_.refs_2_, f32[256,384]{1,0:T(8,128)S(1)} %get-tuple-element.63.refs_1_.refs_3_, f32[512,384]{1,0:T(8,128)S(1)} %get-tuple-element.54.refs_0_.refs_2_, ...), custom_call_target="tpu_custom_call" | custom-call | flops 196608 | tf_op jit(solution)/shard_map/operator_local/pallas_call | solution.py:669
  16.1 0.0 collective-permute-done.6.refs_0_
  16.1 0.4 %collective-permute-done.7.refs_1_ = f32[128,128]{1,0:T(8,128)S(1)} collective-permute-done((f32[128,128]{1,0:T(8,128)S(1)}, f32[128,128]{1,0:T(8,128)S(1)}, u32[]{:S(2)}, u32[]{:S(2)}) %collective-permute-start.7) | collective-permute-done | bytes 65568 | tf_op jit(solution)/shard_map/ppermute | solution.py:588
  16.5 0.0 collective-permute-done.8.refs_2_
  16.5 0.0 collective-permute-done.9.refs_3_
  16.5 0.6 %operator_faces_early.1.refs_5_.refs_0_ = f32[512,384]{1,0:T(8,128)S(1)} custom-call(f32[128,128]{1,0:T(8,128)S(1)} %collective-permute-done.6.refs_0_, f32[128,128]{1,0:T(8,128)S(1)} %collective-permute-done.7.refs_1_, f32[128,128]{1,0:T(8,128)S(1)} %collective-permute-done.8.refs_2_, f32[128,128]{1,0:T(8,128)S(1)} %collective-permute-done.9.refs_3_, ...), custom_call_target="tpu_custom_call" | custom-call | tf_op jit(solution)/shard_map/operator_faces_early/pallas_call | solution.py:684
  17.1 0.2 collective-permute-done.5.refs_0_
  17.3 0.5 %operator_faces_late.1 = (f32[256,384]{1,0:T(8,128)S(1)}, f32[128,128]{1,0:T(8,128)S(1)}, f32[128,128]{1,0:T(8,128)S(1)}, f32[128,128]{1,0:T(8,128)S(1)}, f32[128,128]{1,0:T(8,128)S(1)}, /*index=5*/f32[64,128]{1,0:T(8,128)S(1)}) custom-call(f32[64,128]{1,0:T(8,128)S(1)} %collective-permute-done.5.refs_0_, s32[9,128]{1,0:T(8,128)S(1)} %get-tuple-element.42.refs_4_.refs_1_, ...), custom_call_target="tpu_custom_call" | custom-call | tf_op jit(solution)/shard_map/operator_faces_late/pallas_call | solution.py:695
  17.8 0.7 %collective-permute-start.10 = (f32[128,128]{1,0:T(8,128)S(1)}, f32[128,128]{1,0:T(8,128)S(1)}, u32[]{:S(2)}, u32[]{:S(2)}) collective-permute-start(f32[128,128]{1,0:T(8,128)S(1)} %get-tuple-element.65), channel_id=1, source_target_pairs={{0,6},{1,7},{2,4},{3,5},{4,2},{5,3},{6,0},{7,1},{8,14},{9,15},{10,... | collective-permute-start | bytes 196616 | tf_op jit(solution)/shard_map/ppermute | solution.py:588
  18.5 1.4 %collective-permute-start.11 = (f32[128,128]{1,0:T(8,128)S(1)}, f32[128,128]{1,0:T(8,128)S(1)}, u32[]{:S(2)}, u32[]{:S(2)}) collective-permute-start(f32[128,128]{1,0:T(8,128)S(1)} %get-tuple-element.66), channel_id=1, source_target_pairs={{0,8},{1,9},{2,10},{3,11},{4,12},{5,13},{6,14},{7,15},{8,0},{9,1},... | collective-permute-start | bytes 196616 | tf_op jit(solution)/shard_map/ppermute | solution.py:588
  19.8 1.1 %collective-permute-start.12 = (f32[128,128]{1,0:T(8,128)S(1)}, f32[128,128]{1,0:T(8,128)S(1)}, u32[]{:S(2)}, u32[]{:S(2)}) collective-permute-start(f32[128,128]{1,0:T(8,128)S(1)} %get-tuple-element.67), channel_id=1, source_target_pairs={{0,2},{1,3},{2,0},{3,1},{4,6},{5,7},{6,4},{7,5},{8,16},{9,17},{10,... | collective-permute-start | bytes 196616 | tf_op jit(solution)/shard_map/ppermute | solution.py:588
  20.9 1.6 %collective-permute-start.14 = (f32[64,128]{1,0:T(8,128)S(1)}, f32[64,128]{1,0:T(8,128)S(1)}, u32[]{:S(2)}, u32[]{:S(2)}) collective-permute-start(f32[64,128]{1,0:T(8,128)S(1)} %get-tuple-element.70), channel_id=1, source_target_pairs={{0,1},{1,0},{2,3},{3,2},{4,5},{5,4},{6,7},{7,6},{8,9},{9,8},{10,11... | collective-permute-start | bytes 98312 | tf_op jit(solution)/shard_map/ppermute | solution.py:588
  22.5 1.0 %smooth_more_local.1.refs_8_ = f32[512,384]{1,0:T(8,128)S(1)} custom-call(f32[512,384]{1,0:T(8,128)S(1)} %operator_faces_early.1.refs_5_.refs_0_, f32[256,384]{1,0:T(8,128)S(1)} %get-tuple-element.69.refs_1_, f32[512,384]{1,0:T(8,128)S(1)} %smooth_faces_early.1.refs_5_.refs_0_.refs_2_, f32[256,384]{1,0:T(8,128)S(1)} %get-tuple-element.63.refs_1_.refs_3_, ...), custom_call_target="tpu_custom_call" | custom-call | flops 196608 | tf_op jit(solution)/shard_map/smooth_more_local/pallas_call | solution.py:669
  23.5 0.0 collective-permute-done.10.refs_0_
  23.5 0.6 %smooth_more_faces_early.1.refs_5_.whole = f32[512,384]{1,0:T(8,128)S(1)} custom-call(f32[128,128]{1,0:T(8,128)S(1)} %collective-permute-done.10.refs_0_, f32[128,128]{1,0:T(8,128)S(1)} %collective-permute-done.11.refs_1_, f32[128,128]{1,0:T(8,128)S(1)} %collective-permute-done.12.refs_2_, f32[128,128]{1,0:T(8,128)S(1)} %collective-permute-done.13.refs_3_, ...), custom_call_target="tpu_custom_call" | custom-call | tf_op jit(solution)/shard_map/smooth_more_faces_early/pallas_call | solution.py:684
  24.1 0.7 %collective-permute-done.14.refs_0_ = f32[64,128]{1,0:T(8,128)S(1)} collective-permute-done((f32[64,128]{1,0:T(8,128)S(1)}, f32[64,128]{1,0:T(8,128)S(1)}, u32[]{:S(2)}, u32[]{:S(2)}) %collective-permute-start.14) | collective-permute-done | bytes 32800 | tf_op jit(solution)/shard_map/ppermute | solution.py:588
  24.8 0.5 %smooth_more_faces_late.1 = (f32[256,384]{1,0:T(8,128)S(1)}, f32[128,128]{1,0:T(8,128)S(1)}, f32[128,128]{1,0:T(8,128)S(1)}, f32[128,128]{1,0:T(8,128)S(1)}, f32...) custom-call(f32[64,128]{1,0:T(8,128)S(1)} %collective-permute-done.14.refs_0_, ...), custom_call_target="tpu_custom_call" | custom-call | tf_op jit(solution)/shard_map/smooth_more_faces_late/pallas_call | solution.py:695
  25.3 0.1 collective-permute-start.15
  25.4 1.5 %collective-permute-start.16 = (f32[128,128]{1,0:T(8,128)S(1)}, f32[128,128]{1,0:T(8,128)S(1)}, u32[]{:S(2)}, u32[]{:S(2)}) collective-permute-start(f32[128,128]{1,0:T(8,128)S(1)} %get-tuple-element.73), channel_id=1, source_target_pairs={{0,8},{1,9},{2,10},{3,11},{4,12},{5,13},{6,14},{7,15},{8,0},{9,1},... | collective-permute-start | bytes 196616 | tf_op jit(solution)/shard_map/ppermute | solution.py:588
  26.9 0.3 collective-permute-start.17
  27.2 0.2 collective-permute-start.18
  27.4 0.9 %collective-permute-start.19 = (f32[64,128]{1,0:T(8,128)S(1)}, f32[64,128]{1,0:T(8,128)S(1)}, u32[]{:S(2)}, u32[]{:S(2)}) collective-permute-start(f32[64,128]{1,0:T(8,128)S(1)} %get-tuple-element.76), channel_id=1, source_target_pairs={{0,1},{1,0},{2,3},{3,2},{4,5},{5,4},{6,7},{7,6},{8,9},{9,8},{10,11... | collective-permute-start | bytes 98312 | tf_op jit(solution)/shard_map/ppermute | solution.py:588
  28.3 0.9 %collective-permute-done.15.refs_0_ = f32[128,128]{1,0:T(8,128)S(1)} collective-permute-done((f32[128,128]{1,0:T(8,128)S(1)}, f32[128,128]{1,0:T(8,128)S(1)}, u32[]{:S(2)}, u32[]{:S(2)}) %collective-permute-start.15) | collective-permute-done | bytes 65568 | tf_op jit(solution)/shard_map/ppermute | solution.py:588
  29.3 0.9 %collective-permute-done.16.refs_1_ = f32[128,128]{1,0:T(8,128)S(1)} collective-permute-done((f32[128,128]{1,0:T(8,128)S(1)}, f32[128,128]{1,0:T(8,128)S(1)}, u32[]{:S(2)}, u32[]{:S(2)}) %collective-permute-start.16) | collective-permute-done | bytes 65568 | tf_op jit(solution)/shard_map/ppermute | solution.py:588
  30.2 0.5 %last_early.1.begun = f32[512,384]{1,0:T(8,128)S(1)} custom-call(f32[512,384]{1,0:T(8,128)S(1)} %smooth_more_faces_early.1.refs_5_.whole, f32[256,384]{1,0:T(8,128)S(1)} %get-tuple-element.71.edges, f32[128,128]{1,0:T(8,128)S(1)} %collective-permute-done.15.refs_0_, f32[128,128]{1,0:T(8,128)S(1)} %collective-permute-done.16.refs_1_, ...), custom_call_target="tpu_custom_call" | custom-call | bytes 1572864 | tf_op jit(solution)/shard_map/last_early/pallas_call | solution.py:713
  30.7 0.6 %collective-permute-done.19.refs_0_ = f32[64,128]{1,0:T(8,128)S(1)} collective-permute-done((f32[64,128]{1,0:T(8,128)S(1)}, f32[64,128]{1,0:T(8,128)S(1)}, u32[]{:S(2)}, u32[]{:S(2)}) %collective-permute-start.19) | collective-permute-done | bytes 32800 | tf_op jit(solution)/shard_map/ppermute | solution.py:588
  31.3 0.9 %last_late.1 = f32[512,384]{1,0:T(8,128)} custom-call(f32[512,384]{1,0:T(8,128)S(1)} %last_early.1.begun, f32[64,128]{1,0:T(8,128)S(1)} %collective-permute-done.19.refs_0_, s32[9,128]{1,0:T(8,128)S(1)} %get-tuple-element.42.refs_4_.refs_1_, s32[16,384]{1,0:T(8,128)S(1)} %get-tuple-element.43.refs_1_.refs_5_.refs_2_.refs_3_.refs_4_), custom_call_target="tpu_custom_call" | custom-call | bytes 1572864 | tf_op jit(solution)/shard_map/last_late/pallas_call | solution.py:722
  (10 shorter events, 0.0 us)
Async XLA Ops:
  0.0 8.9 %copy-start.1 = (f32[384,384]{1,0:T(8,128)S(1)}, f32[384,384]{1,0:T(8,128)}, u32[]{:S(2)}) copy-start(f32[384,384]{1,0:T(8,128)} %inverse.1) | copy-start | bytes 1769476
  1.6 9.1 %collective-permute-start.1 = (f32[128,128]{1,0:T(8,128)S(1)}, f32[128,128]{1,0:T(8,128)S(1)}, u32[]{:S(2)}, u32[]{:S(2)}) collective-permute-start(f32[128,128]{1,0:T(8,128)S(1)} %get-tuple-element.50), channel_id=1, source_target_pairs={{0,6},{1,7},{2,4},{3,5},{4,2},{5,3},{6,0},{7,1},{8,14},{9,15},{10,... | collective-permute-start | bytes 196616 | tf_op jit(solution)/shard_map/ppermute | solution.py:588
  4.0 6.6 %collective-permute-start.2 = (f32[128,128]{1,0:T(8,128)S(1)}, f32[128,128]{1,0:T(8,128)S(1)}, u32[]{:S(2)}, u32[]{:S(2)}) collective-permute-start(f32[128,128]{1,0:T(8,128)S(1)} %get-tuple-element.51), channel_id=1, source_target_pairs={{0,2},{1,3},{2,0},{3,1},{4,6},{5,7},{6,4},{7,5},{8,16},{9,17},{10,... | collective-permute-start | bytes 196616 | tf_op jit(solution)/shard_map/ppermute | solution.py:588
  4.7 6.0 %collective-permute-start.3 = (f32[128,128]{1,0:T(8,128)S(1)}, f32[128,128]{1,0:T(8,128)S(1)}, u32[]{:S(2)}, u32[]{:S(2)}) collective-permute-start(f32[128,128]{1,0:T(8,128)S(1)} %get-tuple-element.52), channel_id=1, source_target_pairs={{0,8},{1,9},{2,10},{3,11},{4,12},{5,13},{6,14},{7,15},{8,0},{9,1},... | collective-permute-start | bytes 196616 | tf_op jit(solution)/shard_map/ppermute | solution.py:588
  7.2 3.5 %collective-permute-start.4 = (f32[128,128]{1,0:T(8,128)S(1)}, f32[128,128]{1,0:T(8,128)S(1)}, u32[]{:S(2)}, u32[]{:S(2)}) collective-permute-start(f32[128,128]{1,0:T(8,128)S(1)} %get-tuple-element.53), channel_id=1, source_target_pairs={{0,2},{1,3},{2,0},{3,1},{4,6},{5,7},{6,4},{7,5},{8,10},{9,11},{10,... | collective-permute-start | bytes 196616 | tf_op jit(solution)/shard_map/ppermute | solution.py:588
  7.3 4.0 %collective-permute-start = (f32[64,128]{1,0:T(8,128)S(1)}, f32[64,128]{1,0:T(8,128)S(1)}, u32[]{:S(2)}, u32[]{:S(2)}) collective-permute-start(f32[64,128]{1,0:T(8,128)S(1)} %get-tuple-element.41), channel_id=1, source_target_pairs={{0,1},{1,0},{2,3},{3,2},{4,5},{5,4},{6,7},{7,6},{8,9},{9,8},{10,11... | collective-permute-start | bytes 98312 | tf_op jit(solution)/shard_map/ppermute | solution.py:588
  11.3 3.6 %copy-start = (f32[384,384]{1,0:T(8,128)S(1)}, f32[384,384]{1,0:T(8,128)}, u32[]{:S(2)}) copy-start(f32[384,384]{1,0:T(8,128)} %fine.1) | copy-start | bytes 1769476
  11.8 4.3 %collective-permute-start.6 = (f32[128,128]{1,0:T(8,128)S(1)}, f32[128,128]{1,0:T(8,128)S(1)}, u32[]{:S(2)}, u32[]{:S(2)}) collective-permute-start(f32[128,128]{1,0:T(8,128)S(1)} %get-tuple-element.59), channel_id=1, source_target_pairs={{0,6},{1,7},{2,4},{3,5},{4,2},{5,3},{6,0},{7,1},{8,14},{9,15},{10,... | collective-permute-start | bytes 196616 | tf_op jit(solution)/shard_map/ppermute | solution.py:588
  12.2 4.3 %collective-permute-start.7 = (f32[128,128]{1,0:T(8,128)S(1)}, f32[128,128]{1,0:T(8,128)S(1)}, u32[]{:S(2)}, u32[]{:S(2)}) collective-permute-start(f32[128,128]{1,0:T(8,128)S(1)} %get-tuple-element.60), channel_id=1, source_target_pairs={{0,8},{1,9},{2,10},{3,11},{4,12},{5,13},{6,14},{7,15},{8,0},{9,1},... | collective-permute-start | bytes 196616 | tf_op jit(solution)/shard_map/ppermute | solution.py:588
  12.8 3.6 %collective-permute-start.8 = (f32[128,128]{1,0:T(8,128)S(1)}, f32[128,128]{1,0:T(8,128)S(1)}, u32[]{:S(2)}, u32[]{:S(2)}) collective-permute-start(f32[128,128]{1,0:T(8,128)S(1)} %get-tuple-element.61), channel_id=1, source_target_pairs={{0,2},{1,3},{2,0},{3,1},{4,6},{5,7},{6,4},{7,5},{8,16},{9,17},{10,... | collective-permute-start | bytes 196616 | tf_op jit(solution)/shard_map/ppermute | solution.py:588
  13.1 3.4 %collective-permute-start.9 = (f32[128,128]{1,0:T(8,128)S(1)}, f32[128,128]{1,0:T(8,128)S(1)}, u32[]{:S(2)}, u32[]{:S(2)}) collective-permute-start(f32[128,128]{1,0:T(8,128)S(1)} %get-tuple-element.62), channel_id=1, source_target_pairs={{0,2},{1,3},{2,0},{3,1},{4,6},{5,7},{6,4},{7,5},{8,10},{9,11},{10,... | collective-permute-start | bytes 196616 | tf_op jit(solution)/shard_map/ppermute | solution.py:588
  13.4 3.9 %collective-permute-start.5 = (f32[64,128]{1,0:T(8,128)S(1)}, f32[64,128]{1,0:T(8,128)S(1)}, u32[]{:S(2)}, u32[]{:S(2)}) collective-permute-start(f32[64,128]{1,0:T(8,128)S(1)} %get-tuple-element.57), channel_id=1, source_target_pairs={{0,1},{1,0},{2,3},{3,2},{4,5},{5,4},{6,7},{7,6},{8,9},{9,8},{10,11... | collective-permute-start | bytes 98312 | tf_op jit(solution)/shard_map/ppermute | solution.py:588
  17.8 5.7 %collective-permute-start.10 = (f32[128,128]{1,0:T(8,128)S(1)}, f32[128,128]{1,0:T(8,128)S(1)}, u32[]{:S(2)}, u32[]{:S(2)}) collective-permute-start(f32[128,128]{1,0:T(8,128)S(1)} %get-tuple-element.65), channel_id=1, source_target_pairs={{0,6},{1,7},{2,4},{3,5},{4,2},{5,3},{6,0},{7,1},{8,14},{9,15},{10,... | collective-permute-start | bytes 196616 | tf_op jit(solution)/shard_map/ppermute | solution.py:588
  18.5 5.1 %collective-permute-start.11 = (f32[128,128]{1,0:T(8,128)S(1)}, f32[128,128]{1,0:T(8,128)S(1)}, u32[]{:S(2)}, u32[]{:S(2)}) collective-permute-start(f32[128,128]{1,0:T(8,128)S(1)} %get-tuple-element.66), channel_id=1, source_target_pairs={{0,8},{1,9},{2,10},{3,11},{4,12},{5,13},{6,14},{7,15},{8,0},{9,1},... | collective-permute-start | bytes 196616 | tf_op jit(solution)/shard_map/ppermute | solution.py:588
  19.8 3.7 %collective-permute-start.12 = (f32[128,128]{1,0:T(8,128)S(1)}, f32[128,128]{1,0:T(8,128)S(1)}, u32[]{:S(2)}, u32[]{:S(2)}) collective-permute-start(f32[128,128]{1,0:T(8,128)S(1)} %get-tuple-element.67), channel_id=1, source_target_pairs={{0,2},{1,3},{2,0},{3,1},{4,6},{5,7},{6,4},{7,5},{8,16},{9,17},{10,... | collective-permute-start | bytes 196616 | tf_op jit(solution)/shard_map/ppermute | solution.py:588
  20.9 2.6 %collective-permute-start.13 = (f32[128,128]{1,0:T(8,128)S(1)}, f32[128,128]{1,0:T(8,128)S(1)}, u32[]{:S(2)}, u32[]{:S(2)}) collective-permute-start(f32[128,128]{1,0:T(8,128)S(1)} %get-tuple-element.68), channel_id=1, source_target_pairs={{0,2},{1,3},{2,0},{3,1},{4,6},{5,7},{6,4},{7,5},{8,10},{9,11},{10,... | collective-permute-start | bytes 196616 | tf_op jit(solution)/shard_map/ppermute | solution.py:588
  20.9 3.9 %collective-permute-start.14 = (f32[64,128]{1,0:T(8,128)S(1)}, f32[64,128]{1,0:T(8,128)S(1)}, u32[]{:S(2)}, u32[]{:S(2)}) collective-permute-start(f32[64,128]{1,0:T(8,128)S(1)} %get-tuple-element.70), channel_id=1, source_target_pairs={{0,1},{1,0},{2,3},{3,2},{4,5},{5,4},{6,7},{7,6},{8,9},{9,8},{10,11... | collective-permute-start | bytes 98312 | tf_op jit(solution)/shard_map/ppermute | solution.py:588
  25.3 4.0 %collective-permute-start.15 = (f32[128,128]{1,0:T(8,128)S(1)}, f32[128,128]{1,0:T(8,128)S(1)}, u32[]{:S(2)}, u32[]{:S(2)}) collective-permute-start(f32[128,128]{1,0:T(8,128)S(1)} %get-tuple-element.72), channel_id=1, source_target_pairs={{0,6},{1,7},{2,4},{3,5},{4,2},{5,3},{6,0},{7,1},{8,14},{9,15},{10,... | collective-permute-start | bytes 196616 | tf_op jit(solution)/shard_map/ppermute | solution.py:588
  25.4 4.8 %collective-permute-start.16 = (f32[128,128]{1,0:T(8,128)S(1)}, f32[128,128]{1,0:T(8,128)S(1)}, u32[]{:S(2)}, u32[]{:S(2)}) collective-permute-start(f32[128,128]{1,0:T(8,128)S(1)} %get-tuple-element.73), channel_id=1, source_target_pairs={{0,8},{1,9},{2,10},{3,11},{4,12},{5,13},{6,14},{7,15},{8,0},{9,1},... | collective-permute-start | bytes 196616 | tf_op jit(solution)/shard_map/ppermute | solution.py:588
  26.9 3.3 %collective-permute-start.17 = (f32[128,128]{1,0:T(8,128)S(1)}, f32[128,128]{1,0:T(8,128)S(1)}, u32[]{:S(2)}, u32[]{:S(2)}) collective-permute-start(f32[128,128]{1,0:T(8,128)S(1)} %get-tuple-element.74), channel_id=1, source_target_pairs={{0,2},{1,3},{2,0},{3,1},{4,6},{5,7},{6,4},{7,5},{8,16},{9,17},{10,... | collective-permute-start | bytes 196616 | tf_op jit(solution)/shard_map/ppermute | solution.py:588
  27.2 3.0 %collective-permute-start.18 = (f32[128,128]{1,0:T(8,128)S(1)}, f32[128,128]{1,0:T(8,128)S(1)}, u32[]{:S(2)}, u32[]{:S(2)}) collective-permute-start(f32[128,128]{1,0:T(8,128)S(1)} %get-tuple-element.75), channel_id=1, source_target_pairs={{0,2},{1,3},{2,0},{3,1},{4,6},{5,7},{6,4},{7,5},{8,10},{9,11},{10,... | collective-permute-start | bytes 196616 | tf_op jit(solution)/shard_map/ppermute | solution.py:588
  27.4 3.9 %collective-permute-start.19 = (f32[64,128]{1,0:T(8,128)S(1)}, f32[64,128]{1,0:T(8,128)S(1)}, u32[]{:S(2)}, u32[]{:S(2)}) collective-permute-start(f32[64,128]{1,0:T(8,128)S(1)} %get-tuple-element.76), channel_id=1, source_target_pairs={{0,1},{1,0},{2,3},{3,2},{4,5},{5,4},{6,7},{7,6},{8,9},{9,8},{10,11... | collective-permute-start | bytes 98312 | tf_op jit(solution)/shard_map/ppermute | solution.py:588

commit v4 on v0

--- a/solution.py
+++ b/solution.py
@@ -298,6 +298,61 @@
 def taken(layout, dims, refs, order=TURNS):
     turns = layout.turns(dims, order)
     return dict(zip(turns, refs)), refs[len(turns) :]
+
+
+def combined(kind, begun, result):
+    if begun is None:
+        return result
+    return begun - result if kind == "operator" else begun + result
+
+
+def reader(layout, whole, edges=None):
+    edge = [] if edges is None else layout.edge()
+
+    def block(element, dim):
+        if element in edge:
+            return edges[layout.pair_rows(edge.index(element)), columns(dim)]
+        return whole[layout.rows(element), columns(dim)]
+
+    return block
+
+
+def local_kernel(layout, kind, given, *refs):
+    value, begun, refs = refs[: given[0]], refs[given[0] : sum(given)], refs[sum(given) :]
+    masks, keeps, scaling, matrix, out, split, summed = refs
+    value = reader(layout, *value)
+    begun = reader(layout, *begun) if begun else None
+    here = places()
+    factor = scales(layout, kind, scaling)
+    nodes = out.shape[1]
+
+    def assembled(dim, slab):
+        def emit(element, result):
+            high, rest = halves(result * factor(element, dim))
+            for part, piece in enumerate((high, high, rest)):
+                start = part * nodes + dim * WIDTH
+                split[layout.rows(element), start : start + WIDTH] = piece
+
+        assemble(
+            layout,
+            here,
+            dim,
+            value,
+            None,
+            table(layout, masks),
+            table(layout, keeps),
+            emit,
+            slab,
+        )
+
+    for dim in DIMS:
+        assembled(dim, None)
+    summed[...] = dot(split[...], matrix[...])
+    for element in layout.elements():
+        for dim in DIMS:
+            at = (layout.rows(element), columns(dim))
+            result = summed[at] * factor(element, dim)
+            out[at] = combined(kind, begun and begun(element, dim), result)
 
 
 def combined(kind, begun, result):

time: 32.4 us -> 32.4 us (level)
  no operation moved by 1% of the time
where the time goes in v4:
time: 32.4 us; the launch traced here: 32.3 us
  starting transfers between devices  18.1 us (56%)
  Pallas kernels  10.2 us (31%)
  waiting for transfers between devices  3.71 us (11%)
    ppermute x20, starting transfers between devices, exchange(): lax.ppermute(given[turn], AXES, partners(layout, *turn))  18.1 us
    ppermute x20, waiting for transfers between devices, exchange(): lax.ppermute(given[turn], AXES, partners(layout, *turn))  3.71 us
    pallas_call x3, Pallas kernels, stage(): pl.pallas_call(functools.partial(local_kernel, layout, kind, (len(value),...  2.97 us
    pallas_call x3, Pallas kernels, stage(): pl.pallas_call(functools.partial(early_faces_kernel, layout, kind, order)...  1.9 us
    pallas_call x1, Pallas kernels, body(): pl.pallas_call(functools.partial(first_kernel, layout), out_shape=message...  1.56 us
    pallas_call x3, Pallas kernels, stage(): pl.pallas_call(functools.partial(late_faces_kernel, layout, kind, order),...  1.41 us
    pallas_call x1, Pallas kernels, body(): pl.pallas_call(functools.partial(last_late_kernel, layout), out_shape=who...  0.91 us
    pallas_call x1, Pallas kernels, body(): pl.pallas_call(smoother_kernel, out_shape=matrix_shapes, in_specs=in_vmem...  0.79 us
  transfers between devices with their start and end apart: 20, of which 6 were waited for; matrix products, arithmetic and copies ran while one was open for 0% of the time, Pallas kernels for 20%

profile of v4, /device:TPU:0, one launch (start us, length us, event | category | flops | bytes accessed | tf_op | source)
XLA Modules:
  0.0 32.3 jit_solution(8720040626391831122)
XLA Ops:
  0.0 1.6 %pack.1 = (f32[128,128]{1,0:T(8,128)S(1)}, f32[128,128]{1,0:T(8,128)S(1)}, f32[128,128]{1,0:T(8,128)S(1)}, f32[128,128]{1,0:T(8,128)S(1)}, f32[64,128]{1,0:T(8,1...) custom-call(f32[512,384]{1,0:T(8,128)} %bitcast.5, ...), custom_call_target="tpu_custom_call" | custom-call | tf_op jit(solution)/shard_map/pack/pallas_call | solution.py:667
  1.6 2.4 %collective-permute-start.1 = (f32[128,128]{1,0:T(8,128)S(1)}, f32[128,128]{1,0:T(8,128)S(1)}, u32[]{:S(2)}, u32[]{:S(2)}) collective-permute-start(f32[128,128]{1,0:T(8,128)S(1)} %get-tuple-element.48), channel_id=1, source_target_pairs={{0,6},{1,7},{2,4},{3,5},{4,2},{5,3},{6,0},{7,1},{8,14},{9,15},{10,... | collective-permute-start | bytes 196616 | tf_op jit(solution)/shard_map/ppermute | solution.py:633
  4.0 0.7 %collective-permute-start.2 = (f32[128,128]{1,0:T(8,128)S(1)}, f32[128,128]{1,0:T(8,128)S(1)}, u32[]{:S(2)}, u32[]{:S(2)}) collective-permute-start(f32[128,128]{1,0:T(8,128)S(1)} %get-tuple-element.49), channel_id=1, source_target_pairs={{0,2},{1,3},{2,0},{3,1},{4,6},{5,7},{6,4},{7,5},{8,16},{9,17},{10,... | collective-permute-start | bytes 196616 | tf_op jit(solution)/shard_map/ppermute | solution.py:633
  4.7 2.5 %collective-permute-start.3 = (f32[128,128]{1,0:T(8,128)S(1)}, f32[128,128]{1,0:T(8,128)S(1)}, u32[]{:S(2)}, u32[]{:S(2)}) collective-permute-start(f32[128,128]{1,0:T(8,128)S(1)} %get-tuple-element.50), channel_id=1, source_target_pairs={{0,8},{1,9},{2,10},{3,11},{4,12},{5,13},{6,14},{7,15},{8,0},{9,1},... | collective-permute-start | bytes 196616 | tf_op jit(solution)/shard_map/ppermute | solution.py:633
  7.2 0.1 collective-permute-start.4
  7.3 1.5 %collective-permute-start = (f32[64,128]{1,0:T(8,128)S(1)}, f32[64,128]{1,0:T(8,128)S(1)}, u32[]{:S(2)}, u32[]{:S(2)}) collective-permute-start(f32[64,128]{1,0:T(8,128)S(1)} %get-tuple-element.40), channel_id=1, source_target_pairs={{0,1},{1,0},{2,3},{3,2},{4,5},{5,4},{6,7},{7,6},{8,9},{9,8},{10,11... | collective-permute-start | bytes 98312 | tf_op jit(solution)/shard_map/ppermute | solution.py:633
  8.9 0.8 %smoother.1 = (bf16[1152,384]{1,0:T(8,128)(2,1)S(1)}, bf16[6,256,384]{2,1,0:T(8,128)(2,1)S(1)}) custom-call(f32[384,384]{1,0:T(8,128)S(1)} %copy-done.1, f32[98,384]{1,0:T(8,128)S(1)} %get-tuple-element.43.four, f32[98,98]{1,0:T(8,128)S(1)} %get-tuple-element.44.coarse_four, f32[26,384]{1,0:T(8,128)S(1)} %get-tuple-element.45.two, ...), custom_call_target="tpu_custom_call" | custom-call | flops 113246208 | bytes 1179648 | tf_op jit(solution)/shard_map/smoother/pallas_call | solution.py:685
  9.7 1.0 %smooth_local.1.refs_7_ = f32[512,384]{1,0:T(8,128)S(1)} custom-call(f32[512,384]{1,0:T(8,128)S(1)} %get-tuple-element.52.refs_0_.refs_2_, s32[16,384]{1,0:T(8,128)S(1)} %get-tuple-element.41.refs_1_.refs_4_.refs_3_, f32[16,384]{1,0:T(8,128)S(1)} %get-tuple-element.53.refs_2_.refs_4_.refs_5_, ...), custom_call_target="tpu_custom_call" | custom-call | flops 196608 | tf_op jit(solution)/shard_map/smooth_local/pallas_call | solution.py:714
  10.6 0.0 collective-permute-done.1.refs_0_
  10.7 0.0 collective-permute-done.2.refs_1_
  10.7 0.0 collective-permute-done.3.refs_2_
  10.7 0.6 %smooth_faces_early.1.refs_4_.refs_0_.refs_2_ = f32[512,384]{1,0:T(8,128)S(1)} custom-call(f32[128,128]{1,0:T(8,128)S(1)} %collective-permute-done.1.refs_0_, f32[128,128]{1,0:T(8,128)S(1)} %collective-permute-done.2.refs_1_, f32[128,128]{1,0:T(8,128)S(1)} %collective-permute-done.3.refs_2_, f32[128,128]{1,0:T(8,128)S(1)} %collective-permute-done.4.refs_3_, ...), custom_call_target="tpu_custom_call" | custom-call | tf_op jit(solution)/shard_map/smooth_faces_early/pallas_call | solution.py:729
  11.3 0.0 copy-start
  11.3 0.0 collective-permute-done.refs_0_
  11.3 0.5 %smooth_faces_late.1 = (f32[256,384]{1,0:T(8,128)S(1)}, f32[128,128]{1,0:T(8,128)S(1)}, f32[128,128]{1,0:T(8,128)S(1)}, f32[128,128]{1,0:T(8,128)S(1)}, f32[128,128]{1,0:T(8,128)S(1)}, /*index=5*/f32[64,128]{1,0:T(8,128)S(1)}) custom-call(f32[64,128]{1,0:T(8,128)S(1)} %collective-permute-done.refs_0_, ...), custom_call_target="tpu_custom_call" | custom-call | tf_op jit(solution)/shard_map/smooth_faces_late/pallas_call | solution.py:740
  11.8 0.4 %collective-permute-start.6 = (f32[128,128]{1,0:T(8,128)S(1)}, f32[128,128]{1,0:T(8,128)S(1)}, u32[]{:S(2)}, u32[]{:S(2)}) collective-permute-start(f32[128,128]{1,0:T(8,128)S(1)} %get-tuple-element.57), channel_id=1, source_target_pairs={{0,6},{1,7},{2,4},{3,5},{4,2},{5,3},{6,0},{7,1},{8,14},{9,15},{10,... | collective-permute-start | bytes 196616 | tf_op jit(solution)/shard_map/ppermute | solution.py:633
  12.2 0.7 %collective-permute-start.7 = (f32[128,128]{1,0:T(8,128)S(1)}, f32[128,128]{1,0:T(8,128)S(1)}, u32[]{:S(2)}, u32[]{:S(2)}) collective-permute-start(f32[128,128]{1,0:T(8,128)S(1)} %get-tuple-element.58), channel_id=1, source_target_pairs={{0,8},{1,9},{2,10},{3,11},{4,12},{5,13},{6,14},{7,15},{8,0},{9,1},... | collective-permute-start | bytes 196616 | tf_op jit(solution)/shard_map/ppermute | solution.py:633
  12.9 0.3 collective-permute-start.8
  13.1 0.3 collective-permute-start.9
  13.4 1.5 %collective-permute-start.5 = (f32[64,128]{1,0:T(8,128)S(1)}, f32[64,128]{1,0:T(8,128)S(1)}, u32[]{:S(2)}, u32[]{:S(2)}) collective-permute-start(f32[64,128]{1,0:T(8,128)S(1)} %get-tuple-element.55), channel_id=1, source_target_pairs={{0,1},{1,0},{2,3},{3,2},{4,5},{5,4},{6,7},{7,6},{8,9},{9,8},{10,11... | collective-permute-start | bytes 98312 | tf_op jit(solution)/shard_map/ppermute | solution.py:633
  14.9 0.2 operator.1
  15.1 1.0 %operator_local.1.refs_7_ = f32[512,384]{1,0:T(8,128)S(1)} custom-call(f32[512,384]{1,0:T(8,128)S(1)} %smooth_faces_early.1.refs_4_.refs_0_.refs_2_, f32[256,384]{1,0:T(8,128)S(1)} %get-tuple-element.61.refs_1_.refs_3_, f32[512,384]{1,0:T(8,128)S(1)} %get-tuple-element.52.refs_0_.refs_2_, s32[16,384]{1,0:T(8,128)S(1)} %get-tuple-element.41.refs_1_.refs_4_.refs_3_, ...), custom_call_target="tpu_custom_call" | custom-call | flops 196608 | tf_op jit(solution)/shard_map/operator_local/pallas_call | solution.py:714
  16.1 0.0 collective-permute-done.6.refs_0_
  16.1 0.4 %collective-permute-done.7.refs_1_ = f32[128,128]{1,0:T(8,128)S(1)} collective-permute-done((f32[128,128]{1,0:T(8,128)S(1)}, f32[128,128]{1,0:T(8,128)S(1)}, u32[]{:S(2)}, u32[]{:S(2)}) %collective-permute-start.7) | collective-permute-done | bytes 65568 | tf_op jit(solution)/shard_map/ppermute | solution.py:633
  16.5 0.6 %operator_faces_early.1.refs_4_.refs_0_ = f32[512,384]{1,0:T(8,128)S(1)} custom-call(f32[128,128]{1,0:T(8,128)S(1)} %collective-permute-done.6.refs_0_, f32[128,128]{1,0:T(8,128)S(1)} %collective-permute-done.7.refs_1_, f32[128,128]{1,0:T(8,128)S(1)} %collective-permute-done.8.refs_2_, f32[128,128]{1,0:T(8,128)S(1)} %collective-permute-done.9.refs_3_, ...), custom_call_target="tpu_custom_call" | custom-call | tf_op jit(solution)/shard_map/operator_faces_early/pallas_call | solution.py:729
  17.1 0.2 collective-permute-done.5.refs_0_
  17.3 0.5 %operator_faces_late.1 = (f32[256,384]{1,0:T(8,128)S(1)}, f32[128,128]{1,0:T(8,128)S(1)}, f32[128,128]{1,0:T(8,128)S(1)}, f32[128,128]{1,0:T(8,128)S(1)}, f32[128,128]{1,0:T(8,128)S(1)}, /*index=5*/f32[64,128]{1,0:T(8,128)S(1)}) custom-call(f32[64,128]{1,0:T(8,128)S(1)} %collective-permute-done.5.refs_0_, ...), custom_call_target="tpu_custom_call" | custom-call | tf_op jit(solution)/shard_map/operator_faces_late/pallas_call | solution.py:740
  17.8 0.7 %collective-permute-start.10 = (f32[128,128]{1,0:T(8,128)S(1)}, f32[128,128]{1,0:T(8,128)S(1)}, u32[]{:S(2)}, u32[]{:S(2)}) collective-permute-start(f32[128,128]{1,0:T(8,128)S(1)} %get-tuple-element.63), channel_id=1, source_target_pairs={{0,6},{1,7},{2,4},{3,5},{4,2},{5,3},{6,0},{7,1},{8,14},{9,15},{10,... | collective-permute-start | bytes 196616 | tf_op jit(solution)/shard_map/ppermute | solution.py:633
  18.5 1.4 %collective-permute-start.11 = (f32[128,128]{1,0:T(8,128)S(1)}, f32[128,128]{1,0:T(8,128)S(1)}, u32[]{:S(2)}, u32[]{:S(2)}) collective-permute-start(f32[128,128]{1,0:T(8,128)S(1)} %get-tuple-element.64), channel_id=1, source_target_pairs={{0,8},{1,9},{2,10},{3,11},{4,12},{5,13},{6,14},{7,15},{8,0},{9,1},... | collective-permute-start | bytes 196616 | tf_op jit(solution)/shard_map/ppermute | solution.py:633
  19.9 1.1 %collective-permute-start.12 = (f32[128,128]{1,0:T(8,128)S(1)}, f32[128,128]{1,0:T(8,128)S(1)}, u32[]{:S(2)}, u32[]{:S(2)}) collective-permute-start(f32[128,128]{1,0:T(8,128)S(1)} %get-tuple-element.65), channel_id=1, source_target_pairs={{0,2},{1,3},{2,0},{3,1},{4,6},{5,7},{6,4},{7,5},{8,16},{9,17},{10,... | collective-permute-start | bytes 196616 | tf_op jit(solution)/shard_map/ppermute | solution.py:633
  20.9 0.0 collective-permute-start.13
  20.9 1.6 %collective-permute-start.14 = (f32[64,128]{1,0:T(8,128)S(1)}, f32[64,128]{1,0:T(8,128)S(1)}, u32[]{:S(2)}, u32[]{:S(2)}) collective-permute-start(f32[64,128]{1,0:T(8,128)S(1)} %get-tuple-element.68), channel_id=1, source_target_pairs={{0,1},{1,0},{2,3},{3,2},{4,5},{5,4},{6,7},{7,6},{8,9},{9,8},{10,11... | collective-permute-start | bytes 98312 | tf_op jit(solution)/shard_map/ppermute | solution.py:633
  22.5 1.0 %smooth_more_local.1.refs_7_ = f32[512,384]{1,0:T(8,128)S(1)} custom-call(f32[512,384]{1,0:T(8,128)S(1)} %operator_faces_early.1.refs_4_.refs_0_, f32[256,384]{1,0:T(8,128)S(1)} %get-tuple-element.67.refs_1_, f32[512,384]{1,0:T(8,128)S(1)} %smooth_faces_early.1.refs_4_.refs_0_.refs_2_, f32[256,384]{1,0:T(8,128)S(1)} %get-tuple-element.61.refs_1_.refs_3_, ...), custom_call_target="tpu_custom_call" | custom-call | flops 196608 | tf_op jit(solution)/shard_map/smooth_more_local/pallas_call | solution.py:714
  23.5 0.0 collective-permute-done.11.refs_1_
  23.5 0.0 collective-permute-done.12.refs_2_
  23.5 0.6 %smooth_more_faces_early.1.refs_4_.whole = f32[512,384]{1,0:T(8,128)S(1)} custom-call(f32[128,128]{1,0:T(8,128)S(1)} %collective-permute-done.10.refs_0_, f32[128,128]{1,0:T(8,128)S(1)} %collective-permute-done.11.refs_1_, f32[128,128]{1,0:T(8,128)S(1)} %collective-permute-done.12.refs_2_, f32[128,128]{1,0:T(8,128)S(1)} %collective-permute-done.13.refs_3_, ...), custom_call_target="tpu_custom_call" | custom-call | tf_op jit(solution)/shard_map/smooth_more_faces_early/pallas_call | solution.py:729
  24.2 0.6 %collective-permute-done.14.refs_0_ = f32[64,128]{1,0:T(8,128)S(1)} collective-permute-done((f32[64,128]{1,0:T(8,128)S(1)}, f32[64,128]{1,0:T(8,128)S(1)}, u32[]{:S(2)}, u32[]{:S(2)}) %collective-permute-start.14) | collective-permute-done | bytes 32800 | tf_op jit(solution)/shard_map/ppermute | solution.py:633
  24.8 0.5 %smooth_more_faces_late.1 = (f32[256,384]{1,0:T(8,128)S(1)}, f32[128,128]{1,0:T(8,128)S(1)}, f32[128,128]{1,0:T(8,128)S(1)}, f32[128,128]{1,0:T(8,128)S(1)}, f32...) custom-call(f32[64,128]{1,0:T(8,128)S(1)} %collective-permute-done.14.refs_0_, ...), custom_call_target="tpu_custom_call" | custom-call | tf_op jit(solution)/shard_map/smooth_more_faces_late/pallas_call | solution.py:740
  25.3 0.1 collective-permute-start.15
  25.4 1.5 %collective-permute-start.16 = (f32[128,128]{1,0:T(8,128)S(1)}, f32[128,128]{1,0:T(8,128)S(1)}, u32[]{:S(2)}, u32[]{:S(2)}) collective-permute-start(f32[128,128]{1,0:T(8,128)S(1)} %get-tuple-element.71), channel_id=1, source_target_pairs={{0,8},{1,9},{2,10},{3,11},{4,12},{5,13},{6,14},{7,15},{8,0},{9,1},... | collective-permute-start | bytes 196616 | tf_op jit(solution)/shard_map/ppermute | solution.py:633
  26.9 0.3 collective-permute-start.17
  27.2 0.2 collective-permute-start.18
  27.4 0.9 %collective-permute-start.19 = (f32[64,128]{1,0:T(8,128)S(1)}, f32[64,128]{1,0:T(8,128)S(1)}, u32[]{:S(2)}, u32[]{:S(2)}) collective-permute-start(f32[64,128]{1,0:T(8,128)S(1)} %get-tuple-element.74), channel_id=1, source_target_pairs={{0,1},{1,0},{2,3},{3,2},{4,5},{5,4},{6,7},{7,6},{8,9},{9,8},{10,11... | collective-permute-start | bytes 98312 | tf_op jit(solution)/shard_map/ppermute | solution.py:633
  28.4 1.0 %collective-permute-done.15.refs_0_ = f32[128,128]{1,0:T(8,128)S(1)} collective-permute-done((f32[128,128]{1,0:T(8,128)S(1)}, f32[128,128]{1,0:T(8,128)S(1)}, u32[]{:S(2)}, u32[]{:S(2)}) %collective-permute-start.15) | collective-permute-done | bytes 65568 | tf_op jit(solution)/shard_map/ppermute | solution.py:633
  29.3 0.9 %collective-permute-done.16.refs_1_ = f32[128,128]{1,0:T(8,128)S(1)} collective-permute-done((f32[128,128]{1,0:T(8,128)S(1)}, f32[128,128]{1,0:T(8,128)S(1)}, u32[]{:S(2)}, u32[]{:S(2)}) %collective-permute-start.16) | collective-permute-done | bytes 65568 | tf_op jit(solution)/shard_map/ppermute | solution.py:633
  30.3 0.5 %last_early.1.begun = f32[512,384]{1,0:T(8,128)S(1)} custom-call(f32[512,384]{1,0:T(8,128)S(1)} %smooth_more_faces_early.1.refs_4_.whole, f32[256,384]{1,0:T(8,128)S(1)} %get-tuple-element.69.edges, f32[128,128]{1,0:T(8,128)S(1)} %collective-permute-done.15.refs_0_, f32[128,128]{1,0:T(8,128)S(1)} %collective-permute-done.16.refs_1_, ...), custom_call_target="tpu_custom_call" | custom-call | bytes 1572864 | tf_op jit(solution)/shard_map/last_early/pallas_call | solution.py:758
  30.8 0.6 %collective-permute-done.19.refs_0_ = f32[64,128]{1,0:T(8,128)S(1)} collective-permute-done((f32[64,128]{1,0:T(8,128)S(1)}, f32[64,128]{1,0:T(8,128)S(1)}, u32[]{:S(2)}, u32[]{:S(2)}) %collective-permute-start.19) | collective-permute-done | bytes 32800 | tf_op jit(solution)/shard_map/ppermute | solution.py:633
  31.3 0.9 %last_late.1 = f32[512,384]{1,0:T(8,128)} custom-call(f32[512,384]{1,0:T(8,128)S(1)} %last_early.1.begun, f32[64,128]{1,0:T(8,128)S(1)} %collective-permute-done.19.refs_0_, s32[16,384]{1,0:T(8,128)S(1)} %get-tuple-element.41.refs_1_.refs_4_.refs_3_), custom_call_target="tpu_custom_call" | custom-call | bytes 1572864 | tf_op jit(solution)/shard_map/last_late/pallas_call | solution.py:767
  (10 shorter events, 0.0 us)
Async XLA Ops:
  0.0 8.9 %copy-start.1 = (f32[384,384]{1,0:T(8,128)S(1)}, f32[384,384]{1,0:T(8,128)}, u32[]{:S(2)}) copy-start(f32[384,384]{1,0:T(8,128)} %inverse.1) | copy-start | bytes 1769476
  1.6 9.1 %collective-permute-start.1 = (f32[128,128]{1,0:T(8,128)S(1)}, f32[128,128]{1,0:T(8,128)S(1)}, u32[]{:S(2)}, u32[]{:S(2)}) collective-permute-start(f32[128,128]{1,0:T(8,128)S(1)} %get-tuple-element.48), channel_id=1, source_target_pairs={{0,6},{1,7},{2,4},{3,5},{4,2},{5,3},{6,0},{7,1},{8,14},{9,15},{10,... | collective-permute-start | bytes 196616 | tf_op jit(solution)/shard_map/ppermute | solution.py:633
  4.0 6.6 %collective-permute-start.2 = (f32[128,128]{1,0:T(8,128)S(1)}, f32[128,128]{1,0:T(8,128)S(1)}, u32[]{:S(2)}, u32[]{:S(2)}) collective-permute-start(f32[128,128]{1,0:T(8,128)S(1)} %get-tuple-element.49), channel_id=1, source_target_pairs={{0,2},{1,3},{2,0},{3,1},{4,6},{5,7},{6,4},{7,5},{8,16},{9,17},{10,... | collective-permute-start | bytes 196616 | tf_op jit(solution)/shard_map/ppermute | solution.py:633
  4.7 6.0 %collective-permute-start.3 = (f32[128,128]{1,0:T(8,128)S(1)}, f32[128,128]{1,0:T(8,128)S(1)}, u32[]{:S(2)}, u32[]{:S(2)}) collective-permute-start(f32[128,128]{1,0:T(8,128)S(1)} %get-tuple-element.50), channel_id=1, source_target_pairs={{0,8},{1,9},{2,10},{3,11},{4,12},{5,13},{6,14},{7,15},{8,0},{9,1},... | collective-permute-start | bytes 196616 | tf_op jit(solution)/shard_map/ppermute | solution.py:633
  7.2 3.5 %collective-permute-start.4 = (f32[128,128]{1,0:T(8,128)S(1)}, f32[128,128]{1,0:T(8,128)S(1)}, u32[]{:S(2)}, u32[]{:S(2)}) collective-permute-start(f32[128,128]{1,0:T(8,128)S(1)} %get-tuple-element.51), channel_id=1, source_target_pairs={{0,2},{1,3},{2,0},{3,1},{4,6},{5,7},{6,4},{7,5},{8,10},{9,11},{10,... | collective-permute-start | bytes 196616 | tf_op jit(solution)/shard_map/ppermute | solution.py:633
  7.3 4.0 %collective-permute-start = (f32[64,128]{1,0:T(8,128)S(1)}, f32[64,128]{1,0:T(8,128)S(1)}, u32[]{:S(2)}, u32[]{:S(2)}) collective-permute-start(f32[64,128]{1,0:T(8,128)S(1)} %get-tuple-element.40), channel_id=1, source_target_pairs={{0,1},{1,0},{2,3},{3,2},{4,5},{5,4},{6,7},{7,6},{8,9},{9,8},{10,11... | collective-permute-start | bytes 98312 | tf_op jit(solution)/shard_map/ppermute | solution.py:633
  11.3 3.6 %copy-start = (f32[384,384]{1,0:T(8,128)S(1)}, f32[384,384]{1,0:T(8,128)}, u32[]{:S(2)}) copy-start(f32[384,384]{1,0:T(8,128)} %fine.1) | copy-start | bytes 1769476
  11.8 4.3 %collective-permute-start.6 = (f32[128,128]{1,0:T(8,128)S(1)}, f32[128,128]{1,0:T(8,128)S(1)}, u32[]{:S(2)}, u32[]{:S(2)}) collective-permute-start(f32[128,128]{1,0:T(8,128)S(1)} %get-tuple-element.57), channel_id=1, source_target_pairs={{0,6},{1,7},{2,4},{3,5},{4,2},{5,3},{6,0},{7,1},{8,14},{9,15},{10,... | collective-permute-start | bytes 196616 | tf_op jit(solution)/shard_map/ppermute | solution.py:633
  12.2 4.3 %collective-permute-start.7 = (f32[128,128]{1,0:T(8,128)S(1)}, f32[128,128]{1,0:T(8,128)S(1)}, u32[]{:S(2)}, u32[]{:S(2)}) collective-permute-start(f32[128,128]{1,0:T(8,128)S(1)} %get-tuple-element.58), channel_id=1, source_target_pairs={{0,8},{1,9},{2,10},{3,11},{4,12},{5,13},{6,14},{7,15},{8,0},{9,1},... | collective-permute-start | bytes 196616 | tf_op jit(solution)/shard_map/ppermute | solution.py:633
  12.9 3.6 %collective-permute-start.8 = (f32[128,128]{1,0:T(8,128)S(1)}, f32[128,128]{1,0:T(8,128)S(1)}, u32[]{:S(2)}, u32[]{:S(2)}) collective-permute-start(f32[128,128]{1,0:T(8,128)S(1)} %get-tuple-element.59), channel_id=1, source_target_pairs={{0,2},{1,3},{2,0},{3,1},{4,6},{5,7},{6,4},{7,5},{8,16},{9,17},{10,... | collective-permute-start | bytes 196616 | tf_op jit(solution)/shard_map/ppermute | solution.py:633
  13.1 3.4 %collective-permute-start.9 = (f32[128,128]{1,0:T(8,128)S(1)}, f32[128,128]{1,0:T(8,128)S(1)}, u32[]{:S(2)}, u32[]{:S(2)}) collective-permute-start(f32[128,128]{1,0:T(8,128)S(1)} %get-tuple-element.60), channel_id=1, source_target_pairs={{0,2},{1,3},{2,0},{3,1},{4,6},{5,7},{6,4},{7,5},{8,10},{9,11},{10,... | collective-permute-start | bytes 196616 | tf_op jit(solution)/shard_map/ppermute | solution.py:633
  13.4 3.9 %collective-permute-start.5 = (f32[64,128]{1,0:T(8,128)S(1)}, f32[64,128]{1,0:T(8,128)S(1)}, u32[]{:S(2)}, u32[]{:S(2)}) collective-permute-start(f32[64,128]{1,0:T(8,128)S(1)} %get-tuple-element.55), channel_id=1, source_target_pairs={{0,1},{1,0},{2,3},{3,2},{4,5},{5,4},{6,7},{7,6},{8,9},{9,8},{10,11... | collective-permute-start | bytes 98312 | tf_op jit(solution)/shard_map/ppermute | solution.py:633
  17.8 5.7 %collective-permute-start.10 = (f32[128,128]{1,0:T(8,128)S(1)}, f32[128,128]{1,0:T(8,128)S(1)}, u32[]{:S(2)}, u32[]{:S(2)}) collective-permute-start(f32[128,128]{1,0:T(8,128)S(1)} %get-tuple-element.63), channel_id=1, source_target_pairs={{0,6},{1,7},{2,4},{3,5},{4,2},{5,3},{6,0},{7,1},{8,14},{9,15},{10,... | collective-permute-start | bytes 196616 | tf_op jit(solution)/shard_map/ppermute | solution.py:633
  18.5 5.0 %collective-permute-start.11 = (f32[128,128]{1,0:T(8,128)S(1)}, f32[128,128]{1,0:T(8,128)S(1)}, u32[]{:S(2)}, u32[]{:S(2)}) collective-permute-start(f32[128,128]{1,0:T(8,128)S(1)} %get-tuple-element.64), channel_id=1, source_target_pairs={{0,8},{1,9},{2,10},{3,11},{4,12},{5,13},{6,14},{7,15},{8,0},{9,1},... | collective-permute-start | bytes 196616 | tf_op jit(solution)/shard_map/ppermute | solution.py:633
  19.9 3.7 %collective-permute-start.12 = (f32[128,128]{1,0:T(8,128)S(1)}, f32[128,128]{1,0:T(8,128)S(1)}, u32[]{:S(2)}, u32[]{:S(2)}) collective-permute-start(f32[128,128]{1,0:T(8,128)S(1)} %get-tuple-element.65), channel_id=1, source_target_pairs={{0,2},{1,3},{2,0},{3,1},{4,6},{5,7},{6,4},{7,5},{8,16},{9,17},{10,... | collective-permute-start | bytes 196616 | tf_op jit(solution)/shard_map/ppermute | solution.py:633
  20.9 2.6 %collective-permute-start.13 = (f32[128,128]{1,0:T(8,128)S(1)}, f32[128,128]{1,0:T(8,128)S(1)}, u32[]{:S(2)}, u32[]{:S(2)}) collective-permute-start(f32[128,128]{1,0:T(8,128)S(1)} %get-tuple-element.66), channel_id=1, source_target_pairs={{0,2},{1,3},{2,0},{3,1},{4,6},{5,7},{6,4},{7,5},{8,10},{9,11},{10,... | collective-permute-start | bytes 196616 | tf_op jit(solution)/shard_map/ppermute | solution.py:633
  20.9 3.9 %collective-permute-start.14 = (f32[64,128]{1,0:T(8,128)S(1)}, f32[64,128]{1,0:T(8,128)S(1)}, u32[]{:S(2)}, u32[]{:S(2)}) collective-permute-start(f32[64,128]{1,0:T(8,128)S(1)} %get-tuple-element.68), channel_id=1, source_target_pairs={{0,1},{1,0},{2,3},{3,2},{4,5},{5,4},{6,7},{7,6},{8,9},{9,8},{10,11... | collective-permute-start | bytes 98312 | tf_op jit(solution)/shard_map/ppermute | solution.py:633
  25.3 4.0 %collective-permute-start.15 = (f32[128,128]{1,0:T(8,128)S(1)}, f32[128,128]{1,0:T(8,128)S(1)}, u32[]{:S(2)}, u32[]{:S(2)}) collective-permute-start(f32[128,128]{1,0:T(8,128)S(1)} %get-tuple-element.70), channel_id=1, source_target_pairs={{0,6},{1,7},{2,4},{3,5},{4,2},{5,3},{6,0},{7,1},{8,14},{9,15},{10,... | collective-permute-start | bytes 196616 | tf_op jit(solution)/shard_map/ppermute | solution.py:633
  25.4 4.9 %collective-permute-start.16 = (f32[128,128]{1,0:T(8,128)S(1)}, f32[128,128]{1,0:T(8,128)S(1)}, u32[]{:S(2)}, u32[]{:S(2)}) collective-permute-start(f32[128,128]{1,0:T(8,128)S(1)} %get-tuple-element.71), channel_id=1, source_target_pairs={{0,8},{1,9},{2,10},{3,11},{4,12},{5,13},{6,14},{7,15},{8,0},{9,1},... | collective-permute-start | bytes 196616 | tf_op jit(solution)/shard_map/ppermute | solution.py:633
  26.9 3.3 %collective-permute-start.17 = (f32[128,128]{1,0:T(8,128)S(1)}, f32[128,128]{1,0:T(8,128)S(1)}, u32[]{:S(2)}, u32[]{:S(2)}) collective-permute-start(f32[128,128]{1,0:T(8,128)S(1)} %get-tuple-element.72), channel_id=1, source_target_pairs={{0,2},{1,3},{2,0},{3,1},{4,6},{5,7},{6,4},{7,5},{8,16},{9,17},{10,... | collective-permute-start | bytes 196616 | tf_op jit(solution)/shard_map/ppermute | solution.py:633
  27.2 3.1 %collective-permute-start.18 = (f32[128,128]{1,0:T(8,128)S(1)}, f32[128,128]{1,0:T(8,128)S(1)}, u32[]{:S(2)}, u32[]{:S(2)}) collective-permute-start(f32[128,128]{1,0:T(8,128)S(1)} %get-tuple-element.73), channel_id=1, source_target_pairs={{0,2},{1,3},{2,0},{3,1},{4,6},{5,7},{6,4},{7,5},{8,10},{9,11},{10,... | collective-permute-start | bytes 196616 | tf_op jit(solution)/shard_map/ppermute | solution.py:633
  27.4 3.9 %collective-permute-start.19 = (f32[64,128]{1,0:T(8,128)S(1)}, f32[64,128]{1,0:T(8,128)S(1)}, u32[]{:S(2)}, u32[]{:S(2)}) collective-permute-start(f32[64,128]{1,0:T(8,128)S(1)} %get-tuple-element.74), channel_id=1, source_target_pairs={{0,1},{1,0},{2,3},{3,2},{4,5},{5,4},{6,7},{7,6},{8,9},{9,8},{10,11... | collective-permute-start | bytes 98312 | tf_op jit(solution)/shard_map/ppermute | solution.py:633
